TPU v7x, 512 devices: a whole 4x4x16 slice. The times are simulated.
512 devices in a mesh: dp: 8 (over x, z_hi), fsdp: 64 (over y, z_lo, core).
Axes of the slice: x: 4, y: 4, z: 16 (z_hi: 2, z_lo: 8; z = z_hi * 8 + z_lo), core: 2. Of those that a mesh axis runs over, the one named last changes fastest.
Arguments:
- tokens: bfloat16 [65536, 3584], P(('dp', 'fsdp')), may hold values from -6 to 6
- out_grad: bfloat16 [65536, 14336], P(('dp', 'fsdp')), may hold values from -6 to 6
- block_values: bfloat16 [320, 128, 128], P('fsdp'), may hold values from -0.3125 to 0.3125
- active_blocks: int32 [320, 2], P('fsdp'), may hold values from 0 to 111
- drop_slots: int32 [64], P('fsdp'), may hold values from 0 to 4, as said below
- cand_blocks: int32 [64, 2], replicated, may hold values from 0 to 111, as said below
- group_counts: int32 [8], P('dp'), may hold values from 4096 to 8192
Outputs:
- cand_grad: float32 [64, 128, 128], P('fsdp')
- cand_score: float32 [64], P('fsdp')
Inputs may be any that keep to these rules, and one draw needn't show every extreme that they name: `drop_slots`: the 1 entries of each device are distinct local slots. `cand_blocks`: pairs of block row and block column, distinct, none of them a stored block.
All inputs are finite; a program needn't handle non-finite values.
Results may differ from a plain program's by a relative error of at most 0.007.
Values may be sent and summed in bfloat16 or wider, within the bound.
No kernel may reach another device: no remote copies, remote signals or barrier semaphores. Data moves between devices by JAX's collectives and lax.ppermute only.
A program may use at most 128 MiB of HBM per device.

v0:
```python
import jax
import jax.numpy as jnp
from jax import lax
from jax.sharding import PartitionSpec as P


def gelu_slope(value_in):
    normal_cdf = 0.5 * (1.0 + jax.scipy.special.erf(value_in * 0.7071067811865476))
    density = jnp.exp(-0.5 * value_in * value_in) * 0.3989422804014327
    return normal_cdf + value_in * density


def per_device(
    tokens, out_grad, block_values, active_blocks, drop_slots, cand_blocks, group_counts
):
    rows_dev = tokens.shape[0]
    block_size = block_values.shape[1]
    row_blocks = tokens.shape[1] // block_size
    hidden = out_grad.shape[1]
    col_blocks = hidden // block_size
    local_blocks = block_values.shape[0]
    cand_total = cand_blocks.shape[0]
    tok_blocks = tokens.reshape(rows_dev, row_blocks, block_size)
    slot_ids = jnp.arange(local_blocks, dtype=jnp.int32)
    dropped = jnp.any(slot_ids[:, None] == drop_slots[None, :], axis=1)
    kept_flag = 1 - dropped.astype(jnp.int32)
    empty = jnp.zeros((rows_dev, col_blocks, block_size), jnp.float32)
    masked = block_values * kept_flag.astype(jnp.bfloat16)[:, None, None]
    weights = lax.all_gather(masked, "fsdp", axis=0, tiled=True)
    places = lax.all_gather(active_blocks, "fsdp", axis=0, tiled=True)
    picked = tok_blocks[:, places[:, 0], :]
    product = jnp.einsum("tkb,kbc->tkc", picked, weights, preferred_element_type=jnp.float32)
    preact = empty.at[:, places[:, 1], :].add(product)
    position = lax.axis_index("fsdp") * rows_dev + jnp.arange(rows_dev, dtype=jnp.int32)
    usable = (position < group_counts[0]).astype(jnp.float32)
    cand_x = tok_blocks[:, cand_blocks[:, 0], :]
    preact = preact.reshape(rows_dev, hidden)
    pre_grad = (out_grad.astype(jnp.float32) * gelu_slope(preact) * usable[:, None]).astype(
        jnp.bfloat16
    )
    cand_dy = pre_grad.reshape(rows_dev, col_blocks, block_size)[:, cand_blocks[:, 1], :]
    cand_local = cand_total // lax.axis_size("fsdp")
    term = jnp.einsum("tcb,tce->cbe", cand_x, cand_dy, preferred_element_type=jnp.float32)
    shared = lax.psum_scatter(
        term.reshape(cand_local * block_size * lax.axis_size("fsdp"), block_size),
        "fsdp",
        scatter_dimension=0,
        tiled=True,
    )
    summed = lax.psum(shared, "dp")
    scale = (rows_dev * lax.axis_size("dp") * lax.axis_size("fsdp")) ** (-0.5)
    cand_grad = summed.reshape(cand_local, block_size, block_size) * scale
    cand_score = jnp.sqrt(jnp.mean(cand_grad * cand_grad, axis=(1, 2)) + 1e-06)
    return (cand_grad, cand_score)


def solution(mesh):
    return jax.shard_map(
        per_device,
        mesh=mesh,
        in_specs=(
            P(("dp", "fsdp"), None),
            P(("dp", "fsdp"), None),
            P("fsdp", None, None),
            P("fsdp", None),
            P("fsdp"),
            P(),
            P("dp"),
        ),
        out_specs=(P("fsdp", None, None), P("fsdp")),
        check_vma=False,
    )
```

profile of v0, /device:TPU:24, one launch (start us, length us, event | category | flops | bytes accessed | tf_op | source)
XLA Modules:
  0.0 867.9 jit_solution(881897317815401575)
XLA Ops:
  7.2 0.0 all-gather.3.cloned.1.call-start
  7.9 1.7 broadcast_multiply_fusion
  9.5 0.0 all-gather.3.cloned.1.call-update
  9.5 0.0 reduce-scatter.2.cloned.1.call-start
  9.6 1.6 copy.24
  11.2 0.6 copy.25
  11.8 114.3 %all-gather = s32[64,5,2]{1,2,0:T(2,128)S(1)} all-gather(s32[1,5,2]{1,2,0:T(2,128)} %bitcast.41), channel_id=1, replica_groups=mesh['dp'=8,'fsdp'=64] {'fsdp'}, dimensions={0}, use_global_device_ids=true | all-gather | bytes 2600 | tf_op jit(solution)/shard_map/all_gather | solution.py:30
  126.1 0.1 reshape.82
  126.2 6.0 copy.26
  133.0 0.0 copy-start
  133.0 10.6 %gather_fusion.1 = bf16[320,128,128]{2,1,0:T(8,128)(2,1)} fusion(bf16[128,28,128]{2,0,1:T(8,128)(2,1)S(1)} %copy.25, s32[1024]{0:T(1024)S(1)} %pad_clamp_fusion.1), kind=kCustom, calls=%fused_computation.1 | custom fusion | bytes 20972800 | tf_op jit(solution)/shard_map/gather | solution.py:31
  143.6 0.0 copy-done
  143.6 1.0 gather_fusion
  144.6 0.0 all-gather.3.cloned.1.call-done
  144.6 16.8 %fusion = f32[320,128,128]{2,1,0:T(8,128)} fusion(bf16[320,128,128]{2,1,0:T(8,128)(2,1)} %all-gather.3.cloned.1.call-done, bf16[320,128,128]{2,1,0:T(8,128)(2,1)} %gather_fusion.1), kind=kOutput, calls=%fused_computation.5 | convolution fusion | flops 1342177280 | bytes 41943040 | tf_op jit(solution)/shard_map/tkb,kbc->tkc/dot_general | solution.py:32
  161.4 3.9 broadcast_in_dim.2
  165.4 65.8 %scatter_fusion = f32[128,112,128]{2,0,1:T(8,128)} fusion(f32[128,112,128]{2,0,1:T(8,128)} %broadcast_in_dim.2, s32[320]{0:T(512)S(1)} %get-tuple-element.3, f32[320,128,128]{2,1,0:T(8,128)} %fusion), kind=kCustom, calls=%fused_computation.3 | custom fusion | flops 5242880 | bytes 62915840 | tf_op jit(solution)/shard_map/scatter-add | solution.py:33
  231.2 8.7 copy.29
  239.8 8.3 fusion.8
  248.2 6.1 copy.30
  254.2 4.2 gather_fusion.2
  258.4 4.4 fusion.12
  262.8 0.0 reduce-scatter.2.cloned.1.call-update
  262.8 0.0 all-reduce.2.cloned.1.call-start
  262.9 411.2 %reduce-scatter.2.cloned.1.call-done = f32[128,128]{1,0:T(8,128)} async-done(((f32[8192,128]{1,0:T(8,128)}), f32[128,128]{1,0:T(8,128)}) %reduce-scatter.2.cloned.1.call-update) | async-done | bytes 65552 | tf_op jit(solution)/shard_map/reduce_scatter | solution.py:44
  674.1 0.0 all-reduce.2.cloned.1.call-update
  674.1 183.4 %all-reduce.2.cloned.1.call-done = f32[128,128]{1,0:T(8,128)} async-done(((f32[128,128]{1,0:T(8,128)}), f32[128,128]{1,0:T(8,128)}) %all-reduce.2.cloned.1.call-update) | async-done | bytes 65552 | tf_op jit(solution)/shard_map/psum | solution.py:50
  857.5 2.1 multiply_reduce_fusion
  (7 shorter events, 0.1 us)
Async XLA Ops:
  7.2 137.4 %all-gather.3.cloned.1.call-start = ((), (), s32[]{:S(2)}) async-start(), calls=%async_computation.1 | async-start | bytes 10649600 | tf_op jit(solution)/shard_map/all_gather | solution.py:29
  9.5 664.5 %reduce-scatter.2.cloned.1.call-start = ((), (), s32[]{:S(2)}) async-start(), calls=%async_computation.2 | async-start | bytes 4259840 | tf_op jit(solution)/shard_map/reduce_scatter | solution.py:44
  133.0 10.6 %copy-start = (s32[64,2]{0,1:T(2,128)S(1)}, s32[64,2]{0,1:T(2,128)}, u32[]{:S(2)}) copy-start(s32[64,2]{0,1:T(2,128)} %param.12) | copy-start | bytes 1540
  262.8 594.7 %all-reduce.2.cloned.1.call-start = ((), (), s32[]{:S(2)}) async-start(), calls=%async_computation.3 | async-start | bytes 131072 | tf_op jit(solution)/shard_map/psum | solution.py:50
Sparse Core Ops, SparseCore 0:
  10.1 132.9 all-gather.2
  262.9 411.0 reduce-scatter.1
  677.2 180.2 all-reduce.1
where the time goes:
time: 869 us; the launch traced here: 868 us
  waiting for transfers between devices  595 us (68%)
  blocking collectives  114 us (13%)
  other arithmetic  77.9 us (9%)
  local copies, waits for them, and re-layouts  42.8 us (5%)
  matrix products  21.2 us (2%)
  between operations  16.9 us (2%)
    reduce_scatter x1, waiting for transfers between devices, per_device(): lax.psum_scatter(term.reshape(cand_local * block_size * lax.axis_size('fs...  411 us
    psum x1, waiting for transfers between devices, per_device(): summed = lax.psum(shared, 'dp')  183 us
    all_gather x1, blocking collectives, per_device(): places = lax.all_gather(active_blocks, 'fsdp', axis=0, tiled=True)  114 us
    scatter-add x1, other arithmetic, per_device(): preact = empty.at[:, places[:, 1], :].add(product)  65.8 us
  transfers between devices with their start and end apart: 3, of which 2 were waited for; matrix products, arithmetic and copies ran while one was open for 2% of the time, Pallas kernels for 0%

commit v1 on v0

v1 whole, which is shorter than its diff:
```python
import functools

import jax
import jax.numpy as jnp
from jax import lax
from jax.experimental import pallas as pl
from jax.experimental.pallas import tpu as pltpu
from jax.sharding import Mesh, PartitionSpec as P

AXES = ("x", "zh", "y", "zl", "c")
SIZES = (4, 2, 4, 8, 2)
NX, NZH, NY, NZL, NC = SIZES
BLK = 128
TAIL = 16
PIECE = NZL * BLK + TAIL


def lines(axis_of_core):
    def flat(x, zh, y, zl, c):
        return (((x * NZH + zh) * NY + y) * NZL + zl) * NC + c

    groups = []
    for c, axis in enumerate(axis_of_core):
        for zh in range(NZH):
            for zl in range(NZL):
                for other in range(4):
                    if axis == "y":
                        groups.append([flat(other, zh, y, zl, c) for y in range(NY)])
                    else:
                        groups.append([flat(x, zh, other, zl, c) for x in range(NX)])
    return groups


def to_all(value, axis, count, groups=None):
    copies = jnp.broadcast_to(value[None], (count,) + value.shape)
    return lax.all_to_all(copies, axis, 0, 0, axis_index_groups=groups, tiled=True)


def gelu_slope(value_in):
    normal_cdf = 0.5 * (1.0 + lax.erf(value_in * 0.7071067811865476))
    density = jnp.exp(-0.5 * value_in * value_in) * 0.3989422804014327
    return normal_cdf + value_in * density


def local_kernel(
    stored, places, cand, info,
    tok_ref, grad_hbm, own_hbm, other_hbm,
    out_ref,
    weights, grad, acc, pre, need, rows, cols, offs, used, sems,
):
    half = own_hbm.shape[0]
    copy_own = pltpu.make_async_copy(own_hbm, weights.at[pl.ds(0, half)], sems.at[0])
    copy_other = pltpu.make_async_copy(other_hbm, weights.at[pl.ds(half, half)], sems.at[1])
    copy_grad = pltpu.make_async_copy(grad_hbm, grad, sems.at[2])
    copy_own.start()
    copy_other.start()
    copy_grad.start()
    spare = acc.shape[0] - 1
    cands = cand.shape[0] // 2
    tokens = tok_ref.shape[0]

    def clear(i, carry):
        need[i] = 0
        return carry

    lax.fori_loop(0, spare + 1, clear, 0, unroll=8)

    def mark(j, count):
        col = cand[2 * j + 1]
        fresh = 1 - need[col]
        need[col] = 1
        used[count] = col
        acc[col] = jnp.zeros((tokens, BLK), jnp.float32)
        return count + fresh

    n_cols = lax.fori_loop(0, cands, mark, 0, unroll=4)

    def choose(k, count):
        col = places[2 * k + 1]
        rows[count] = places[2 * k]
        cols[count] = col
        offs[count] = (k // NZL) * PIECE + (k % NZL) * BLK
        return count + need[col]

    n_blocks = lax.fori_loop(0, stored, choose, 0, unroll=8)
    for u in range(4):
        rows[n_blocks + u] = 0
        cols[n_blocks + u] = spare
        offs[n_blocks + u] = 0
    copy_own.wait()
    copy_other.wait()

    def multiply(step, carry):
        products = []
        for u in range(4):
            i = step * 4 + u
            row = pl.multiple_of(rows[i] * BLK, BLK)
            off = pl.multiple_of(offs[i], 16)
            products.append(
                jnp.dot(
                    tok_ref[:, pl.ds(row, BLK)],
                    weights[pl.ds(off, BLK), :],
                    preferred_element_type=jnp.float32,
                )
            )
        for u in range(4):
            i = step * 4 + u
            acc[cols[i]] += products[u]
        return carry

    lax.fori_loop(0, (n_blocks + 3) // 4, multiply, 0)
    copy_grad.wait()
    position = info[0] + lax.broadcasted_iota(jnp.int32, (tokens, BLK), 0)
    usable = (position < info[1]).astype(jnp.float32)

    def slope(i, carry):
        col = used[i]
        lanes = pl.ds(pl.multiple_of(col * BLK, BLK), BLK)
        given = grad[:, lanes].astype(jnp.float32)
        pre[col] = (given * gelu_slope(acc[col]) * usable).astype(jnp.bfloat16)
        return carry

    lax.fori_loop(0, n_cols, slope, 0)

    def gradient(q, carry):
        y, z = q // NZL, q % NZL
        for core in range(NC):
            j = q * NC + core
            row = pl.multiple_of(cand[2 * j] * BLK, BLK)
            part = lax.dot_general(
                tok_ref[:, pl.ds(row, BLK)],
                pre[cand[2 * j + 1]],
                (((0,), (0,)), ((), ())),
                preferred_element_type=jnp.float32,
            ).astype(jnp.bfloat16)
            for x in range(NX):
                out_ref[core, x, y, z] = part[x * 32 : (x + 1) * 32]
        return carry

    lax.fori_loop(0, cands // NC, gradient, 0, unroll=2)


def local_part(tokens, out_grad, own, other, places, cand, info):
    stored = places.shape[0] // 2
    col_blocks = out_grad.shape[1] // BLK
    rows_dev = tokens.shape[0]
    shape = (NC, NX, NY, NZL, BLK // NX, BLK)
    smem = lambda count: pltpu.SMEM((count,), jnp.int32)
    return pl.pallas_call(
        functools.partial(local_kernel, stored),
        out_shape=jax.ShapeDtypeStruct(shape, jnp.bfloat16),
        grid_spec=pltpu.PrefetchScalarGridSpec(
            num_scalar_prefetch=3,
            grid=(),
            in_specs=[
                pl.BlockSpec(memory_space=pltpu.VMEM),
                pl.BlockSpec(memory_space=pl.ANY),
                pl.BlockSpec(memory_space=pl.ANY),
                pl.BlockSpec(memory_space=pl.ANY),
            ],
            out_specs=pl.BlockSpec(memory_space=pltpu.VMEM),
            scratch_shapes=[
                pltpu.VMEM((2 * own.shape[0], BLK), jnp.bfloat16),
                pltpu.VMEM(out_grad.shape, jnp.bfloat16),
                pltpu.VMEM((col_blocks + 1, rows_dev, BLK), jnp.float32),
                pltpu.VMEM((col_blocks, rows_dev, BLK), jnp.bfloat16),
                smem(col_blocks + 1),
                smem(stored + 8),
                smem(stored + 8),
                smem(stored + 8),
                smem(cand.shape[0] // 2 + 8),
                pltpu.SemaphoreType.DMA((3,)),
            ],
        ),
        compiler_params=pltpu.CompilerParams(vmem_limit_bytes=48 * 1024 * 1024),
        cost_estimate=pl.CostEstimate(
            flops=2 * (stored + 64) * rows_dev * BLK * BLK,
            bytes_accessed=20_000_000,
            transcendentals=2_000_000,
        ),
    )(places, cand, info, tokens, out_grad, own, other)


def per_device(
    tokens, out_grad, block_values, active_blocks, drop_slots, cand_blocks, group_counts
):
    rows_dev = tokens.shape[0]
    me = {name: lax.axis_index(name) for name in AXES}
    slot = me["x"] + (me["x"] >= drop_slots[0]).astype(jnp.int32)
    block = lax.dynamic_index_in_dim(block_values, slot, 0, keepdims=False)
    place = lax.dynamic_index_in_dim(active_blocks, slot, 0, keepdims=False)
    lane = lax.broadcasted_iota(jnp.int32, (TAIL, BLK), 1)
    tail = jnp.where(lane == 0, place[0], jnp.where(lane == 1, place[1], 0))
    piece = jnp.concatenate([block, tail.astype(jnp.bfloat16)], axis=0)
    along_z = to_all(piece, "zl", NZL).reshape(NZL, BLK + TAIL, BLK)
    tails = jnp.pad(along_z[:, BLK, :], ((0, TAIL - NZL), (0, 0)))
    pack = jnp.concatenate([along_z[:, :BLK, :].reshape(NZL * BLK, BLK), tails], axis=0)
    line = to_all(pack, AXES, 4, lines("yx"))
    plane = to_all(line.reshape(4 * PIECE, BLK), AXES, 4, lines("xy")).reshape(16 * PIECE, BLK)
    other = lax.ppermute(plane, "c", [(0, 1), (1, 0)])

    def places_of(part):
        return part.reshape(16, PIECE, BLK)[:, NZL * BLK : NZL * BLK + NZL, :2]

    places = jnp.stack([places_of(plane), places_of(other)]).astype(jnp.int32).reshape(-1)
    fsdp = (me["y"] * NZL + me["zl"]) * NC + me["c"]
    info = jnp.stack([fsdp * rows_dev, group_counts[0]]).astype(jnp.int32)
    partial = local_part(
        tokens, out_grad, plane, other, places, cand_blocks.reshape(-1), info
    )
    pair = lax.all_to_all(partial, "c", 0, 0, tiled=True)
    mine = jnp.sum(pair.astype(jnp.float32), axis=0).astype(jnp.bfloat16)
    mine = mine.reshape(NX * NY, NZL, BLK // NX, BLK)
    planes = lax.all_to_all(mine, ("x", "y"), 0, 0, tiled=True)
    strip = jnp.sum(planes.astype(jnp.float32), axis=0).astype(jnp.bfloat16)
    strips = jnp.broadcast_to(strip[None], (NZH,) + strip.shape).reshape(NZH * NZL, BLK // NX, BLK)
    strips = lax.all_to_all(strips, ("zh", "zl"), 0, 0, tiled=True)
    summed = jnp.sum(strips.astype(jnp.float32), axis=0)
    whole = to_all(summed, "x", NX).reshape(1, BLK, BLK)
    scale = (rows_dev * NX * NZH * NY * NZL * NC) ** (-0.5)
    cand_grad = whole * scale
    cand_score = jnp.sqrt(jnp.mean(cand_grad * cand_grad, axis=(1, 2)) + 1e-06)
    return (cand_grad, cand_score)


def solution(mesh):
    fine = Mesh(mesh.devices.reshape(SIZES), AXES)
    dp, fsdp = ("x", "zh"), ("y", "zl", "c")
    return jax.shard_map(
        per_device,
        mesh=fine,
        in_specs=(
            P(AXES, None),
            P(AXES, None),
            P(fsdp, None, None),
            P(fsdp, None),
            P(fsdp),
            P(),
            P(dp),
        ),
        out_specs=(P(fsdp, None, None), P(fsdp)),
        check_vma=False,
    )
```

time: 869 us -> 169 us (0.19)
  waiting for transfers between devices: 595 us -> 5.67 us
  other arithmetic: 77.9 us -> 3.51 us
  local copies, waits for them, and re-layouts: 42.8 us -> 4.45 us
  matrix products: 21.2 us -> 0 us
  blocking collectives: 114 us -> 132 us
  Pallas kernels: 0 us -> 15.3 us
  between operations: 16.9 us -> 3.99 us
    reduce_scatter x1 -> x0, waiting for transfers between devices: 411 us -> none  [per_device(): lax.psum_scatter(term.reshape(cand_local * block_size * lax.axis_size('fs...]
    psum x1 -> x0, waiting for transfers between devices: 183 us -> none  [per_device(): summed = lax.psum(shared, 'dp')]
    all_to_all x0 -> x7, blocking collectives: none -> 132 us  [the longest x4 85.4 us: to_all(): lax.all_to_all(copies, axis, 0, 0, axis_index_groups=groups, tiled=True)]
    all_gather x1 -> x0, blocking collectives: 114 us -> none  [per_device(): places = lax.all_gather(active_blocks, 'fsdp', axis=0, tiled=True)]
    scatter-add x1 -> x0, other arithmetic: 65.8 us -> none  [per_device(): preact = empty.at[:, places[:, 1], :].add(product)]
    dot_general x2 -> x0, matrix products: 21.2 us -> none  [the longest x1 16.8 us: per_device(): jnp.einsum('tkb,kbc->tkc', picked, weights, preferred_element_type=jnp.fl...]
    gather x3 -> x0, local copies, waits for them, and re-layouts: 15.7 us -> none  [the longest x1 10.6 us: per_device(): picked = tok_blocks[:, places[:, 0], :]]
    pallas_call x0 -> x1, Pallas kernels: none -> 15.3 us  [local_part(): pl.pallas_call(functools.partial(local_kernel, stored), out_shape=jax.Sha...]
  transfers between devices with their start and end apart: 3 -> 1, of which waited for: 2 -> 1; matrix products, arithmetic and copies ran while one was open for 2% -> 1% of each run, Pallas kernels for 0% -> 0%
where the time goes in v1:
time: 169 us; the launch traced here: 167 us
  blocking collectives  132 us (78%)
  Pallas kernels  15.3 us (9%)
  waiting for transfers between devices  5.67 us (3%)
  local copies, waits for them, and re-layouts  4.45 us (3%)
  between operations  3.99 us (2%)
  other arithmetic  3.51 us (2%)
  starting transfers between devices  1.91 us (1%)
    all_to_all x4, blocking collectives, to_all(): lax.all_to_all(copies, axis, 0, 0, axis_index_groups=groups, tiled=True)  85.4 us
    all_to_all x1, blocking collectives, per_device(): strips = lax.all_to_all(strips, ('zh', 'zl'), 0, 0, tiled=True)  21.4 us
    all_to_all x1, blocking collectives, per_device(): planes = lax.all_to_all(mine, ('x', 'y'), 0, 0, tiled=True)  19.8 us
    pallas_call x1, Pallas kernels, local_part(): pl.pallas_call(functools.partial(local_kernel, stored), out_shape=jax.Sha...  15.3 us
    ppermute x1, waiting for transfers between devices, per_device(): other = lax.ppermute(plane, 'c', [(0, 1), (1, 0)])  5.67 us
    all_to_all x1, blocking collectives, per_device(): pair = lax.all_to_all(partial, 'c', 0, 0, tiled=True)  5.42 us
  transfers between devices with their start and end apart: 1, of which 1 were waited for; matrix products, arithmetic and copies ran while one was open for 1% of the time, Pallas kernels for 0%

profile of v1, /device:TPU:24, one launch (start us, length us, event | category | flops | bytes accessed | tf_op | source)
XLA Modules:
  0.0 166.8 jit_solution(17179194789490921859)
XLA Ops:
  0.6 0.0 copy-start
  1.3 0.8 constant_dynamic-slice_fusion
  2.1 0.5 fusion.2
  2.6 0.6 compare_select_fusion
  3.3 0.7 select_convert_fusion
  4.0 31.2 %all_to_all.35 = bf16[8,144,128]{2,1,0:T(8,128)(2,1)S(1)} all-to-all(bf16[8,144,128]{2,1,0:T(8,128)(2,1)S(1)} %broadcast_in_dim.24), channel_id=1, replica_groups=mesh['x'=4,'zh'=2,'y'=4,'zl'=8,'c'=2] {'zl'}, dimensions={0} | all-to-all | bytes 589824 | tf_op jit(solution)/shard_map/all_to_all | solution.py:36
  35.3 0.1 broadcast_in_dim.44
  35.5 13.4 %all_to_all.36 = bf16[4,1040,128]{2,1,0:T(8,128)(2,1)S(1)} all-to-all(bf16[4,1040,128]{2,1,0:T(8,128)(2,1)S(1)} %broadcast_in_dim.44), channel_id=1, replica_groups={{0,16,32,48},{128,144,160,176},{256,272,288,304},{384,400,416,432},{2,1..., dimensions={0} | all-to-all | bytes 2129920 | tf_op jit(solution)/shard_map/all_to_all | solution.py:36
  48.9 0.5 broadcast_in_dim.46
  49.4 0.0 copy-start.2
  49.5 0.0 copy-start.1
  49.5 32.4 %all_to_all.37 = bf16[4,4160,128]{2,1,0:T(8,128)(2,1)} all-to-all(bf16[4,4160,128]{2,1,0:T(8,128)(2,1)S(1)} %broadcast_in_dim.46), channel_id=1, replica_groups={{0,128,256,384},{16,144,272,400},{32,160,288,416},{48,176,304,432},{2,1..., dimensions={0} | all-to-all | bytes 8519680 | tf_op jit(solution)/shard_map/all_to_all | solution.py:36
  81.9 1.9 %collective-permute-start = (bf16[16640,128]{1,0:T(8,128)(2,1)}, bf16[16640,128]{1,0:T(8,128)(2,1)}, u32[]{:S(2)}, u32[]{:S(2)}) collective-permute-start(bf16[16640,128]{1,0:T(8,128)(2,1)} %bitcast.9.own_hbm), channel_id=1, source_target_pairs={{0,1},{1,0},{2,3},{3,2},{4,5},{5,4},{6,7},{7,6},{8,9},{9,8},{10,11... | collective-permute-start | bytes 12779528 | tf_op jit(solution)/shard_map/ppermute | solution.py:200
  84.5 0.0 copy-done.2
  84.5 0.1 copy.25
  84.6 0.1 reshape.61.cand
  84.7 0.1 pad_add_fusion.info
  84.8 0.8 slice_bitcast_fusion
  85.6 0.1 copy.23
  85.7 5.7 %collective-permute-done.other_hbm = bf16[16640,128]{1,0:T(8,128)(2,1)} collective-permute-done((bf16[16640,128]{1,0:T(8,128)(2,1)}, bf16[16640,128]{1,0:T(8,128)(2,1)}, u32[]{:S(2)}, u32[]{:S(2)}) %collective-permute-start) | collective-permute-done | bytes 4259872 | tf_op jit(solution)/shard_map/ppermute | solution.py:200
  91.4 0.8 slice.29
  92.1 0.1 copy.27
  92.3 0.2 copy.24
  92.5 0.1 reshape.64.places
  92.6 15.3 %shard_map.86 = bf16[2,4,4,8,32,128]{5,4,3,2,1,0:T(8,128)(2,1)S(1)} custom-call(s32[512]{0:T(512)S(1)} %reshape.64.places, s32[128]{0:T(128)S(1)} %reshape.61.cand, s32[2]{0:T(128)S(1)} %pad_add_fusion.info, bf16[128,3584]{1,0:T(8,128)(2,1)S(1)} %copy-done.1, bf16[128,14336]{1,0:T(8,128)(2,1)} %grad_hbm.1, bf16[16640,128]{1,0:T(8,128)(2,1)} %bitcast.9.own_hbm, ...), custom_call_target="tpu_custom_call" | custom-call | flops 1342177280 | bytes 20000000 | tf_op jit(solution)/shard_map/pallas_call | solution.py:149
  108.0 5.4 %all_to_all.38 = bf16[2,4,4,8,32,128]{5,4,3,2,1,0:T(8,128)(2,1)S(1)} all-to-all(bf16[2,4,4,8,32,128]{5,4,3,2,1,0:T(8,128)(2,1)S(1)} %shard_map.86), channel_id=1, replica_groups=mesh['x'=4,'zh'=2,'y'=4,'zl'=8,'c'=2] {'c'}, dimensions={0} | all-to-all | bytes 4194304 | tf_op jit(solution)/shard_map/all_to_all | solution.py:211
  113.4 0.7 reduce_sum.42
  114.1 19.8 %all_to_all.39 = bf16[16,8,32,128]{3,2,1,0:T(8,128)(2,1)S(1)} all-to-all(bf16[16,8,32,128]{3,2,1,0:T(8,128)(2,1)S(1)} %bitcast.25), channel_id=1, replica_groups=mesh['x'=4,'zh'=2,'y'=4,'zl'=8,'c'=2] {'x','y'}, dimensions={0} | all-to-all | bytes 2097152 | tf_op jit(solution)/shard_map/all_to_all | solution.py:214
  133.8 0.1 reduce_sum.43
  134.0 21.4 %all_to_all.40 = bf16[16,32,128]{2,1,0:T(8,128)(2,1)S(1)} all-to-all(bf16[16,32,128]{2,1,0:T(8,128)(2,1)S(1)} %bitcast.27), channel_id=1, replica_groups=mesh['x'=4,'zh'=2,'y'=4,'zl'=8,'c'=2] {'zh','zl'}, dimensions={0} | all-to-all | bytes 262144 | tf_op jit(solution)/shard_map/all_to_all | solution.py:217
  155.5 8.3 %all_to_all.41 = f32[4,32,128]{2,1,0:T(8,128)S(1)} all-to-all(f32[4,32,128]{2,1,0:T(8,128)S(1)} %broadcast_in_dim.48), channel_id=1, replica_groups=mesh['x'=4,'zh'=2,'y'=4,'zl'=8,'c'=2] {'x'}, dimensions={0} | all-to-all | bytes 131072 | tf_op jit(solution)/shard_map/all_to_all | solution.py:36
  163.8 1.2 multiply_reduce_fusion
  (14 shorter events, 0.2 us)
Async XLA Ops:
  0.6 2.7 %copy-start = (bf16[5,128,128]{2,1,0:T(8,128)(2,1)S(1)}, bf16[5,128,128]{2,1,0:T(8,128)(2,1)}, u32[]{:S(2)}) copy-start(bf16[5,128,128]{2,1,0:T(8,128)(2,1)} %param.9) | copy-start | bytes 491524
  49.4 35.0 %copy-start.2 = (s32[64,2]{0,1:T(2,128)S(1)}, s32[64,2]{0,1:T(2,128)}, u32[]{:S(2)}) copy-start(s32[64,2]{0,1:T(2,128)} %param.12) | copy-start | bytes 1540
  49.5 43.2 %copy-start.1 = (bf16[128,3584]{1,0:T(8,128)(2,1)S(1)}, bf16[128,3584]{1,0:T(8,128)(2,1)}, u32[]{:S(2)}) copy-start(bf16[128,3584]{1,0:T(8,128)(2,1)} %tok_ref.1) | copy-start | bytes 2752516
  81.9 9.5 %collective-permute-start = (bf16[16640,128]{1,0:T(8,128)(2,1)}, bf16[16640,128]{1,0:T(8,128)(2,1)}, u32[]{:S(2)}, u32[]{:S(2)}) collective-permute-start(bf16[16640,128]{1,0:T(8,128)(2,1)} %bitcast.9.own_hbm), channel_id=1, source_target_pairs={{0,1},{1,0},{2,3},{3,2},{4,5},{5,4},{6,7},{7,6},{8,9},{9,8},{10,11... | collective-permute-start | bytes 12779528 | tf_op jit(solution)/shard_map/ppermute | solution.py:200

commit v2 on v1

v2 whole, which is shorter than its diff:
```python
import jax
import jax.numpy as jnp
from jax import lax
from jax.experimental import pallas as pl
from jax.experimental.pallas import tpu as pltpu
from jax.sharding import Mesh, PartitionSpec as P

AXES = ("x", "zh", "y", "zl", "c")
SIZES = (4, 2, 4, 8, 2)
NX, NZH, NY, NZL, NC = SIZES
BLK = 128
TAIL = 16
PIECE = NZL * BLK + TAIL
MUL = 8


def flat(x, zh, y, zl, c):
    return (((x * NZH + zh) * NY + y) * NZL + zl) * NC + c


def runs_along_z():
    return [
        [flat(x, (z // NZL) % NZH, y, z % NZL, c) for z in range(start, start + NZL)]
        for c in range(NC)
        for x in range(NX)
        for y in range(NY)
        for start in (4 * c, 4 * c + NZL)
    ]


def lines(axis_of_core):
    groups = []
    for c, axis in enumerate(axis_of_core):
        for zh in range(NZH):
            for zl in range(NZL):
                for other in range(4):
                    if axis == "y":
                        groups.append([flat(other, zh, y, zl, c) for y in range(NY)])
                    else:
                        groups.append([flat(x, zh, other, zl, c) for x in range(NX)])
    return groups


def to_all(value, axis, count, groups=None):
    copies = jnp.broadcast_to(value[None], (count,) + value.shape)
    return lax.all_to_all(copies, axis, 0, 0, axis_index_groups=groups, tiled=True)


def gelu_slope(value_in):
    normal_cdf = 0.5 * (1.0 + lax.erf(value_in * 0.7071067811865476))
    density = jnp.exp(-0.5 * value_in * value_in) * 0.3989422804014327
    return normal_cdf + value_in * density


def choose_blocks(places, slot_of, rows, slots, offs, spare, unroll):
    def choose(k, count):
        slot = slot_of[places[2 * k + 1]]
        rows[count] = places[2 * k]
        slots[count] = slot
        offs[count] = (k // NZL) * PIECE + (k % NZL) * BLK
        return count + (slot != spare).astype(jnp.int32)

    count = lax.fori_loop(0, places.shape[0] // 2, choose, 0, unroll=8)
    for u in range(unroll):
        rows[count + u] = 0
        slots[count + u] = spare
        offs[count + u] = 0
    return count


def give_slots(cand, slot_of, used, spare):
    def clear(i, carry):
        slot_of[i] = spare
        return carry

    lax.fori_loop(0, slot_of.shape[0], clear, 0, unroll=8)

    def mark(j, count):
        col = cand[2 * j + 1]
        had = slot_of[col]
        fresh = had == spare
        slot_of[col] = jnp.where(fresh, count, had)
        used[count] = col
        return count + fresh.astype(jnp.int32)

    return lax.fori_loop(0, cand.shape[0] // 2, mark, 0, unroll=4)


def add_products(count, tok_ref, weights, acc, rows, slots, offs, unroll):
    def multiply(step, carry):
        products = []
        for u in range(unroll):
            i = step * unroll + u
            row = pl.multiple_of(rows[i] * BLK, BLK)
            off = pl.multiple_of(offs[i], 16)
            products.append(
                jnp.dot(
                    tok_ref[:, pl.ds(row, BLK)],
                    weights[pl.ds(off, BLK), :],
                    preferred_element_type=jnp.float32,
                )
            )
        for u in range(unroll):
            acc[slots[step * unroll + u]] += products[u]
        return carry

    lax.fori_loop(0, (count + unroll - 1) // unroll, multiply, 0)


def first_kernel(
    places, cand, tok_ref, own_hbm, acc,
    weights, slot_of, used, rows, slots, offs, sem,
):
    copy_own = pltpu.make_async_copy(own_hbm, weights, sem.at[0])
    copy_own.start()
    spare = acc.shape[0] - 1
    give_slots(cand, slot_of, used, spare)

    def zero(i, carry):
        acc[i] = jnp.zeros(acc.shape[1:], jnp.float32)
        return carry

    lax.fori_loop(0, spare + 1, zero, 0, unroll=5)
    count = choose_blocks(places, slot_of, rows, slots, offs, spare, MUL)
    copy_own.wait()
    add_products(count, tok_ref, weights, acc, rows, slots, offs, MUL)


def second_kernel(
    places, cand, info, tok_ref, grad_hbm, other_hbm, first, out_ref,
    weights, grad, acc, pre, slot_of, used, rows, slots, offs, sem,
):
    copy_other = pltpu.make_async_copy(other_hbm, weights, sem.at[0])
    copy_grad = pltpu.make_async_copy(grad_hbm, grad, sem.at[1])
    copy_other.start()
    copy_grad.start()
    spare = acc.shape[0] - 1
    tokens = tok_ref.shape[0]
    n_cols = give_slots(cand, slot_of, used, spare)

    def zero(i, carry):
        acc[i] = jnp.zeros(acc.shape[1:], jnp.float32)
        return carry

    lax.fori_loop(0, spare + 1, zero, 0, unroll=5)
    count = choose_blocks(places, slot_of, rows, slots, offs, spare, MUL)
    copy_other.wait()
    add_products(count, tok_ref, weights, acc, rows, slots, offs, MUL)
    copy_grad.wait()
    position = info[0] + lax.broadcasted_iota(jnp.int32, (tokens, BLK), 0)
    usable = (position < info[1]).astype(jnp.float32)

    def slope(i, carry):
        lanes = pl.ds(pl.multiple_of(used[i] * BLK, BLK), BLK)
        given = grad[:, lanes].astype(jnp.float32)
        preact = first[i] + acc[i]
        pre[i] = (given * gelu_slope(preact) * usable).astype(jnp.bfloat16)
        return carry

    lax.fori_loop(0, n_cols, slope, 0)

    def gradient(q, carry):
        y, z = q // NZL, q % NZL
        for core in range(NC):
            j = q * NC + core
            row = pl.multiple_of(cand[2 * j] * BLK, BLK)
            part = lax.dot_general(
                tok_ref[:, pl.ds(row, BLK)],
                pre[slot_of[cand[2 * j + 1]]],
                (((0,), (0,)), ((), ())),
                preferred_element_type=jnp.float32,
            ).astype(jnp.bfloat16)
            for x in range(NX):
                out_ref[core, x, y, z] = part[x * 32 : (x + 1) * 32]
        return carry

    lax.fori_loop(0, cand.shape[0] // (2 * NC), gradient, 0, unroll=4)


def lists(cols, cands, stored):
    smem = lambda count: pltpu.SMEM((count,), jnp.int32)
    return [smem(cols), smem(cands + 8)] + [smem(stored + 2 * MUL)] * 3


VMEM = pl.BlockSpec(memory_space=pltpu.VMEM)
ANY = pl.BlockSpec(memory_space=pl.ANY)


def first_half(tokens, own, places, cand, col_blocks):
    stored, cands = places.shape[0] // 2, cand.shape[0] // 2
    rows_dev = tokens.shape[0]
    return pl.pallas_call(
        first_kernel,
        out_shape=jax.ShapeDtypeStruct((cands + 1, rows_dev, BLK), jnp.float32),
        grid_spec=pltpu.PrefetchScalarGridSpec(
            num_scalar_prefetch=2,
            grid=(),
            in_specs=[VMEM, ANY],
            out_specs=VMEM,
            scratch_shapes=[pltpu.VMEM(own.shape, jnp.bfloat16)]
            + lists(col_blocks, cands, stored)
            + [pltpu.SemaphoreType.DMA((1,))],
        ),
        compiler_params=pltpu.CompilerParams(vmem_limit_bytes=20 * 1024 * 1024),
        cost_estimate=pl.CostEstimate(
            flops=2 * stored * rows_dev * BLK * BLK, bytes_accessed=10_000_000, transcendentals=0
        ),
    )(places, cand, tokens, own)


def second_half(tokens, out_grad, other, first, places, cand, info):
    stored, cands = places.shape[0] // 2, cand.shape[0] // 2
    col_blocks = out_grad.shape[1] // BLK
    rows_dev = tokens.shape[0]
    return pl.pallas_call(
        second_kernel,
        out_shape=jax.ShapeDtypeStruct((NC, NX, NY, NZL, BLK // NX, BLK), jnp.bfloat16),
        grid_spec=pltpu.PrefetchScalarGridSpec(
            num_scalar_prefetch=3,
            grid=(),
            in_specs=[VMEM, ANY, ANY, VMEM],
            out_specs=VMEM,
            scratch_shapes=[
                pltpu.VMEM(other.shape, jnp.bfloat16),
                pltpu.VMEM(out_grad.shape, jnp.bfloat16),
                pltpu.VMEM((cands + 1, rows_dev, BLK), jnp.float32),
                pltpu.VMEM((cands, rows_dev, BLK), jnp.bfloat16),
            ]
            + lists(col_blocks, cands, stored)
            + [pltpu.SemaphoreType.DMA((2,))],
        ),
        compiler_params=pltpu.CompilerParams(vmem_limit_bytes=32 * 1024 * 1024),
        cost_estimate=pl.CostEstimate(
            flops=2 * (stored + cands) * rows_dev * BLK * BLK,
            bytes_accessed=15_000_000,
            transcendentals=2_000_000,
        ),
    )(places, cand, info, tokens, out_grad, other, first)


def per_device(
    tokens, out_grad, block_values, active_blocks, drop_slots, cand_blocks, group_counts
):
    rows_dev = tokens.shape[0]
    me = {name: lax.axis_index(name) for name in AXES}
    slots = lax.broadcasted_iota(jnp.int32, (block_values.shape[0],), 0)
    mine = slots == me["x"] + (me["x"] >= drop_slots).astype(jnp.int32)
    block = jnp.sum(jnp.where(mine[:, None, None], block_values, 0), axis=0)
    place = jnp.sum(jnp.where(mine[:, None], active_blocks, 0), axis=0)
    tail = jnp.pad(place.astype(jnp.bfloat16)[None, :], ((0, 7), (0, BLK - 2)))
    piece = jnp.concatenate([block, tail], axis=0)
    along_z = to_all(piece, AXES, NZL, runs_along_z())
    tails = jnp.pad(along_z[:, BLK, :], ((0, TAIL - NZL), (0, 0)))
    pack = jnp.concatenate([along_z[:, :BLK, :].reshape(NZL * BLK, BLK), tails], axis=0)
    line = to_all(pack, AXES, 4, lines("yx"))
    plane = to_all(line.reshape(4 * PIECE, BLK), AXES, 4, lines("xy")).reshape(16 * PIECE, BLK)
    other = lax.ppermute(plane, "c", [(0, 1), (1, 0)])

    def places_of(part):
        part = part.reshape(16, PIECE, BLK)[:, NZL * BLK : NZL * BLK + NZL, :2]
        return part.astype(jnp.int32).reshape(-1)

    cand = cand_blocks.reshape(-1)
    fsdp = (me["y"] * NZL + me["zl"]) * NC + me["c"]
    info = jnp.stack([fsdp * rows_dev, group_counts[0]]).astype(jnp.int32)
    first = first_half(tokens, plane, places_of(plane), cand, out_grad.shape[1] // BLK)
    partial = second_half(tokens, out_grad, other, first, places_of(other), cand, info)
    pair = lax.all_to_all(partial, "c", 0, 0, tiled=True)
    mine = jnp.sum(pair.astype(jnp.float32), axis=0).astype(jnp.bfloat16)
    mine = mine.reshape(NX * NY, NZL, BLK // NX, BLK)
    planes = lax.all_to_all(mine, ("x", "y"), 0, 0, tiled=True)
    strip = jnp.sum(planes.astype(jnp.float32), axis=0).astype(jnp.bfloat16)
    strips = jnp.broadcast_to(strip[None], (NZH,) + strip.shape).reshape(NZH * NZL, BLK // NX, BLK)
    strips = lax.all_to_all(strips, ("zh", "zl"), 0, 0, tiled=True)
    summed = jnp.sum(strips.astype(jnp.float32), axis=0)
    whole = to_all(summed, "x", NX).reshape(1, BLK, BLK)
    scale = (rows_dev * NX * NZH * NY * NZL * NC) ** (-0.5)
    cand_grad = whole * scale
    cand_score = jnp.sqrt(jnp.mean(cand_grad * cand_grad, axis=(1, 2)) + 1e-06)
    return (cand_grad, cand_score)


def solution(mesh):
    fine = Mesh(mesh.devices.reshape(SIZES), AXES)
    dp, fsdp = ("x", "zh"), ("y", "zl", "c")
    return jax.shard_map(
        per_device,
        mesh=fine,
        in_specs=(
            P(AXES, None),
            P(AXES, None),
            P(fsdp, None, None),
            P(fsdp, None),
            P(fsdp),
            P(),
            P(dp),
        ),
        out_specs=(P(fsdp, None, None), P(fsdp)),
        check_vma=False,
    )
```

time: 169 us -> 163 us (0.964)
  waiting for transfers between devices: 5.67 us -> 0.01 us
  blocking collectives: 132 us -> 128 us
  local copies, waits for them, and re-layouts: 4.45 us -> 7.52 us
  other arithmetic: 3.51 us -> 5.56 us
    unnamed x9 -> x12, local copies, waits for them, and re-layouts: 0.26 us -> 6.33 us
    ppermute x1, waiting for transfers between devices: 5.67 us -> 0.01 us  [per_device(): other = lax.ppermute(plane, 'c', [(0, 1), (1, 0)])]
    all_to_all x4, blocking collectives: 85.4 us -> 82.9 us  [to_all(): lax.all_to_all(copies, axis, 0, 0, axis_index_groups=groups, tiled=True)]
    reduce_sum x0 -> x2, other arithmetic: none -> 1.81 us  [the longest x1 1.02 us: per_device(): block = jnp.sum(jnp.where(mine[:, None, None], block_values, 0), axis=0)]
    pallas_call x1 -> x2, Pallas kernels: 15.3 us -> 14.3 us  [the longest x1 9.32 us: second_half(): pl.pallas_call(second_kernel, out_shape=jax.ShapeDtypeStruct((NC, NX, NY,...]
  transfers between devices with their start and end apart: 1 -> 1, of which waited for: 1 -> 0; matrix products, arithmetic and copies ran while one was open for 1% -> 1% of each run, Pallas kernels for 0% -> 3%
where the time goes in v2:
time: 163 us; the launch traced here: 162 us
  blocking collectives  128 us (79%)
  Pallas kernels  14.3 us (9%)
  local copies, waits for them, and re-layouts  7.52 us (5%)
  other arithmetic  5.56 us (3%)
  between operations  3.94 us (2%)
  starting transfers between devices  1.91 us (1%)
    all_to_all x4, blocking collectives, to_all(): lax.all_to_all(copies, axis, 0, 0, axis_index_groups=groups, tiled=True)  82.9 us
    all_to_all x1, blocking collectives, per_device(): strips = lax.all_to_all(strips, ('zh', 'zl'), 0, 0, tiled=True)  20.4 us
    all_to_all x1, blocking collectives, per_device(): planes = lax.all_to_all(mine, ('x', 'y'), 0, 0, tiled=True)  19.8 us
    pallas_call x1, Pallas kernels, second_half(): pl.pallas_call(second_kernel, out_shape=jax.ShapeDtypeStruct((NC, NX, NY,...  9.32 us
    unnamed x12, local copies, waits for them, and re-layouts  6.33 us
    all_to_all x1, blocking collectives, per_device(): pair = lax.all_to_all(partial, 'c', 0, 0, tiled=True)  5.42 us
    pallas_call x1, Pallas kernels, first_half(): pl.pallas_call(first_kernel, out_shape=jax.ShapeDtypeStruct((cands + 1, r...  4.97 us
  transfers between devices with their start and end apart: 1, of which 0 were waited for; matrix products, arithmetic and copies ran while one was open for 1% of the time, Pallas kernels for 3%

profile of v2, /device:TPU:24, one launch (start us, length us, event | category | flops | bytes accessed | tf_op | source)
XLA Modules:
  0.0 161.7 jit_solution(12227911920546438153)
XLA Ops:
  1.3 0.8 select_reduce_fusion.1
  2.1 1.0 select_reduce_fusion
  3.2 28.8 %all_to_all.35 = bf16[8,136,128]{2,1,0:T(8,128)(2,1)S(1)} all-to-all(bf16[8,136,128]{2,1,0:T(8,128)(2,1)S(1)} %broadcast_in_dim.62), channel_id=1, replica_groups={{0,2,4,6,8,10,12,14},{64,66,68,70,72,74,76,78},{16,18,20,22,24,26,28,30..., dimensions={0} | all-to-all | bytes 557056 | tf_op jit(solution)/shard_map/all_to_all | solution.py:46
  32.0 0.1 broadcast_in_dim.63
  32.2 13.4 %all_to_all.36 = bf16[4,1040,128]{2,1,0:T(8,128)(2,1)S(1)} all-to-all(bf16[4,1040,128]{2,1,0:T(8,128)(2,1)S(1)} %broadcast_in_dim.63), channel_id=1, replica_groups={{0,16,32,48},{128,144,160,176},{256,272,288,304},{384,400,416,432},{2,1..., dimensions={0} | all-to-all | bytes 2129920 | tf_op jit(solution)/shard_map/all_to_all | solution.py:46
  45.6 0.5 broadcast_in_dim.65
  46.1 0.0 copy-start.4
  46.1 0.0 copy-start.2
  46.2 32.4 %all_to_all.37 = bf16[4,4160,128]{2,1,0:T(8,128)(2,1)} all-to-all(bf16[4,4160,128]{2,1,0:T(8,128)(2,1)S(1)} %broadcast_in_dim.65), channel_id=1, replica_groups={{0,128,256,384},{16,144,272,400},{32,160,288,416},{48,176,304,432},{2,1..., dimensions={0} | all-to-all | bytes 8519680 | tf_op jit(solution)/shard_map/all_to_all | solution.py:46
  78.6 1.9 %collective-permute-start = (bf16[16640,128]{1,0:T(8,128)(2,1)}, bf16[16640,128]{1,0:T(8,128)(2,1)}, u32[]{:S(2)}, u32[]{:S(2)}) collective-permute-start(bf16[16640,128]{1,0:T(8,128)(2,1)} %bitcast.6.own_hbm), channel_id=1, source_target_pairs={{0,1},{1,0},{2,3},{3,2},{4,5},{5,4},{6,7},{7,6},{8,9},{9,8},{10,11... | collective-permute-start | bytes 12779528 | tf_op jit(solution)/shard_map/ppermute | solution.py:257
  80.5 0.0 copy-done.4
  80.5 0.1 copy.15
  80.6 0.1 reshape.81.cand
  81.4 0.1 pad_add_fusion.info
  81.5 0.8 slice_convert_fusion
  82.3 0.1 reshape.89.places
  82.4 0.0 copy-done.2
  82.4 5.0 %shard_map.86.first = f32[65,128,128]{2,1,0:T(8,128)S(1)} custom-call(s32[256]{0:T(256)S(1)} %reshape.89.places, s32[128]{0:T(128)S(1)} %reshape.81.cand, bf16[128,3584]{1,0:T(8,128)(2,1)S(1)} %copy-done.2, bf16[16640,128]{1,0:T(8,128)(2,1)} %bitcast.6.own_hbm), custom_call_target="tpu_custom_call" | custom-call | flops 536870912 | bytes 10000000 | tf_op jit(solution)/shard_map/pallas_call | solution.py:192
  87.4 2.0 %copy-done = f32[65,128,128]{2,1,0:T(8,128)} copy-done((f32[65,128,128]{2,1,0:T(8,128)}, f32[65,128,128]{2,1,0:T(8,128)S(1)}, u32[]{:S(2)}) %copy-start) | copy-done | bytes 4259864
  89.4 0.0 collective-permute-done.other_hbm
  89.4 0.8 slice_convert_fusion.1
  90.1 0.1 reshape.87.places
  90.3 2.2 %copy-done.1 = f32[65,128,128]{2,1,0:T(8,128)S(1)} copy-done((f32[65,128,128]{2,1,0:T(8,128)S(1)}, f32[65,128,128]{2,1,0:T(8,128)}, u32[]{:S(2)}) %copy-start.1) | copy-done | bytes 4259864
  92.5 2.0 %copy-done.3 = bf16[128,14336]{1,0:T(8,128)(2,1)S(1)} copy-done((bf16[128,14336]{1,0:T(8,128)(2,1)S(1)}, bf16[128,14336]{1,0:T(8,128)(2,1)}, u32[]{:S(2)}) %copy-start.3) | copy-done | bytes 3670040
  94.5 9.3 %shard_map.87 = bf16[2,4,4,8,32,128]{5,4,3,2,1,0:T(8,128)(2,1)S(1)} custom-call(s32[256]{0:T(256)S(1)} %reshape.87.places, s32[128]{0:T(128)S(1)} %reshape.81.cand, s32[2]{0:T(128)S(1)} %pad_add_fusion.info, bf16[128,3584]{1,0:T(8,128)(2,1)S(1)} %copy-done.2, bf16[128,14336]{1,0:T(8,128)(2,1)S(1)} %copy-done.3, ...), custom_call_target="tpu_custom_call" | custom-call | flops 805306368 | bytes 15000000 | tf_op jit(solution)/shard_map/pallas_call | solution.py:215
  103.9 5.4 %all_to_all.38 = bf16[2,4,4,8,32,128]{5,4,3,2,1,0:T(8,128)(2,1)S(1)} all-to-all(bf16[2,4,4,8,32,128]{5,4,3,2,1,0:T(8,128)(2,1)S(1)} %shard_map.87), channel_id=1, replica_groups=mesh['x'=4,'zh'=2,'y'=4,'zl'=8,'c'=2] {'c'}, dimensions={0} | all-to-all | bytes 4194304 | tf_op jit(solution)/shard_map/all_to_all | solution.py:268
  109.3 0.7 reduce_sum.65
  110.0 19.8 %all_to_all.39 = bf16[16,8,32,128]{3,2,1,0:T(8,128)(2,1)S(1)} all-to-all(bf16[16,8,32,128]{3,2,1,0:T(8,128)(2,1)S(1)} %bitcast.18), channel_id=1, replica_groups=mesh['x'=4,'zh'=2,'y'=4,'zl'=8,'c'=2] {'x','y'}, dimensions={0} | all-to-all | bytes 2097152 | tf_op jit(solution)/shard_map/all_to_all | solution.py:271
  129.7 0.1 reduce_sum.66
  129.9 20.4 %all_to_all.40 = bf16[16,32,128]{2,1,0:T(8,128)(2,1)S(1)} all-to-all(bf16[16,32,128]{2,1,0:T(8,128)(2,1)S(1)} %bitcast.20), channel_id=1, replica_groups=mesh['x'=4,'zh'=2,'y'=4,'zl'=8,'c'=2] {'zh','zl'}, dimensions={0} | all-to-all | bytes 262144 | tf_op jit(solution)/shard_map/all_to_all | solution.py:274
  150.3 8.3 %all_to_all.41 = f32[4,32,128]{2,1,0:T(8,128)S(1)} all-to-all(f32[4,32,128]{2,1,0:T(8,128)S(1)} %broadcast_in_dim.67), channel_id=1, replica_groups=mesh['x'=4,'zh'=2,'y'=4,'zl'=8,'c'=2] {'x'}, dimensions={0} | all-to-all | bytes 131072 | tf_op jit(solution)/shard_map/all_to_all | solution.py:46
  158.6 1.2 multiply_reduce_fusion
  (14 shorter events, 0.2 us)
Async XLA Ops:
  46.1 34.4 %copy-start.4 = (s32[64,2]{0,1:T(2,128)S(1)}, s32[64,2]{0,1:T(2,128)}, u32[]{:S(2)}) copy-start(s32[64,2]{0,1:T(2,128)} %param.12) | copy-start | bytes 1540
  46.1 36.3 %copy-start.2 = (bf16[128,3584]{1,0:T(8,128)(2,1)S(1)}, bf16[128,3584]{1,0:T(8,128)(2,1)}, u32[]{:S(2)}) copy-start(bf16[128,3584]{1,0:T(8,128)(2,1)} %tok_ref.3) | copy-start | bytes 2752516
  78.6 10.8 %collective-permute-start = (bf16[16640,128]{1,0:T(8,128)(2,1)}, bf16[16640,128]{1,0:T(8,128)(2,1)}, u32[]{:S(2)}, u32[]{:S(2)}) collective-permute-start(bf16[16640,128]{1,0:T(8,128)(2,1)} %bitcast.6.own_hbm), channel_id=1, source_target_pairs={{0,1},{1,0},{2,3},{3,2},{4,5},{5,4},{6,7},{7,6},{8,9},{9,8},{10,11... | collective-permute-start | bytes 12779528 | tf_op jit(solution)/shard_map/ppermute | solution.py:257
  87.4 2.0 %copy-start = (f32[65,128,128]{2,1,0:T(8,128)}, f32[65,128,128]{2,1,0:T(8,128)S(1)}, u32[]{:S(2)}) copy-start(f32[65,128,128]{2,1,0:T(8,128)S(1)} %shard_map.86.first) | copy-start | bytes 12779524
  90.3 2.2 %copy-start.1 = (f32[65,128,128]{2,1,0:T(8,128)S(1)}, f32[65,128,128]{2,1,0:T(8,128)}, u32[]{:S(2)}) copy-start(f32[65,128,128]{2,1,0:T(8,128)} %copy-done) | copy-start | bytes 12779524
  92.5 2.0 %copy-start.3 = (bf16[128,14336]{1,0:T(8,128)(2,1)S(1)}, bf16[128,14336]{1,0:T(8,128)(2,1)}, u32[]{:S(2)}) copy-start(bf16[128,14336]{1,0:T(8,128)(2,1)} %grad_hbm.1) | copy-start | bytes 11010052

commit v3 on v2

v3 whole, which is shorter than its diff:
```python
import jax
import jax.numpy as jnp
from jax import lax
from jax.experimental import pallas as pl
from jax.experimental.pallas import tpu as pltpu
from jax.sharding import Mesh, PartitionSpec as P

AXES = ("x", "zh", "y", "zl", "c")
SIZES = (4, 2, 4, 8, 2)
NX, NZH, NY, NZL, NC = SIZES
BLK = 128
TAIL = 16
PIECE = NZL * BLK + TAIL
MUL = 8
LIMIT1 = 20
LIMIT2 = 24


def flat(x, zh, y, zl, c):
    return (((x * NZH + zh) * NY + y) * NZL + zl) * NC + c


def runs_along_z():
    return [
        [flat(x, (z // NZL) % NZH, y, z % NZL, c) for z in range(start, start + NZL)]
        for c in range(NC)
        for x in range(NX)
        for y in range(NY)
        for start in (4 * c, 4 * c + NZL)
    ]


def lines(axis_of_core):
    groups = []
    for c, axis in enumerate(axis_of_core):
        for zh in range(NZH):
            for zl in range(NZL):
                for other in range(4):
                    if axis == "y":
                        groups.append([flat(other, zh, y, zl, c) for y in range(NY)])
                    else:
                        groups.append([flat(x, zh, other, zl, c) for x in range(NX)])
    return groups


def to_all(value, axis, count, groups=None):
    copies = jnp.broadcast_to(value[None], (count,) + value.shape)
    return lax.all_to_all(copies, axis, 0, 0, axis_index_groups=groups, tiled=True)


def gelu_slope(value_in):
    normal_cdf = 0.5 * (1.0 + lax.erf(value_in * 0.7071067811865476))
    density = jnp.exp(-0.5 * value_in * value_in) * 0.3989422804014327
    return normal_cdf + value_in * density


def tails_copy(pack_hbm, tails, sem):
    return pltpu.make_async_copy(pack_hbm.at[:, pl.ds(NZL * BLK, TAIL), :], tails, sem)


def read_places(tails, numbers, places, sem):
    row = lax.broadcasted_iota(jnp.int32, (TAIL, BLK), 0)
    table = jnp.zeros((TAIL, BLK), jnp.float32)
    for p in range(tails.shape[0]):
        table = jnp.where(row == p, tails[p].astype(jnp.float32), table)
    numbers[...] = table.astype(jnp.int32)
    move = pltpu.make_async_copy(numbers, places, sem)
    move.start()
    move.wait()


def choose_blocks(places, slot_of, rows, slots, offs, spare, unroll):
    def choose(pack, count):
        found = [places[pack, 2 * z + 1] for z in range(NZL)]
        found = [slot_of[col] for col in found]
        where = [places[pack, 2 * z] for z in range(NZL)]
        for z in range(NZL):
            rows[count] = where[z]
            slots[count] = found[z]
            offs[count] = pack * NZL + z
            count = count + (found[z] != spare).astype(jnp.int32)
        return count

    count = lax.fori_loop(0, places.shape[0], choose, 0, unroll=2)
    for u in range(unroll):
        rows[count + u] = 0
        slots[count + u] = spare
        offs[count + u] = 0
    return count


def give_slots(cand, slot_of, spare):
    def clear(i, carry):
        slot_of[i] = spare
        return carry

    lax.fori_loop(0, slot_of.shape[0], clear, 0, unroll=8)

    def mark(j, count):
        col = cand[1, j]
        had = slot_of[col]
        fresh = had == spare
        slot_of[col] = jnp.where(fresh, count, had)
        return count + fresh.astype(jnp.int32)

    return lax.fori_loop(0, cand.shape[1], mark, 0, unroll=4)


def add_products(count, tok_ref, weights, acc, rows, slots, offs, unroll):
    def multiply(step, carry):
        products = []
        for u in range(unroll):
            i = step * unroll + u
            row = pl.multiple_of(rows[i] * BLK, BLK)
            pack = offs[i] // NZL
            off = pl.multiple_of(offs[i] % NZL * BLK, BLK)
            products.append(
                jnp.dot(
                    tok_ref[:, pl.ds(row, BLK)],
                    weights[pack, pl.ds(off, BLK), :],
                    preferred_element_type=jnp.float32,
                )
            )
        for u in range(unroll):
            acc[slots[step * unroll + u]] += products[u]
        return carry

    lax.fori_loop(0, (count + unroll - 1) // unroll, multiply, 0)


def piece_kernel(drop, active, blocks, out_ref, block, sem):
    slot = lax.axis_index("x")
    slot = slot + (slot >= drop[0]).astype(jnp.int32)
    fetch = pltpu.make_async_copy(blocks.at[slot], block, sem)
    fetch.start()
    lane = lax.broadcasted_iota(jnp.int32, (TAIL, BLK), 1)
    spot = 2 * ((lax.axis_index("zl") + 4 * lax.axis_index("c")) % NZL)
    tail = jnp.where(lane == spot, active[0, slot], 0)
    tail = jnp.where(lane == spot + 1, active[1, slot], tail)
    tail = tail.astype(jnp.float32).astype(jnp.bfloat16)
    for e in range(NZL):
        out_ref[e, pl.ds(BLK, TAIL), :] = tail
    fetch.wait()
    for e in range(NZL):
        out_ref[e, pl.ds(0, BLK), :] = block[...]


def first_pieces(drop, active, blocks):
    return pl.pallas_call(
        piece_kernel,
        out_shape=jax.ShapeDtypeStruct((NZL, BLK + TAIL, BLK), jnp.bfloat16),
        grid_spec=pltpu.PrefetchScalarGridSpec(
            num_scalar_prefetch=2,
            grid=(),
            in_specs=[ANY],
            out_specs=VMEM,
            scratch_shapes=[pltpu.VMEM((BLK, BLK), jnp.bfloat16), pltpu.SemaphoreType.DMA],
        ),
        compiler_params=pltpu.CompilerParams(vmem_limit_bytes=16 * 1024 * 1024),
    )(drop, active, blocks)


def first_kernel(
    cand, tok_ref, own_hbm, acc,
    weights, tails, numbers, places, slot_of, rows, slots, offs, sem,
):
    copy_own = pltpu.make_async_copy(own_hbm, weights, sem.at[0])
    copy_tails = tails_copy(own_hbm, tails, sem.at[1])
    copy_tails.start()
    copy_own.start()
    spare = acc.shape[0] - 1
    give_slots(cand, slot_of, spare)

    copy_tails.wait()
    read_places(tails, numbers, places, sem.at[1])

    def zero(i, carry):
        acc[i] = jnp.zeros(acc.shape[1:], jnp.float32)
        return carry

    lax.fori_loop(0, spare + 1, zero, 0, unroll=5)
    count = choose_blocks(places, slot_of, rows, slots, offs, spare, MUL)
    copy_own.wait()
    add_products(count, tok_ref, weights, acc, rows, slots, offs, MUL)


def second_kernel(
    cand, info, tok_ref, other_hbm, first, grad_ref, send_ref, keep_ref,
    weights, acc, tails, numbers, places, slot_of, rows, slots, offs, sem,
):
    copy_other = pltpu.make_async_copy(other_hbm, weights, sem.at[0])
    copy_tails = tails_copy(other_hbm, tails, sem.at[1])
    copy_tails.start()
    copy_other.start()
    spare = acc.shape[0] - 1
    tokens = tok_ref.shape[0]
    give_slots(cand, slot_of, spare)

    def zero(i, carry):
        acc[i] = jnp.zeros(acc.shape[1:], jnp.float32)
        return carry

    lax.fori_loop(0, spare + 1, zero, 0, unroll=5)
    copy_tails.wait()
    read_places(tails, numbers, places, sem.at[1])
    count = choose_blocks(places, slot_of, rows, slots, offs, spare, MUL)
    copy_other.wait()
    add_products(count, tok_ref, weights, acc, rows, slots, offs, MUL)
    position = info[0] + lax.broadcasted_iota(jnp.int32, (tokens, BLK), 0)
    usable = (position < info[1]).astype(jnp.float32)

    def gradient(q, carry):
        y, z = q // NZL, q % NZL
        for out_ref, core in ((send_ref, 1 - info[2]), (keep_ref, info[2])):
            j = q * NC + core
            col = cand[1, j]
            slot = slot_of[col]
            lanes = pl.ds(pl.multiple_of(col * BLK, BLK), BLK)
            slope = gelu_slope(first[slot] + acc[slot])
            given = grad_ref[:, lanes].astype(jnp.float32)
            row = pl.multiple_of(cand[0, j] * BLK, BLK)
            part = lax.dot_general(
                tok_ref[:, pl.ds(row, BLK)],
                (given * slope * usable).astype(jnp.bfloat16),
                (((0,), (0,)), ((), ())),
                preferred_element_type=jnp.float32,
            ).astype(jnp.bfloat16)
            for x in range(NX):
                out_ref[x, y, z] = part[x * 32 : (x + 1) * 32]
        return carry

    lax.fori_loop(0, cand.shape[1] // NC, gradient, 0, unroll=4)


def place_scratch(packs):
    return [
        pltpu.VMEM((packs, TAIL, BLK), jnp.bfloat16),
        pltpu.VMEM((TAIL, BLK), jnp.int32),
        pltpu.SMEM((TAIL, BLK), jnp.int32),
    ]


def lists(cols, stored):
    smem = lambda count: pltpu.SMEM((count,), jnp.int32)
    return [smem(cols)] + [smem(stored + 2 * MUL)] * 3


VMEM = pl.BlockSpec(memory_space=pltpu.VMEM)
ANY = pl.BlockSpec(memory_space=pl.ANY)


def first_half(tokens, own, cand, col_blocks):
    packs, cands = own.shape[0], cand.shape[1]
    rows_dev = tokens.shape[0]
    return pl.pallas_call(
        first_kernel,
        out_shape=jax.ShapeDtypeStruct((cands + 1, rows_dev, BLK), jnp.float32),
        grid_spec=pltpu.PrefetchScalarGridSpec(
            num_scalar_prefetch=1,
            grid=(),
            in_specs=[VMEM, ANY],
            out_specs=VMEM,
            scratch_shapes=[pltpu.VMEM(own.shape, jnp.bfloat16)]
            + place_scratch(packs)
            + lists(col_blocks, packs * NZL)
            + [pltpu.SemaphoreType.DMA((2,))],
        ),
        compiler_params=pltpu.CompilerParams(vmem_limit_bytes=LIMIT1 * 1024 * 1024),
        cost_estimate=pl.CostEstimate(
            flops=2 * packs * NZL * rows_dev * BLK * BLK,
            bytes_accessed=10_000_000,
            transcendentals=0,
        ),
    )(cand, tokens, own)


def second_half(tokens, other, first, out_grad, cand, info):
    packs, cands = other.shape[0], cand.shape[1]
    col_blocks = out_grad.shape[1] // BLK
    rows_dev = tokens.shape[0]
    part = jax.ShapeDtypeStruct((NX, NY, NZL, BLK // NX, BLK), jnp.bfloat16)
    return pl.pallas_call(
        second_kernel,
        out_shape=(part, part),
        grid_spec=pltpu.PrefetchScalarGridSpec(
            num_scalar_prefetch=2,
            grid=(),
            in_specs=[VMEM, ANY, VMEM, VMEM],
            out_specs=(VMEM, VMEM),
            scratch_shapes=[
                pltpu.VMEM(other.shape, jnp.bfloat16),
                pltpu.VMEM((cands + 1, rows_dev, BLK), jnp.float32),
            ]
            + place_scratch(packs)
            + lists(col_blocks, packs * NZL)
            + [pltpu.SemaphoreType.DMA((2,))],
        ),
        compiler_params=pltpu.CompilerParams(vmem_limit_bytes=LIMIT2 * 1024 * 1024),
        cost_estimate=pl.CostEstimate(
            flops=2 * (packs * NZL + cands) * rows_dev * BLK * BLK,
            bytes_accessed=15_000_000,
            transcendentals=2_000_000,
        ),
    )(cand, info, tokens, other, first, out_grad)


def per_device(
    tokens, out_grad, block_values, active_blocks, drop_slots, cand_blocks, group_counts
):
    rows_dev = tokens.shape[0]
    me = {name: lax.axis_index(name) for name in AXES}
    pieces = first_pieces(drop_slots, active_blocks.T, block_values)
    along_z = lax.all_to_all(
        pieces, AXES, 0, 0, axis_index_groups=runs_along_z(), tiled=True
    )
    tail = jnp.sum(along_z[:, BLK:, :], axis=0)
    pack = jnp.concatenate([along_z[:, :BLK, :].reshape(NZL * BLK, BLK), tail], axis=0)
    line = to_all(pack, AXES, 4, lines("yx"))
    plane = to_all(line.reshape(4 * PIECE, BLK), AXES, 4, lines("xy")).reshape(16, PIECE, BLK)
    other = lax.ppermute(plane, "c", [(0, 1), (1, 0)])
    cand = cand_blocks.T
    fsdp = (me["y"] * NZL + me["zl"]) * NC + me["c"]
    info = jnp.stack([fsdp * rows_dev, group_counts[0], me["c"]]).astype(jnp.int32)
    first = first_half(tokens, plane, cand, out_grad.shape[1] // BLK)
    send, keep = second_half(tokens, other, first, out_grad, cand, info)
    given = lax.ppermute(send, "c", [(0, 1), (1, 0)])
    mine = (keep.astype(jnp.float32) + given.astype(jnp.float32)).astype(jnp.bfloat16)
    mine = mine.reshape(NX * NY, NZL, BLK // NX, BLK)
    planes = lax.all_to_all(mine, ("x", "y"), 0, 0, tiled=True)
    strip = jnp.sum(planes.astype(jnp.float32), axis=0).astype(jnp.bfloat16)
    strips = jnp.broadcast_to(strip[None], (NZH,) + strip.shape).reshape(NZH * NZL, BLK // NX, BLK)
    strips = lax.all_to_all(strips, ("zh", "zl"), 0, 0, tiled=True)
    summed = jnp.sum(strips.astype(jnp.float32), axis=0)
    whole = to_all(summed, "x", NX).reshape(1, BLK, BLK)
    scale = (rows_dev * NX * NZH * NY * NZL * NC) ** (-0.5)
    cand_grad = whole * scale
    cand_score = jnp.sqrt(jnp.mean(cand_grad * cand_grad, axis=(1, 2)) + 1e-06)
    return (cand_grad, cand_score)


def solution(mesh):
    fine = Mesh(mesh.devices.reshape(SIZES), AXES)
    dp, fsdp = ("x", "zh"), ("y", "zl", "c")
    return jax.shard_map(
        per_device,
        mesh=fine,
        in_specs=(
            P(AXES, None),
            P(AXES, None),
            P(fsdp, None, None),
            P(fsdp, None),
            P(fsdp),
            P(),
            P(dp),
        ),
        out_specs=(P(fsdp, None, None), P(fsdp)),
        check_vma=False,
    )
```

time: 163 us -> 156 us (0.957)
  local copies, waits for them, and re-layouts: 7.52 us -> 2.34 us
  blocking collectives: 128 us -> 123 us
  waiting for transfers between devices: 0.01 us -> 4.49 us
  other arithmetic: 5.56 us -> 1.81 us
  starting transfers between devices: 1.91 us -> 3.83 us
    all_to_all x4 -> x3, blocking collectives: 82.9 us -> 54.1 us  [to_all(): lax.all_to_all(copies, axis, 0, 0, axis_index_groups=groups, tiled=True)]
    all_to_all x1, blocking collectives: 5.42 us -> 29.1 us  [per_device(): lax.all_to_all(pieces, AXES, 0, 0, axis_index_groups=runs_along_z(), tile...]
    unnamed x12 -> x10, local copies, waits for them, and re-layouts: 6.33 us -> 1.6 us
    ppermute x0 -> x1, waiting for transfers between devices: none -> 2.63 us  [per_device(): given = lax.ppermute(send, 'c', [(0, 1), (1, 0)])]
    reduce_sum x3 -> x1, other arithmetic: 2.5 us -> 0.01 us  [per_device(): tail = jnp.sum(along_z[:, BLK:, :], axis=0)]
    ppermute x0 -> x1, starting transfers between devices: none -> 1.92 us  [per_device(): given = lax.ppermute(send, 'c', [(0, 1), (1, 0)])]
    ppermute x1, waiting for transfers between devices: 0.01 us -> 1.86 us  [per_device(): other = lax.ppermute(plane, 'c', [(0, 1), (1, 0)])]
    pallas_call x1 -> x2, Pallas kernels: 9.32 us -> 9.33 us  [the longest x1 8.67 us: second_half(): pl.pallas_call(second_kernel, out_shape=(part, part), grid_spec=pltpu.Pre...]
  transfers between devices with their start and end apart: 1 -> 2, of which waited for: 0 -> 2; matrix products, arithmetic and copies ran while one was open for 1% -> 0% of each run, Pallas kernels for 3% -> 3%
where the time goes in v3:
time: 156 us; the launch traced here: 154 us
  blocking collectives  123 us (79%)
  Pallas kernels  14.3 us (9%)
  waiting for transfers between devices  4.49 us (3%)
  between operations  3.88 us (2%)
  starting transfers between devices  3.83 us (2%)
  local copies, waits for them, and re-layouts  2.34 us (2%)
  other arithmetic  1.81 us (1%)
    all_to_all x3, blocking collectives, to_all(): lax.all_to_all(copies, axis, 0, 0, axis_index_groups=groups, tiled=True)  54.1 us
    all_to_all x1, blocking collectives, per_device(): lax.all_to_all(pieces, AXES, 0, 0, axis_index_groups=runs_along_z(), tile...  29.1 us
    all_to_all x1, blocking collectives, per_device(): strips = lax.all_to_all(strips, ('zh', 'zl'), 0, 0, tiled=True)  20.4 us
    all_to_all x1, blocking collectives, per_device(): planes = lax.all_to_all(mine, ('x', 'y'), 0, 0, tiled=True)  19.8 us
    pallas_call x1, Pallas kernels, second_half(): pl.pallas_call(second_kernel, out_shape=(part, part), grid_spec=pltpu.Pre...  8.67 us
    pallas_call x1, Pallas kernels, first_half(): pl.pallas_call(first_kernel, out_shape=jax.ShapeDtypeStruct((cands + 1, r...  4.95 us
  transfers between devices with their start and end apart: 2, of which 2 were waited for; matrix products, arithmetic and copies ran while one was open for 0% of the time, Pallas kernels for 3%

profile of v3, /device:TPU:24, one launch (start us, length us, event | category | flops | bytes accessed | tf_op | source)
XLA Modules:
  0.0 154.0 jit_solution(13332202522374912749)
XLA Ops:
  1.3 0.0 copy-start.2
  1.3 0.9 copy-done.2
  2.2 0.0 copy-start.4
  2.2 0.7 copy-done.4
  2.9 0.7 shard_map.86
  3.5 29.1 %all_to_all.30 = bf16[8,144,128]{2,1,0:T(8,128)(2,1)S(1)} all-to-all(bf16[8,144,128]{2,1,0:T(8,128)(2,1)S(1)} %shard_map.86), channel_id=1, replica_groups={{0,2,4,6,8,10,12,14},{64,66,68,70,72,74,76,78},{16,18,20,22,24,26,28,30..., dimensions={0} | all-to-all | bytes 589824 | tf_op jit(solution)/shard_map/all_to_all | solution.py:313
  32.7 0.1 broadcast_in_dim.10
  32.8 13.4 %all_to_all.31 = bf16[4,1040,128]{2,1,0:T(8,128)(2,1)S(1)} all-to-all(bf16[4,1040,128]{2,1,0:T(8,128)(2,1)S(1)} %broadcast_in_dim.10), channel_id=1, replica_groups={{0,16,32,48},{128,144,160,176},{256,272,288,304},{384,400,416,432},{2,1..., dimensions={0} | all-to-all | bytes 2129920 | tf_op jit(solution)/shard_map/all_to_all | solution.py:48
  46.2 0.5 broadcast_in_dim.12
  46.8 0.0 copy-start
  46.8 0.0 copy-start.3
  46.8 32.4 %all_to_all.32 = bf16[4,4160,128]{2,1,0:T(8,128)(2,1)} all-to-all(bf16[4,4160,128]{2,1,0:T(8,128)(2,1)S(1)} %broadcast_in_dim.12), channel_id=1, replica_groups={{0,128,256,384},{16,144,272,400},{32,160,288,416},{48,176,304,432},{2,1..., dimensions={0} | all-to-all | bytes 8519680 | tf_op jit(solution)/shard_map/all_to_all | solution.py:48
  79.2 1.9 %collective-permute-start = (bf16[16,1040,128]{2,1,0:T(8,128)(2,1)}, bf16[16,1040,128]{2,1,0:T(8,128)(2,1)}, u32[]{:S(2)}, u32[]{:S(2)}) collective-permute-start(bf16[16,1040,128]{2,1,0:T(8,128)(2,1)} %bitcast.6.own_hbm), channel_id=1, source_target_pairs={{0,1},{1,0},{2,3},{3,2},{4,5},{5,4},{6,7},{7,6},{8,9},{9,8},{10,11... | collective-permute-start | bytes 12779528 | tf_op jit(solution)/shard_map/ppermute | solution.py:320
  81.8 0.1 pad_add_fusion.info
  81.9 0.0 copy-done
  81.9 0.0 copy-done.3
  81.9 0.0 copy-start.1
  81.9 4.9 %shard_map.87.first = f32[65,128,128]{2,1,0:T(8,128)S(1)} custom-call(s32[2,64]{1,0:T(2,128)S(1)} %bitcast.11, bf16[128,3584]{1,0:T(8,128)(2,1)S(1)} %copy-done, bf16[16,1040,128]{2,1,0:T(8,128)(2,1)} %bitcast.6.own_hbm), custom_call_target="tpu_custom_call" | custom-call | flops 536870912 | bytes 10000000 | tf_op jit(solution)/shard_map/pallas_call | solution.py:255
  86.9 1.9 %collective-permute-done.other_hbm = bf16[16,1040,128]{2,1,0:T(8,128)(2,1)} collective-permute-done((bf16[16,1040,128]{2,1,0:T(8,128)(2,1)}, bf16[16,1040,128]{2,1,0:T(8,128)(2,1)}, u32[]{:S(2)}, u32[]{:S(2)}) %collective-permute-start) | collective-permute-done | bytes 4259872 | tf_op jit(solution)/shard_map/ppermute | solution.py:320
  88.7 0.0 copy-done.1
  88.7 8.7 %shard_map.88 = (bf16[4,4,8,32,128]{4,3,2,1,0:T(8,128)(2,1)S(1)}, bf16[4,4,8,32,128]{4,3,2,1,0:T(8,128)(2,1)S(1)}) custom-call(s32[2,64]{1,0:T(2,128)S(1)} %bitcast.12, s32[3]{0:T(128)S(1)} %pad_add_fusion.info, bf16[128,3584]{1,0:T(8,128)(2,1)S(1)} %copy-done, bf16[16,1040,128]{2,1,0:T(8,128)(2,1)} %collective-permute-done.other_hbm, ...), custom_call_target="tpu_custom_call" | custom-call | flops 805306368 | bytes 15000000 | tf_op jit(solution)/shard_map/pallas_call | solution.py:282
  97.4 1.9 %collective-permute-start.1 = (bf16[4,4,8,32,128]{4,3,2,1,0:T(8,128)(2,1)S(1)}, bf16[4,4,8,32,128]{4,3,2,1,0:T(8,128)(2,1)S(1)}, u32[]{:S(2)}, u32[]{:S(2)}) collective-permute-start(bf16[4,4,8,32,128]{4,3,2,1,0:T(8,128)(2,1)S(1)} %get-tuple-element.5), channel_id=1, source_target_pairs={{0,1},{1,0},{2,3},{3,2},{4,5},{5,4},{6,7},{7,6},{8,9},{9,8},{10,11... | collective-permute-start | bytes 3145736 | tf_op jit(solution)/shard_map/ppermute | solution.py:326
  99.3 2.6 %collective-permute-done.1 = bf16[4,4,8,32,128]{4,3,2,1,0:T(8,128)(2,1)S(1)} collective-permute-done((bf16[4,4,8,32,128]{4,3,2,1,0:T(8,128)(2,1)S(1)}, bf16[4,4,8,32,128]{4,3,2,1,0:T(8,128)(2,1)S(1)}, u32[]{:S(2)}, u32[]{:S(2)}) %collective-permute-start.1) | collective-permute-done | bytes 1048608 | tf_op jit(solution)/shard_map/ppermute | solution.py:326
  102.0 0.3 add_convert_fusion
  102.3 19.8 %all_to_all.33 = bf16[16,8,32,128]{3,2,1,0:T(8,128)(2,1)S(1)} all-to-all(bf16[16,8,32,128]{3,2,1,0:T(8,128)(2,1)S(1)} %bitcast.15), channel_id=1, replica_groups=mesh['x'=4,'zh'=2,'y'=4,'zl'=8,'c'=2] {'x','y'}, dimensions={0} | all-to-all | bytes 2097152 | tf_op jit(solution)/shard_map/all_to_all | solution.py:329
  122.0 0.1 reduce_sum.43
  122.2 20.4 %all_to_all.34 = bf16[16,32,128]{2,1,0:T(8,128)(2,1)S(1)} all-to-all(bf16[16,32,128]{2,1,0:T(8,128)(2,1)S(1)} %bitcast.17), channel_id=1, replica_groups=mesh['x'=4,'zh'=2,'y'=4,'zl'=8,'c'=2] {'zh','zl'}, dimensions={0} | all-to-all | bytes 262144 | tf_op jit(solution)/shard_map/all_to_all | solution.py:332
  142.6 8.3 %all_to_all.35 = f32[4,32,128]{2,1,0:T(8,128)S(1)} all-to-all(f32[4,32,128]{2,1,0:T(8,128)S(1)} %broadcast_in_dim.14), channel_id=1, replica_groups=mesh['x'=4,'zh'=2,'y'=4,'zl'=8,'c'=2] {'x'}, dimensions={0} | all-to-all | bytes 131072 | tf_op jit(solution)/shard_map/all_to_all | solution.py:48
  150.9 1.2 multiply_reduce_fusion
  (6 shorter events, 0.1 us)
Async XLA Ops:
  1.3 0.9 copy-start.2
  2.2 0.7 copy-start.4
  46.8 35.1 %copy-start = (bf16[128,3584]{1,0:T(8,128)(2,1)S(1)}, bf16[128,3584]{1,0:T(8,128)(2,1)}, u32[]{:S(2)}) copy-start(bf16[128,3584]{1,0:T(8,128)(2,1)} %tok_ref.3) | copy-start | bytes 2752516
  46.8 35.1 %copy-start.3 = (s32[64,2]{0,1:T(2,128)S(1)}, s32[64,2]{0,1:T(2,128)}, u32[]{:S(2)}) copy-start(s32[64,2]{0,1:T(2,128)} %param.12) | copy-start | bytes 1540
  79.2 9.5 %collective-permute-start = (bf16[16,1040,128]{2,1,0:T(8,128)(2,1)}, bf16[16,1040,128]{2,1,0:T(8,128)(2,1)}, u32[]{:S(2)}, u32[]{:S(2)}) collective-permute-start(bf16[16,1040,128]{2,1,0:T(8,128)(2,1)} %bitcast.6.own_hbm), channel_id=1, source_target_pairs={{0,1},{1,0},{2,3},{3,2},{4,5},{5,4},{6,7},{7,6},{8,9},{9,8},{10,11... | collective-permute-start | bytes 12779528 | tf_op jit(solution)/shard_map/ppermute | solution.py:320
  81.9 6.8 %copy-start.1 = (bf16[128,14336]{1,0:T(8,128)(2,1)S(1)}, bf16[128,14336]{1,0:T(8,128)(2,1)}, u32[]{:S(2)}) copy-start(bf16[128,14336]{1,0:T(8,128)(2,1)} %grad_ref.1) | copy-start | bytes 11010052
  97.4 4.6 %collective-permute-start.1 = (bf16[4,4,8,32,128]{4,3,2,1,0:T(8,128)(2,1)S(1)}, bf16[4,4,8,32,128]{4,3,2,1,0:T(8,128)(2,1)S(1)}, u32[]{:S(2)}, u32[]{:S(2)}) collective-permute-start(bf16[4,4,8,32,128]{4,3,2,1,0:T(8,128)(2,1)S(1)} %get-tuple-element.5), channel_id=1, source_target_pairs={{0,1},{1,0},{2,3},{3,2},{4,5},{5,4},{6,7},{7,6},{8,9},{9,8},{10,11... | collective-permute-start | bytes 3145736 | tf_op jit(solution)/shard_map/ppermute | solution.py:326

commit v4 on v3

--- a/solution.py
+++ b/solution.py
@@ -1,3 +1,5 @@
+import functools
+
 import jax
 import jax.numpy as jnp
 from jax import lax
@@ -26,8 +28,12 @@
         for c in range(NC)
         for x in range(NX)
         for y in range(NY)
-        for start in (4 * c, 4 * c + NZL)
+        for start in (4 - 4 * c, 4 - 4 * c + NZL)
     ]
+
+
+def shift(groups, by):
+    return [(group[i], group[(i + by) % 4]) for group in groups for i in range(4)]
 
 
 def lines(axis_of_core):
@@ -54,10 +60,6 @@
     return normal_cdf + value_in * density
 
 
-def tails_copy(pack_hbm, tails, sem):
-    return pltpu.make_async_copy(pack_hbm.at[:, pl.ds(NZL * BLK, TAIL), :], tails, sem)
-
-
 def read_places(tails, numbers, places, sem):
     row = lax.broadcasted_iota(jnp.int32, (TAIL, BLK), 0)
     table = jnp.zeros((TAIL, BLK), jnp.float32)
@@ -69,7 +71,7 @@
     move.wait()
 
 
-def choose_blocks(places, slot_of, rows, slots, offs, spare, unroll):
+def choose_blocks(packs, places, slot_of, rows, slots, offs, spare, unroll):
     def choose(pack, count):
         found = [places[pack, 2 * z + 1] for z in range(NZL)]
         found = [slot_of[col] for col in found]
@@ -81,7 +83,7 @@
             count = count + (found[z] != spare).astype(jnp.int32)
         return count
 
-    count = lax.fori_loop(0, places.shape[0], choose, 0, unroll=2)
+    count = lax.fori_loop(0, packs, choose, 0, unroll=2)
     for u in range(unroll):
         rows[count + u] = 0
         slots[count + u] = spare
@@ -134,7 +136,7 @@
     fetch = pltpu.make_async_copy(blocks.at[slot], block, sem)
     fetch.start()
     lane = lax.broadcasted_iota(jnp.int32, (TAIL, BLK), 1)
-    spot = 2 * ((lax.axis_index("zl") + 4 * lax.axis_index("c")) % NZL)
+    spot = 2 * ((lax.axis_index("zl") + 4 - 4 * lax.axis_index("c")) % NZL)
     tail = jnp.where(lane == spot, active[0, slot], 0)
     tail = jnp.where(lane == spot + 1, active[1, slot], tail)
     tail = tail.astype(jnp.float32).astype(jnp.bfloat16)
@@ -160,38 +162,54 @@
     )(drop, active, blocks)
 
 
-def first_kernel(
-    cand, tok_ref, own_hbm, acc,
-    weights, tails, numbers, places, slot_of, rows, slots, offs, sem,
-):
-    copy_own = pltpu.make_async_copy(own_hbm, weights, sem.at[0])
-    copy_tails = tails_copy(own_hbm, tails, sem.at[1])
-    copy_tails.start()
-    copy_own.start()
+def fetch_pieces(pieces, weights, tails, sem, tail_sem):
+    blocks, ends, at = [], [], 0
+    for i, piece in enumerate(pieces):
+        span = pl.ds(at, piece.shape[0])
+        ends.append(
+            pltpu.make_async_copy(
+                piece.at[:, pl.ds(NZL * BLK, TAIL), :], tails.at[span], tail_sem.at[i]
+            )
+        )
+        blocks.append(pltpu.make_async_copy(piece, weights.at[span], sem.at[i]))
+        at += piece.shape[0]
+    for copy in ends + blocks:
+        copy.start()
+
+    def wait(copies):
+        for copy in copies:
+            copy.wait()
+
+    return functools.partial(wait, ends), functools.partial(wait, blocks)
+
+
+def add_kernel(count, later, cand, tok_ref, *refs):
+    pieces, refs = refs[:count], refs[count:]
+    if later:
+        before, refs = refs[0], refs[1:]
+    (acc, weights, tails, numbers, places, slot_of, rows, slots, offs,
+     sem, tail_sem, move_sem) = refs
+    wait_tails, wait_blocks = fetch_pieces(pieces, weights, tails, sem, tail_sem)
     spare = acc.shape[0] - 1
     give_slots(cand, slot_of, spare)
 
-    copy_tails.wait()
-    read_places(tails, numbers, places, sem.at[1])
-
-    def zero(i, carry):
-        acc[i] = jnp.zeros(acc.shape[1:], jnp.float32)
-        return carry
-
-    lax.fori_loop(0, spare + 1, zero, 0, unroll=5)
-    count = choose_blocks(places, slot_of, rows, slots, offs, spare, MUL)
-    copy_own.wait()
-    add_products(count, tok_ref, weights, acc, rows, slots, offs, MUL)
+    def begin(i, carry):
+        acc[i] = before[i] if later else jnp.zeros(acc.shape[1:], jnp.float32)
+        return carry
+
+    lax.fori_loop(0, spare + 1, begin, 0, unroll=5)
+    wait_tails()
+    read_places(tails, numbers, places, move_sem)
+    found = choose_blocks(tails.shape[0], places, slot_of, rows, slots, offs, spare, MUL)
+    wait_blocks()
+    add_products(found, tok_ref, weights, acc, rows, slots, offs, MUL)
 
 
 def second_kernel(
-    cand, info, tok_ref, other_hbm, first, grad_ref, send_ref, keep_ref,
-    weights, acc, tails, numbers, places, slot_of, rows, slots, offs, sem,
+    cand, counts, tok_ref, one, two, first, grad_ref, send_ref, keep_ref,
+    weights, acc, tails, numbers, places, slot_of, rows, slots, offs, sem, tail_sem, move_sem,
 ):
-    copy_other = pltpu.make_async_copy(other_hbm, weights, sem.at[0])
-    copy_tails = tails_copy(other_hbm, tails, sem.at[1])
-    copy_tails.start()
-    copy_other.start()
+    wait_tails, wait_blocks = fetch_pieces([one, two], weights, tails, sem, tail_sem)
     spare = acc.shape[0] - 1
     tokens = tok_ref.shape[0]
     give_slots(cand, slot_of, spare)
@@ -201,17 +219,19 @@
         return carry
 
     lax.fori_loop(0, spare + 1, zero, 0, unroll=5)
-    copy_tails.wait()
-    read_places(tails, numbers, places, sem.at[1])
-    count = choose_blocks(places, slot_of, rows, slots, offs, spare, MUL)
-    copy_other.wait()
-    add_products(count, tok_ref, weights, acc, rows, slots, offs, MUL)
-    position = info[0] + lax.broadcasted_iota(jnp.int32, (tokens, BLK), 0)
-    usable = (position < info[1]).astype(jnp.float32)
+    wait_tails()
+    read_places(tails, numbers, places, move_sem)
+    found = choose_blocks(tails.shape[0], places, slot_of, rows, slots, offs, spare, MUL)
+    wait_blocks()
+    add_products(found, tok_ref, weights, acc, rows, slots, offs, MUL)
+    core_here = lax.axis_index("c")
+    index = (lax.axis_index("y") * NZL + lax.axis_index("zl")) * NC + core_here
+    position = index * tokens + lax.broadcasted_iota(jnp.int32, (tokens, BLK), 0)
+    usable = (position < counts[0]).astype(jnp.float32)
 
     def gradient(q, carry):
         y, z = q // NZL, q % NZL
-        for out_ref, core in ((send_ref, 1 - info[2]), (keep_ref, info[2])):
+        for out_ref, core in ((send_ref, 1 - core_here), (keep_ref, core_here)):
             j = q * NC + core
             col = cand[1, j]
             slot = slot_of[col]
@@ -249,21 +269,23 @@
 ANY = pl.BlockSpec(memory_space=pl.ANY)
 
 
-def first_half(tokens, own, cand, col_blocks):
-    packs, cands = own.shape[0], cand.shape[1]
-    rows_dev = tokens.shape[0]
+def add_pieces(tokens, pieces, cand, col_blocks, before=None):
+    packs, cands = sum(piece.shape[0] for piece in pieces), cand.shape[1]
+    rows_dev, count = tokens.shape[0], len(pieces)
+    later = before is not None
     return pl.pallas_call(
-        first_kernel,
+        functools.partial(add_kernel, count, later),
         out_shape=jax.ShapeDtypeStruct((cands + 1, rows_dev, BLK), jnp.float32),
         grid_spec=pltpu.PrefetchScalarGridSpec(
             num_scalar_prefetch=1,
             grid=(),
-            in_specs=[VMEM, ANY],
+            in_specs=[VMEM] + [ANY] * count + [VMEM] * later,
             out_specs=VMEM,
-            scratch_shapes=[pltpu.VMEM(own.shape, jnp.bfloat16)]
+            scratch_shapes=[pltpu.VMEM((packs, PIECE, BLK), jnp.bfloat16)]
             + place_scratch(packs)
             + lists(col_blocks, packs * NZL)
-            + [pltpu.SemaphoreType.DMA((2,))],
+            + [pltpu.SemaphoreType.DMA((count,))] * 2
+            + [pltpu.SemaphoreType.DMA],
         ),
         compiler_params=pltpu.CompilerParams(vmem_limit_bytes=LIMIT1 * 1024 * 1024),
         cost_estimate=pl.CostEstimate(
@@ -271,11 +293,11 @@
             bytes_accessed=10_000_000,
             transcendentals=0,
         ),
-    )(cand, tokens, own)
-
-
-def second_half(tokens, other, first, out_grad, cand, info):
-    packs, cands = other.shape[0], cand.shape[1]
+    )(cand, tokens, *pieces, *([before] if later else []))
+
+
+def second_half(tokens, pieces, first, out_grad, cand, counts):
+    packs, cands = sum(piece.shape[0] for piece in pieces), cand.shape[1]
     col_blocks = out_grad.shape[1] // BLK
     rows_dev = tokens.shape[0]
     part = jax.ShapeDtypeStruct((NX, NY, NZL, BLK // NX, BLK), jnp.bfloat16)
@@ -285,15 +307,15 @@
         grid_spec=pltpu.PrefetchScalarGridSpec(
             num_scalar_prefetch=2,
             grid=(),
-            in_specs=[VMEM, ANY, VMEM, VMEM],
+            in_specs=[VMEM, ANY, ANY, VMEM, VMEM],
             out_specs=(VMEM, VMEM),
             scratch_shapes=[
-                pltpu.VMEM(other.shape, jnp.bfloat16),
+                pltpu.VMEM((packs, PIECE, BLK), jnp.bfloat16),
                 pltpu.VMEM((cands + 1, rows_dev, BLK), jnp.float32),
             ]
             + place_scratch(packs)
             + lists(col_blocks, packs * NZL)
-            + [pltpu.SemaphoreType.DMA((2,))],
+            + [pltpu.SemaphoreType.DMA((2,))] * 2 + [pltpu.SemaphoreType.DMA],
         ),
         compiler_params=pltpu.CompilerParams(vmem_limit_bytes=LIMIT2 * 1024 * 1024),
         cost_estimate=pl.CostEstimate(
@@ -301,14 +323,13 @@
             bytes_accessed=15_000_000,
             transcendentals=2_000_000,
         ),
-    )(cand, info, tokens, other, first, out_grad)
+    )(cand, counts, tokens, *pieces, first, out_grad)
 
 
 def per_device(
     tokens, out_grad, block_values, active_blocks, drop_slots, cand_blocks, group_counts
 ):
     rows_dev = tokens.shape[0]
-    me = {name: lax.axis_index(name) for name in AXES}
     pieces = first_pieces(drop_slots, active_blocks.T, block_values)
     along_z = lax.all_to_all(
         pieces, AXES, 0, 0, axis_index_groups=runs_along_z(), tiled=True
@@ -316,13 +337,24 @@
     tail = jnp.sum(along_z[:, BLK:, :], axis=0)
     pack = jnp.concatenate([along_z[:, :BLK, :].reshape(NZL * BLK, BLK), tail], axis=0)
     line = to_all(pack, AXES, 4, lines("yx"))
-    plane = to_all(line.reshape(4 * PIECE, BLK), AXES, 4, lines("xy")).reshape(16, PIECE, BLK)
-    other = lax.ppermute(plane, "c", [(0, 1), (1, 0)])
     cand = cand_blocks.T
-    fsdp = (me["y"] * NZL + me["zl"]) * NC + me["c"]
-    info = jnp.stack([fsdp * rows_dev, group_counts[0], me["c"]]).astype(jnp.int32)
-    first = first_half(tokens, plane, cand, out_grad.shape[1] // BLK)
-    send, keep = second_half(tokens, other, first, out_grad, cand, info)
+    rings = lines("xy")
+    swap = [(i, i ^ 1) for i in range(NX * NZH * NY * NZL * NC)]
+
+    def swapped(value):
+        return lax.ppermute(value, AXES, swap)
+
+    cols = out_grad.shape[1] // BLK
+    one, two, three = (lax.ppermute(line, AXES, shift(rings, by)) for by in (2, 1, 3))
+    line_other = swapped(line)
+    acc = add_pieces(tokens, [line], cand, cols)
+    one, acc = lax.optimization_barrier((one, acc))
+    one_other = swapped(one)
+    acc = add_pieces(tokens, [one, line_other], cand, cols, acc)
+    two, three, acc = lax.optimization_barrier((two, three, acc))
+    two_other, three_other = swapped(two), swapped(three)
+    acc = add_pieces(tokens, [two, three, one_other], cand, cols, acc)
+    send, keep = second_half(tokens, [two_other, three_other], acc, out_grad, cand, group_counts)
     given = lax.ppermute(send, "c", [(0, 1), (1, 0)])
     mine = (keep.astype(jnp.float32) + given.astype(jnp.float32)).astype(jnp.bfloat16)
     mine = mine.reshape(NX * NY, NZL, BLK // NX, BLK)

time: 156 us -> 153 us (0.981)
  blocking collectives: 123 us -> 90.6 us
  starting transfers between devices: 3.83 us -> 28.1 us
  Pallas kernels: 14.3 us -> 19.4 us
    all_to_all x3 -> x2, blocking collectives: 54.1 us -> 21.8 us  [to_all(): lax.all_to_all(copies, axis, 0, 0, axis_index_groups=groups, tiled=True)]
    ppermute x1 -> x7, starting transfers between devices: 1.91 us -> 25.7 us  [the longest x4 13.7 us: swapped(): return lax.ppermute(value, AXES, swap)]
    pallas_call x1 -> x3, Pallas kernels: 4.95 us -> 11.2 us  [add_pieces(): pl.pallas_call(functools.partial(add_kernel, count, later), out_shape=jax...]
    all_to_all x1, blocking collectives: 29.1 us -> 25.3 us  [per_device(): lax.all_to_all(pieces, AXES, 0, 0, axis_index_groups=runs_along_z(), tile...]
    all_to_all x1, blocking collectives: 20.4 us -> 23.1 us  [per_device(): strips = lax.all_to_all(strips, ('zh', 'zl'), 0, 0, tiled=True)]
    ppermute x1 -> x7, waiting for transfers between devices: 1.86 us -> 3.44 us  [the longest x3 3.43 us: per_device(): lax.ppermute(line, AXES, shift(rings, by))]
  transfers between devices with their start and end apart: 2 -> 8, of which waited for: 2 -> 3; matrix products, arithmetic and copies ran while one was open for 0% -> 0% of each run, Pallas kernels for 3% -> 7%
where the time goes in v4:
time: 153 us; the launch traced here: 151 us
  blocking collectives  90.6 us (59%)
  starting transfers between devices  28.1 us (18%)
  Pallas kernels  19.4 us (13%)
  waiting for transfers between devices  5.7 us (4%)
  between operations  4 us (3%)
  local copies, waits for them, and re-layouts  1.79 us (1%)
  other arithmetic  1.74 us (1%)
    all_to_all x1, blocking collectives, per_device(): lax.all_to_all(pieces, AXES, 0, 0, axis_index_groups=runs_along_z(), tile...  25.3 us
    all_to_all x1, blocking collectives, per_device(): strips = lax.all_to_all(strips, ('zh', 'zl'), 0, 0, tiled=True)  23.1 us
    all_to_all x2, blocking collectives, to_all(): lax.all_to_all(copies, axis, 0, 0, axis_index_groups=groups, tiled=True)  21.8 us
    all_to_all x1, blocking collectives, per_device(): planes = lax.all_to_all(mine, ('x', 'y'), 0, 0, tiled=True)  20.4 us
    ppermute x4, starting transfers between devices, swapped(): return lax.ppermute(value, AXES, swap)  13.7 us
    ppermute x3, starting transfers between devices, per_device(): lax.ppermute(line, AXES, shift(rings, by))  12 us
    pallas_call x3, Pallas kernels, add_pieces(): pl.pallas_call(functools.partial(add_kernel, count, later), out_shape=jax...  11.2 us
    pallas_call x1, Pallas kernels, second_half(): pl.pallas_call(second_kernel, out_shape=(part, part), grid_spec=pltpu.Pre...  7.58 us
  transfers between devices with their start and end apart: 8, of which 3 were waited for; matrix products, arithmetic and copies ran while one was open for 0% of the time, Pallas kernels for 7%

profile of v4, /device:TPU:24, one launch (start us, length us, event | category | flops | bytes accessed | tf_op | source)
XLA Modules:
  0.0 151.3 jit_solution(15856549166353447462)
XLA Ops:
  1.3 0.9 copy-done.2
  2.2 0.7 copy-done.4
  2.9 0.7 shard_map.86
  3.5 25.3 %all_to_all.25 = bf16[8,144,128]{2,1,0:T(8,128)(2,1)S(1)} all-to-all(bf16[8,144,128]{2,1,0:T(8,128)(2,1)S(1)} %shard_map.86), channel_id=1, replica_groups={{8,10,12,14,64,66,68,70},{72,74,76,78,0,2,4,6},{24,26,28,30,80,82,84,86..., dimensions={0} | all-to-all | bytes 589824 | tf_op jit(solution)/shard_map/all_to_all | solution.py:334
  28.9 0.1 broadcast_in_dim.6
  29.0 0.0 copy-start
  29.0 0.0 copy-start.3
  29.1 13.5 %all_to_all.26.refs_0_ = bf16[4,1040,128]{2,1,0:T(8,128)(2,1)S(1)} all-to-all(bf16[4,1040,128]{2,1,0:T(8,128)(2,1)S(1)} %broadcast_in_dim.6), channel_id=1, replica_groups={{0,16,32,48},{128,144,160,176},{256,272,288,304},{384,400,416,432},{2,1..., dimensions={0} | all-to-all | bytes 2129920 | tf_op jit(solution)/shard_map/all_to_all | solution.py:54
  42.6 4.9 %collective-permute-start.2 = (bf16[4,1040,128]{2,1,0:T(8,128)(2,1)S(1)}, bf16[4,1040,128]{2,1,0:T(8,128)(2,1)S(1)}, u32[]{:S(2)}, u32[]{:S(2)}) collective-permute-start(bf16[4,1040,128]{2,1,0:T(8,128)(2,1)S(1)} %all_to_all.26.refs_0_), channel_id=1, source_target_pairs={{0,256},{128,384},{256,0},{384,128},{16,272},{144,400},{272,16},{4... | collective-permute-start | bytes 3194888 | tf_op jit(solution)/shard_map/ppermute | solution.py:348
  47.5 3.4 %collective-permute-start.3 = (bf16[4,1040,128]{2,1,0:T(8,128)(2,1)S(1)}, bf16[4,1040,128]{2,1,0:T(8,128)(2,1)S(1)}, u32[]{:S(2)}, u32[]{:S(2)}) collective-permute-start(bf16[4,1040,128]{2,1,0:T(8,128)(2,1)S(1)} %all_to_all.26.refs_0_), channel_id=1, source_target_pairs={{0,1},{1,0},{2,3},{3,2},{4,5},{5,4},{6,7},{7,6},{8,9},{9,8},{10,11... | collective-permute-start | bytes 3194888 | tf_op jit(solution)/shard_map/ppermute | solution.py:345
  50.9 2.5 %collective-permute-start = (bf16[4,1040,128]{2,1,0:T(8,128)(2,1)S(1)}, bf16[4,1040,128]{2,1,0:T(8,128)(2,1)S(1)}, u32[]{:S(2)}, u32[]{:S(2)}) collective-permute-start(bf16[4,1040,128]{2,1,0:T(8,128)(2,1)S(1)} %all_to_all.26.refs_0_), channel_id=1, source_target_pairs={{0,128},{128,256},{256,384},{384,0},{16,144},{144,272},{272,400},{... | collective-permute-start | bytes 3194888 | tf_op jit(solution)/shard_map/ppermute | solution.py:348
  53.4 4.6 %collective-permute-start.1 = (bf16[4,1040,128]{2,1,0:T(8,128)(2,1)S(1)}, bf16[4,1040,128]{2,1,0:T(8,128)(2,1)S(1)}, u32[]{:S(2)}, u32[]{:S(2)}) collective-permute-start(bf16[4,1040,128]{2,1,0:T(8,128)(2,1)S(1)} %all_to_all.26.refs_0_), channel_id=1, source_target_pairs={{0,384},{128,0},{256,128},{384,256},{16,400},{144,16},{272,144},{4... | collective-permute-start | bytes 3194888 | tf_op jit(solution)/shard_map/ppermute | solution.py:348
  58.0 3.1 %shard_map.87.refs_2_ = f32[65,128,128]{2,1,0:T(8,128)S(1)} custom-call(s32[2,64]{1,0:T(2,128)S(1)} %bitcast.7, bf16[128,3584]{1,0:T(8,128)(2,1)S(1)} %copy-done, bf16[4,1040,128]{2,1,0:T(8,128)(2,1)S(1)} %all_to_all.26.refs_0_), custom_call_target="tpu_custom_call" | custom-call | flops 134217728 | bytes 10000000 | tf_op jit(solution)/shard_map/pallas_call | solution.py:276
  61.1 0.0 collective-permute-done.2.refs_0_
  61.1 4.2 %collective-permute-start.6 = (bf16[4,1040,128]{2,1,0:T(8,128)(2,1)S(1)}, bf16[4,1040,128]{2,1,0:T(8,128)(2,1)S(1)}, u32[]{:S(2)}, u32[]{:S(2)}) collective-permute-start(bf16[4,1040,128]{2,1,0:T(8,128)(2,1)S(1)} %collective-permute-done.2.refs_0_), channel_id=1, source_target_pairs={{0,1},{1,0},{2,3},{3,2},{4,5},{5,4},{6,7},{7,6},{8,9},{9,8},{10,11... | collective-permute-start | bytes 3194888 | tf_op jit(solution)/shard_map/ppermute | solution.py:345
  65.3 0.0 collective-permute-done.3.refs_1_
  65.4 3.7 %shard_map.88.refs_3_ = f32[65,128,128]{2,1,0:T(8,128)S(1)} custom-call(s32[2,64]{1,0:T(2,128)S(1)} %bitcast.8, bf16[128,3584]{1,0:T(8,128)(2,1)S(1)} %copy-done, bf16[4,1040,128]{2,1,0:T(8,128)(2,1)S(1)} %collective-permute-done.2.refs_0_, bf16[4,1040,128]{2,1,0:T(8,128)(2,1)S(1)} %collective-permute-done.3.refs_1_, f32[65,128,128]{2,1,0:T(8,128)S(1)} %shard_map.87.refs_2_), custom_call_target="tpu_custom_call" | custom-call | flops 268435456 | bytes 10000000 | tf_op jit(solution)/shard_map/pallas_call | solution.py:276
  69.0 3.3 %collective-permute-done.refs_0_ = bf16[4,1040,128]{2,1,0:T(8,128)(2,1)S(1)} collective-permute-done((bf16[4,1040,128]{2,1,0:T(8,128)(2,1)S(1)}, bf16[4,1040,128]{2,1,0:T(8,128)(2,1)S(1)}, u32[]{:S(2)}, u32[]{:S(2)}) %collective-permute-start) | collective-permute-done | bytes 1064992 | tf_op jit(solution)/shard_map/ppermute | solution.py:348
  72.4 0.1 collective-permute-done.1.refs_1_
  72.4 4.2 %collective-permute-start.4 = (bf16[4,1040,128]{2,1,0:T(8,128)(2,1)S(1)}, bf16[4,1040,128]{2,1,0:T(8,128)(2,1)S(1)}, u32[]{:S(2)}, u32[]{:S(2)}) collective-permute-start(bf16[4,1040,128]{2,1,0:T(8,128)(2,1)S(1)} %collective-permute-done.refs_0_), channel_id=1, source_target_pairs={{0,1},{1,0},{2,3},{3,2},{4,5},{5,4},{6,7},{7,6},{8,9},{9,8},{10,11... | collective-permute-start | bytes 3194888 | tf_op jit(solution)/shard_map/ppermute | solution.py:345
  76.7 1.9 %collective-permute-start.5 = (bf16[4,1040,128]{2,1,0:T(8,128)(2,1)S(1)}, bf16[4,1040,128]{2,1,0:T(8,128)(2,1)S(1)}, u32[]{:S(2)}, u32[]{:S(2)}) collective-permute-start(bf16[4,1040,128]{2,1,0:T(8,128)(2,1)S(1)} %collective-permute-done.1.refs_1_), channel_id=1, source_target_pairs={{0,1},{1,0},{2,3},{3,2},{4,5},{5,4},{6,7},{7,6},{8,9},{9,8},{10,11... | collective-permute-start | bytes 3194888 | tf_op jit(solution)/shard_map/ppermute | solution.py:345
  79.2 0.0 copy-start.1
  79.3 4.4 %shard_map.89.first = f32[65,128,128]{2,1,0:T(8,128)S(1)} custom-call(s32[2,64]{1,0:T(2,128)S(1)} %bitcast.9, bf16[128,3584]{1,0:T(8,128)(2,1)S(1)} %copy-done, bf16[4,1040,128]{2,1,0:T(8,128)(2,1)S(1)} %collective-permute-done.refs_0_, bf16[4,1040,128]{2,1,0:T(8,128)(2,1)S(1)} %collective-permute-done.1.refs_1_, ...), custom_call_target="tpu_custom_call" | custom-call | flops 402653184 | bytes 10000000 | tf_op jit(solution)/shard_map/pallas_call | solution.py:276
  83.7 7.6 %shard_map.90 = (bf16[4,4,8,32,128]{4,3,2,1,0:T(8,128)(2,1)S(1)}, bf16[4,4,8,32,128]{4,3,2,1,0:T(8,128)(2,1)S(1)}) custom-call(s32[2,64]{1,0:T(2,128)S(1)} %bitcast.10, s32[1]{0:T(128)S(6)} %copy.10.counts, bf16[128,3584]{1,0:T(8,128)(2,1)S(1)} %copy-done, bf16[4,1040,128]{2,1,0:T(8,128)(2,1)S(1)} %collective-permute-done.4.one, ...), custom_call_target="tpu_custom_call" | custom-call | flops 536870912 | bytes 15000000 | tf_op jit(solution)/shard_map/pallas_call | solution.py:304
  91.3 2.4 %collective-permute-start.7 = (bf16[4,4,8,32,128]{4,3,2,1,0:T(8,128)(2,1)S(1)}, bf16[4,4,8,32,128]{4,3,2,1,0:T(8,128)(2,1)S(1)}, u32[]{:S(2)}, u32[]{:S(2)}) collective-permute-start(bf16[4,4,8,32,128]{4,3,2,1,0:T(8,128)(2,1)S(1)} %get-tuple-element.15), channel_id=1, source_target_pairs={{0,1},{1,0},{2,3},{3,2},{4,5},{5,4},{6,7},{7,6},{8,9},{9,8},{10,11... | collective-permute-start | bytes 3145736 | tf_op jit(solution)/shard_map/ppermute | solution.py:358
  93.7 2.3 %collective-permute-done.7 = bf16[4,4,8,32,128]{4,3,2,1,0:T(8,128)(2,1)S(1)} collective-permute-done((bf16[4,4,8,32,128]{4,3,2,1,0:T(8,128)(2,1)S(1)}, bf16[4,4,8,32,128]{4,3,2,1,0:T(8,128)(2,1)S(1)}, u32[]{:S(2)}, u32[]{:S(2)}) %collective-permute-start.7) | collective-permute-done | bytes 1048608 | tf_op jit(solution)/shard_map/ppermute | solution.py:358
  95.9 0.3 add_convert_fusion
  96.3 20.4 %all_to_all.27 = bf16[16,8,32,128]{3,2,1,0:T(8,128)(2,1)S(1)} all-to-all(bf16[16,8,32,128]{3,2,1,0:T(8,128)(2,1)S(1)} %bitcast.12), channel_id=1, replica_groups=mesh['x'=4,'zh'=2,'y'=4,'zl'=8,'c'=2] {'x','y'}, dimensions={0} | all-to-all | bytes 2097152 | tf_op jit(solution)/shard_map/all_to_all | solution.py:361
  116.6 0.1 reduce_sum.43
  116.8 23.1 %all_to_all.28 = bf16[16,32,128]{2,1,0:T(8,128)(2,1)S(1)} all-to-all(bf16[16,32,128]{2,1,0:T(8,128)(2,1)S(1)} %bitcast.14), channel_id=1, replica_groups=mesh['x'=4,'zh'=2,'y'=4,'zl'=8,'c'=2] {'zh','zl'}, dimensions={0} | all-to-all | bytes 262144 | tf_op jit(solution)/shard_map/all_to_all | solution.py:364
  140.0 8.3 %all_to_all.29 = f32[4,32,128]{2,1,0:T(8,128)S(1)} all-to-all(f32[4,32,128]{2,1,0:T(8,128)S(1)} %broadcast_in_dim.8), channel_id=1, replica_groups=mesh['x'=4,'zh'=2,'y'=4,'zl'=8,'c'=2] {'x'}, dimensions={0} | all-to-all | bytes 131072 | tf_op jit(solution)/shard_map/all_to_all | solution.py:54
  148.3 1.2 multiply_reduce_fusion
  (14 shorter events, 0.1 us)
Async XLA Ops:
  1.3 0.9 copy-start.2
  2.2 0.7 copy-start.4
  29.0 28.9 %copy-start = (bf16[128,3584]{1,0:T(8,128)(2,1)S(1)}, bf16[128,3584]{1,0:T(8,128)(2,1)}, u32[]{:S(2)}) copy-start(bf16[128,3584]{1,0:T(8,128)(2,1)} %tok_ref.7) | copy-start | bytes 2752516
  29.0 28.9 %copy-start.3 = (s32[64,2]{0,1:T(2,128)S(1)}, s32[64,2]{0,1:T(2,128)}, u32[]{:S(2)}) copy-start(s32[64,2]{0,1:T(2,128)} %param.12) | copy-start | bytes 1540
  42.6 18.5 %collective-permute-start.2 = (bf16[4,1040,128]{2,1,0:T(8,128)(2,1)S(1)}, bf16[4,1040,128]{2,1,0:T(8,128)(2,1)S(1)}, u32[]{:S(2)}, u32[]{:S(2)}) collective-permute-start(bf16[4,1040,128]{2,1,0:T(8,128)(2,1)S(1)} %all_to_all.26.refs_0_), channel_id=1, source_target_pairs={{0,256},{128,384},{256,0},{384,128},{16,272},{144,400},{272,16},{4... | collective-permute-start | bytes 3194888 | tf_op jit(solution)/shard_map/ppermute | solution.py:348
  47.5 17.8 %collective-permute-start.3 = (bf16[4,1040,128]{2,1,0:T(8,128)(2,1)S(1)}, bf16[4,1040,128]{2,1,0:T(8,128)(2,1)S(1)}, u32[]{:S(2)}, u32[]{:S(2)}) collective-permute-start(bf16[4,1040,128]{2,1,0:T(8,128)(2,1)S(1)} %all_to_all.26.refs_0_), channel_id=1, source_target_pairs={{0,1},{1,0},{2,3},{3,2},{4,5},{5,4},{6,7},{7,6},{8,9},{9,8},{10,11... | collective-permute-start | bytes 3194888 | tf_op jit(solution)/shard_map/ppermute | solution.py:345
  50.9 21.5 %collective-permute-start = (bf16[4,1040,128]{2,1,0:T(8,128)(2,1)S(1)}, bf16[4,1040,128]{2,1,0:T(8,128)(2,1)S(1)}, u32[]{:S(2)}, u32[]{:S(2)}) collective-permute-start(bf16[4,1040,128]{2,1,0:T(8,128)(2,1)S(1)} %all_to_all.26.refs_0_), channel_id=1, source_target_pairs={{0,128},{128,256},{256,384},{384,0},{16,144},{144,272},{272,400},{... | collective-permute-start | bytes 3194888 | tf_op jit(solution)/shard_map/ppermute | solution.py:348
  53.4 19.1 %collective-permute-start.1 = (bf16[4,1040,128]{2,1,0:T(8,128)(2,1)S(1)}, bf16[4,1040,128]{2,1,0:T(8,128)(2,1)S(1)}, u32[]{:S(2)}, u32[]{:S(2)}) collective-permute-start(bf16[4,1040,128]{2,1,0:T(8,128)(2,1)S(1)} %all_to_all.26.refs_0_), channel_id=1, source_target_pairs={{0,384},{128,0},{256,128},{384,256},{16,400},{144,16},{272,144},{4... | collective-permute-start | bytes 3194888 | tf_op jit(solution)/shard_map/ppermute | solution.py:348
  61.1 18.1 %collective-permute-start.6 = (bf16[4,1040,128]{2,1,0:T(8,128)(2,1)S(1)}, bf16[4,1040,128]{2,1,0:T(8,128)(2,1)S(1)}, u32[]{:S(2)}, u32[]{:S(2)}) collective-permute-start(bf16[4,1040,128]{2,1,0:T(8,128)(2,1)S(1)} %collective-permute-done.2.refs_0_), channel_id=1, source_target_pairs={{0,1},{1,0},{2,3},{3,2},{4,5},{5,4},{6,7},{7,6},{8,9},{9,8},{10,11... | collective-permute-start | bytes 3194888 | tf_op jit(solution)/shard_map/ppermute | solution.py:345
  72.4 11.2 %collective-permute-start.4 = (bf16[4,1040,128]{2,1,0:T(8,128)(2,1)S(1)}, bf16[4,1040,128]{2,1,0:T(8,128)(2,1)S(1)}, u32[]{:S(2)}, u32[]{:S(2)}) collective-permute-start(bf16[4,1040,128]{2,1,0:T(8,128)(2,1)S(1)} %collective-permute-done.refs_0_), channel_id=1, source_target_pairs={{0,1},{1,0},{2,3},{3,2},{4,5},{5,4},{6,7},{7,6},{8,9},{9,8},{10,11... | collective-permute-start | bytes 3194888 | tf_op jit(solution)/shard_map/ppermute | solution.py:345
  76.7 7.0 %collective-permute-start.5 = (bf16[4,1040,128]{2,1,0:T(8,128)(2,1)S(1)}, bf16[4,1040,128]{2,1,0:T(8,128)(2,1)S(1)}, u32[]{:S(2)}, u32[]{:S(2)}) collective-permute-start(bf16[4,1040,128]{2,1,0:T(8,128)(2,1)S(1)} %collective-permute-done.1.refs_1_), channel_id=1, source_target_pairs={{0,1},{1,0},{2,3},{3,2},{4,5},{5,4},{6,7},{7,6},{8,9},{9,8},{10,11... | collective-permute-start | bytes 3194888 | tf_op jit(solution)/shard_map/ppermute | solution.py:345
  79.2 4.4 %copy-start.1 = (bf16[128,14336]{1,0:T(8,128)(2,1)S(1)}, bf16[128,14336]{1,0:T(8,128)(2,1)}, u32[]{:S(2)}) copy-start(bf16[128,14336]{1,0:T(8,128)(2,1)} %grad_ref.1) | copy-start | bytes 11010052
  91.3 4.7 %collective-permute-start.7 = (bf16[4,4,8,32,128]{4,3,2,1,0:T(8,128)(2,1)S(1)}, bf16[4,4,8,32,128]{4,3,2,1,0:T(8,128)(2,1)S(1)}, u32[]{:S(2)}, u32[]{:S(2)}) collective-permute-start(bf16[4,4,8,32,128]{4,3,2,1,0:T(8,128)(2,1)S(1)} %get-tuple-element.15), channel_id=1, source_target_pairs={{0,1},{1,0},{2,3},{3,2},{4,5},{5,4},{6,7},{7,6},{8,9},{9,8},{10,11... | collective-permute-start | bytes 3145736 | tf_op jit(solution)/shard_map/ppermute | solution.py:358

commit v5 on v4

--- a/solution.py
+++ b/solution.py
@@ -186,8 +186,10 @@
 def add_kernel(count, later, cand, tok_ref, *refs):
     pieces, refs = refs[:count], refs[count:]
     if later:
-        before, refs = refs[0], refs[1:]
-    (acc, weights, tails, numbers, places, slot_of, rows, slots, offs,
+        (before, acc), refs = refs[:2], refs[2:]
+    else:
+        (acc, turned), refs = refs[:2], refs[2:]
+    (weights, tails, numbers, places, slot_of, rows, slots, offs,
      sem, tail_sem, move_sem) = refs
     wait_tails, wait_blocks = fetch_pieces(pieces, weights, tails, sem, tail_sem)
     spare = acc.shape[0] - 1
@@ -195,6 +197,54 @@
 
     def begin(i, carry):
         acc[i] = before[i] if later else jnp.zeros(acc.shape[1:], jnp.float32)
+        return carry
+
+    lax.fori_loop(0, spare + 1, begin, 0, unroll=5)
+    wait_tails()
+    read_places(tails, numbers, places, move_sem)
+    found = choose_blocks(tails.shape[0], places, slot_of, rows, slots, offs, spare, MUL)
+    if not later:
+        for r in range(turned.shape[0]):
+            turned[r] = tok_ref[:, r * BLK : (r + 1) * BLK].T
+    wait_blocks()
+    add_products(found, tok_ref, weights, acc, rows, slots, offs, MUL)
+
+
+def gradients(core, cand, counts, turned, slot_of, acc, grad_ref, out_ref):
+    tokens = acc.shape[1]
+    index = (lax.axis_index("y") * NZL + lax.axis_index("zl")) * NC + lax.axis_index("c")
+    position = index * tokens + lax.broadcasted_iota(jnp.int32, (tokens, BLK), 0)
+    usable = (position < counts[0]).astype(jnp.float32)
+
+    def gradient(q, carry):
+        y, z = q // NZL, q % NZL
+        j = q * NC + core
+        col = cand[1, j]
+        lanes = pl.ds(pl.multiple_of(col * BLK, BLK), BLK)
+        slope = gelu_slope(acc[slot_of[col]])
+        given = grad_ref[:, lanes].astype(jnp.float32)
+        part = jnp.dot(
+            turned[cand[0, j]],
+            (given * slope * usable).astype(jnp.bfloat16),
+            preferred_element_type=jnp.float32,
+        ).astype(jnp.bfloat16)
+        for x in range(NX):
+            out_ref[x, y, z] = part[x * 32 : (x + 1) * 32]
+        return carry
+
+    lax.fori_loop(0, cand.shape[1] // NC, gradient, 0, unroll=8)
+
+
+def second_kernel(
+    cand, counts, tok_ref, turned, one, two, before, grad_ref, acc, send_ref,
+    weights, tails, numbers, places, slot_of, rows, slots, offs, sem, tail_sem, move_sem,
+):
+    wait_tails, wait_blocks = fetch_pieces([one, two], weights, tails, sem, tail_sem)
+    spare = acc.shape[0] - 1
+    give_slots(cand, slot_of, spare)
+
+    def begin(i, carry):
+        acc[i] = before[i]
         return carry
 
     lax.fori_loop(0, spare + 1, begin, 0, unroll=5)
@@ -203,53 +253,14 @@
     found = choose_blocks(tails.shape[0], places, slot_of, rows, slots, offs, spare, MUL)
     wait_blocks()
     add_products(found, tok_ref, weights, acc, rows, slots, offs, MUL)
-
-
-def second_kernel(
-    cand, counts, tok_ref, one, two, first, grad_ref, send_ref, keep_ref,
-    weights, acc, tails, numbers, places, slot_of, rows, slots, offs, sem, tail_sem, move_sem,
-):
-    wait_tails, wait_blocks = fetch_pieces([one, two], weights, tails, sem, tail_sem)
-    spare = acc.shape[0] - 1
-    tokens = tok_ref.shape[0]
-    give_slots(cand, slot_of, spare)
-
-    def zero(i, carry):
-        acc[i] = jnp.zeros(acc.shape[1:], jnp.float32)
-        return carry
-
-    lax.fori_loop(0, spare + 1, zero, 0, unroll=5)
-    wait_tails()
-    read_places(tails, numbers, places, move_sem)
-    found = choose_blocks(tails.shape[0], places, slot_of, rows, slots, offs, spare, MUL)
-    wait_blocks()
-    add_products(found, tok_ref, weights, acc, rows, slots, offs, MUL)
-    core_here = lax.axis_index("c")
-    index = (lax.axis_index("y") * NZL + lax.axis_index("zl")) * NC + core_here
-    position = index * tokens + lax.broadcasted_iota(jnp.int32, (tokens, BLK), 0)
-    usable = (position < counts[0]).astype(jnp.float32)
-
-    def gradient(q, carry):
-        y, z = q // NZL, q % NZL
-        for out_ref, core in ((send_ref, 1 - core_here), (keep_ref, core_here)):
-            j = q * NC + core
-            col = cand[1, j]
-            slot = slot_of[col]
-            lanes = pl.ds(pl.multiple_of(col * BLK, BLK), BLK)
-            slope = gelu_slope(first[slot] + acc[slot])
-            given = grad_ref[:, lanes].astype(jnp.float32)
-            row = pl.multiple_of(cand[0, j] * BLK, BLK)
-            part = lax.dot_general(
-                tok_ref[:, pl.ds(row, BLK)],
-                (given * slope * usable).astype(jnp.bfloat16),
-                (((0,), (0,)), ((), ())),
-                preferred_element_type=jnp.float32,
-            ).astype(jnp.bfloat16)
-            for x in range(NX):
-                out_ref[x, y, z] = part[x * 32 : (x + 1) * 32]
-        return carry
-
-    lax.fori_loop(0, cand.shape[1] // NC, gradient, 0, unroll=4)
+    gradients(
+        1 - lax.axis_index("c"), cand, counts, turned, slot_of, acc, grad_ref, send_ref
+    )
+
+
+def third_kernel(cand, counts, turned, acc, grad_ref, keep_ref, slot_of):
+    give_slots(cand, slot_of, acc.shape[0] - 1)
+    gradients(lax.axis_index("c"), cand, counts, turned, slot_of, acc, grad_ref, keep_ref)
 
 
 def place_scratch(packs):
@@ -273,14 +284,16 @@
     packs, cands = sum(piece.shape[0] for piece in pieces), cand.shape[1]
     rows_dev, count = tokens.shape[0], len(pieces)
     later = before is not None
+    sums = jax.ShapeDtypeStruct((cands + 1, rows_dev, BLK), jnp.float32)
+    turned = jax.ShapeDtypeStruct((tokens.shape[1] // BLK, BLK, rows_dev), jnp.bfloat16)
     return pl.pallas_call(
         functools.partial(add_kernel, count, later),
-        out_shape=jax.ShapeDtypeStruct((cands + 1, rows_dev, BLK), jnp.float32),
+        out_shape=sums if later else (sums, turned),
         grid_spec=pltpu.PrefetchScalarGridSpec(
             num_scalar_prefetch=1,
             grid=(),
             in_specs=[VMEM] + [ANY] * count + [VMEM] * later,
-            out_specs=VMEM,
+            out_specs=VMEM if later else (VMEM, VMEM),
             scratch_shapes=[pltpu.VMEM((packs, PIECE, BLK), jnp.bfloat16)]
             + place_scratch(packs)
             + lists(col_blocks, packs * NZL)
@@ -296,34 +309,52 @@
     )(cand, tokens, *pieces, *([before] if later else []))
 
 
-def second_half(tokens, pieces, first, out_grad, cand, counts):
-    packs, cands = sum(piece.shape[0] for piece in pieces), cand.shape[1]
+PART = jax.ShapeDtypeStruct((NX, NY, NZL, BLK // NX, BLK), jnp.bfloat16)
+
+
+def second_half(tokens, turned, pieces, before, out_grad, cand, counts):
+    packs = sum(piece.shape[0] for piece in pieces)
     col_blocks = out_grad.shape[1] // BLK
     rows_dev = tokens.shape[0]
-    part = jax.ShapeDtypeStruct((NX, NY, NZL, BLK // NX, BLK), jnp.bfloat16)
     return pl.pallas_call(
         second_kernel,
-        out_shape=(part, part),
+        out_shape=(jax.ShapeDtypeStruct(before.shape, jnp.float32), PART),
         grid_spec=pltpu.PrefetchScalarGridSpec(
             num_scalar_prefetch=2,
             grid=(),
-            in_specs=[VMEM, ANY, ANY, VMEM, VMEM],
+            in_specs=[VMEM, VMEM, ANY, ANY, VMEM, VMEM],
             out_specs=(VMEM, VMEM),
-            scratch_shapes=[
-                pltpu.VMEM((packs, PIECE, BLK), jnp.bfloat16),
-                pltpu.VMEM((cands + 1, rows_dev, BLK), jnp.float32),
-            ]
+            scratch_shapes=[pltpu.VMEM((packs, PIECE, BLK), jnp.bfloat16)]
             + place_scratch(packs)
             + lists(col_blocks, packs * NZL)
-            + [pltpu.SemaphoreType.DMA((2,))] * 2 + [pltpu.SemaphoreType.DMA],
+            + [pltpu.SemaphoreType.DMA((2,))] * 2
+            + [pltpu.SemaphoreType.DMA],
         ),
         compiler_params=pltpu.CompilerParams(vmem_limit_bytes=LIMIT2 * 1024 * 1024),
         cost_estimate=pl.CostEstimate(
-            flops=2 * (packs * NZL + cands) * rows_dev * BLK * BLK,
+            flops=2 * (packs * NZL + 32) * rows_dev * BLK * BLK,
             bytes_accessed=15_000_000,
-            transcendentals=2_000_000,
-        ),
-    )(cand, counts, tokens, *pieces, first, out_grad)
+            transcendentals=1_000_000,
+        ),
+    )(cand, counts, tokens, turned, *pieces, before, out_grad)
+
+
+def third_part(turned, acc, out_grad, cand, counts):
+    return pl.pallas_call(
+        third_kernel,
+        out_shape=PART,
+        grid_spec=pltpu.PrefetchScalarGridSpec(
+            num_scalar_prefetch=2,
+            grid=(),
+            in_specs=[VMEM, VMEM, VMEM],
+            out_specs=VMEM,
+            scratch_shapes=[pltpu.SMEM((out_grad.shape[1] // BLK,), jnp.int32)],
+        ),
+        compiler_params=pltpu.CompilerParams(vmem_limit_bytes=LIMIT2 * 1024 * 1024),
+        cost_estimate=pl.CostEstimate(
+            flops=2 * 32 * BLK**3, bytes_accessed=8_000_000, transcendentals=1_000_000
+        ),
+    )(cand, counts, turned, acc, out_grad)
 
 
 def per_device(
@@ -347,18 +378,22 @@
     cols = out_grad.shape[1] // BLK
     one, two, three = (lax.ppermute(line, AXES, shift(rings, by)) for by in (2, 1, 3))
     line_other = swapped(line)
-    acc = add_pieces(tokens, [line], cand, cols)
+    acc, turned = add_pieces(tokens, [line], cand, cols)
     one, acc = lax.optimization_barrier((one, acc))
     one_other = swapped(one)
     acc = add_pieces(tokens, [one, line_other], cand, cols, acc)
     two, three, acc = lax.optimization_barrier((two, three, acc))
     two_other, three_other = swapped(two), swapped(three)
     acc = add_pieces(tokens, [two, three, one_other], cand, cols, acc)
-    send, keep = second_half(tokens, [two_other, three_other], acc, out_grad, cand, group_counts)
+    acc, send = second_half(
+        tokens, turned, [two_other, three_other], acc, out_grad, cand, group_counts
+    )
     given = lax.ppermute(send, "c", [(0, 1), (1, 0)])
+    keep = third_part(turned, acc, out_grad, cand, group_counts)
     mine = (keep.astype(jnp.float32) + given.astype(jnp.float32)).astype(jnp.bfloat16)
-    mine = mine.reshape(NX * NY, NZL, BLK // NX, BLK)
+    mine = mine.reshape(NX * NY, NZL * (BLK // NX), BLK)
     planes = lax.all_to_all(mine, ("x", "y"), 0, 0, tiled=True)
+    planes = planes.reshape(NX * NY, NZL, BLK // NX, BLK)
     strip = jnp.sum(planes.astype(jnp.float32), axis=0).astype(jnp.bfloat16)
     strips = jnp.broadcast_to(strip[None], (NZH,) + strip.shape).reshape(NZH * NZL, BLK // NX, BLK)
     strips = lax.all_to_all(strips, ("zh", "zl"), 0, 0, tiled=True)

time: 153 us -> 151 us (0.987)
  waiting for transfers between devices: 5.7 us -> 3.44 us
    ppermute x1, waiting for transfers between devices: 2.26 us -> 0.01 us  [per_device(): given = lax.ppermute(send, 'c', [(0, 1), (1, 0)])]
    pallas_call x4 -> x5, Pallas kernels: 18.8 us -> 19.5 us  [the longest x3 11.2 us: add_pieces(): pl.pallas_call(functools.partial(add_kernel, count, later), out_shape=sum...]
  transfers between devices with their start and end apart: 8 -> 8, of which waited for: 3 -> 2; matrix products, arithmetic and copies ran while one was open for 0% -> 0% of each run, Pallas kernels for 7% -> 9%
where the time goes in v5:
time: 151 us; the launch traced here: 150 us
  blocking collectives  90.7 us (60%)
  starting transfers between devices  27.8 us (18%)
  Pallas kernels  20.2 us (13%)
  between operations  4.02 us (3%)
  waiting for transfers between devices  3.44 us (2%)
  local copies, waits for them, and re-layouts  1.79 us (1%)
  other arithmetic  1.73 us (1%)
    all_to_all x1, blocking collectives, per_device(): lax.all_to_all(pieces, AXES, 0, 0, axis_index_groups=runs_along_z(), tile...  25.3 us
    all_to_all x1, blocking collectives, per_device(): strips = lax.all_to_all(strips, ('zh', 'zl'), 0, 0, tiled=True)  23.7 us
    all_to_all x2, blocking collectives, to_all(): lax.all_to_all(copies, axis, 0, 0, axis_index_groups=groups, tiled=True)  21.7 us
    all_to_all x1, blocking collectives, per_device(): planes = lax.all_to_all(mine, ('x', 'y'), 0, 0, tiled=True)  20.1 us
    ppermute x4, starting transfers between devices, swapped(): return lax.ppermute(value, AXES, swap)  13.7 us
    ppermute x3, starting transfers between devices, per_device(): lax.ppermute(line, AXES, shift(rings, by))  12 us
    pallas_call x3, Pallas kernels, add_pieces(): pl.pallas_call(functools.partial(add_kernel, count, later), out_shape=sum...  11.2 us
    pallas_call x1, Pallas kernels, second_half(): pl.pallas_call(second_kernel, out_shape=(jax.ShapeDtypeStruct(before.shap...  5.4 us
  transfers between devices with their start and end apart: 8, of which 2 were waited for; matrix products, arithmetic and copies ran while one was open for 0% of the time, Pallas kernels for 9%

profile of v5, /device:TPU:24, one launch (start us, length us, event | category | flops | bytes accessed | tf_op | source)
XLA Modules:
  0.0 149.7 jit_solution(15081355701238985168)
XLA Ops:
  1.3 0.9 copy-done.2
  2.2 0.7 copy-done.4
  2.9 0.7 shard_map.86
  3.5 25.3 %all_to_all.25 = bf16[8,144,128]{2,1,0:T(8,128)(2,1)S(1)} all-to-all(bf16[8,144,128]{2,1,0:T(8,128)(2,1)S(1)} %shard_map.86), channel_id=1, replica_groups={{8,10,12,14,64,66,68,70},{72,74,76,78,0,2,4,6},{24,26,28,30,80,82,84,86..., dimensions={0} | all-to-all | bytes 589824 | tf_op jit(solution)/shard_map/all_to_all | solution.py:365
  28.9 0.1 broadcast_in_dim.8
  29.0 0.0 copy-start
  29.0 0.0 copy-start.3
  29.1 13.5 %all_to_all.26.refs_0_ = bf16[4,1040,128]{2,1,0:T(8,128)(2,1)S(1)} all-to-all(bf16[4,1040,128]{2,1,0:T(8,128)(2,1)S(1)} %broadcast_in_dim.8), channel_id=1, replica_groups={{0,16,32,48},{128,144,160,176},{256,272,288,304},{384,400,416,432},{2,1..., dimensions={0} | all-to-all | bytes 2129920 | tf_op jit(solution)/shard_map/all_to_all | solution.py:54
  42.6 4.9 %collective-permute-start.2 = (bf16[4,1040,128]{2,1,0:T(8,128)(2,1)S(1)}, bf16[4,1040,128]{2,1,0:T(8,128)(2,1)S(1)}, u32[]{:S(2)}, u32[]{:S(2)}) collective-permute-start(bf16[4,1040,128]{2,1,0:T(8,128)(2,1)S(1)} %all_to_all.26.refs_0_), channel_id=1, source_target_pairs={{0,256},{128,384},{256,0},{384,128},{16,272},{144,400},{272,16},{4... | collective-permute-start | bytes 3194888 | tf_op jit(solution)/shard_map/ppermute | solution.py:379
  47.5 3.4 %collective-permute-start.3 = (bf16[4,1040,128]{2,1,0:T(8,128)(2,1)S(1)}, bf16[4,1040,128]{2,1,0:T(8,128)(2,1)S(1)}, u32[]{:S(2)}, u32[]{:S(2)}) collective-permute-start(bf16[4,1040,128]{2,1,0:T(8,128)(2,1)S(1)} %all_to_all.26.refs_0_), channel_id=1, source_target_pairs={{0,1},{1,0},{2,3},{3,2},{4,5},{5,4},{6,7},{7,6},{8,9},{9,8},{10,11... | collective-permute-start | bytes 3194888 | tf_op jit(solution)/shard_map/ppermute | solution.py:376
  50.9 2.5 %collective-permute-start = (bf16[4,1040,128]{2,1,0:T(8,128)(2,1)S(1)}, bf16[4,1040,128]{2,1,0:T(8,128)(2,1)S(1)}, u32[]{:S(2)}, u32[]{:S(2)}) collective-permute-start(bf16[4,1040,128]{2,1,0:T(8,128)(2,1)S(1)} %all_to_all.26.refs_0_), channel_id=1, source_target_pairs={{0,128},{128,256},{256,384},{384,0},{16,144},{144,272},{272,400},{... | collective-permute-start | bytes 3194888 | tf_op jit(solution)/shard_map/ppermute | solution.py:379
  53.4 4.6 %collective-permute-start.1 = (bf16[4,1040,128]{2,1,0:T(8,128)(2,1)S(1)}, bf16[4,1040,128]{2,1,0:T(8,128)(2,1)S(1)}, u32[]{:S(2)}, u32[]{:S(2)}) collective-permute-start(bf16[4,1040,128]{2,1,0:T(8,128)(2,1)S(1)} %all_to_all.26.refs_0_), channel_id=1, source_target_pairs={{0,384},{128,0},{256,128},{384,256},{16,400},{144,16},{272,144},{4... | collective-permute-start | bytes 3194888 | tf_op jit(solution)/shard_map/ppermute | solution.py:379
  58.0 3.2 %shard_map.87 = (f32[65,128,128]{2,1,0:T(8,128)S(1)}, bf16[28,128,128]{2,1,0:T(8,128)(2,1)S(1)}) custom-call(s32[2,64]{1,0:T(2,128)S(1)} %bitcast.8, bf16[128,3584]{1,0:T(8,128)(2,1)S(1)} %copy-done, bf16[4,1040,128]{2,1,0:T(8,128)(2,1)S(1)} %all_to_all.26.refs_0_), custom_call_target="tpu_custom_call" | custom-call | flops 134217728 | bytes 10000000 | tf_op jit(solution)/shard_map/pallas_call | solution.py:289
  61.2 0.0 collective-permute-done.2.refs_0_
  61.2 4.2 %collective-permute-start.6 = (bf16[4,1040,128]{2,1,0:T(8,128)(2,1)S(1)}, bf16[4,1040,128]{2,1,0:T(8,128)(2,1)S(1)}, u32[]{:S(2)}, u32[]{:S(2)}) collective-permute-start(bf16[4,1040,128]{2,1,0:T(8,128)(2,1)S(1)} %collective-permute-done.2.refs_0_), channel_id=1, source_target_pairs={{0,1},{1,0},{2,3},{3,2},{4,5},{5,4},{6,7},{7,6},{8,9},{9,8},{10,11... | collective-permute-start | bytes 3194888 | tf_op jit(solution)/shard_map/ppermute | solution.py:376
  65.3 0.0 collective-permute-done.3.refs_1_
  65.4 3.7 %shard_map.88.refs_3_ = f32[65,128,128]{2,1,0:T(8,128)S(1)} custom-call(s32[2,64]{1,0:T(2,128)S(1)} %bitcast.9, bf16[128,3584]{1,0:T(8,128)(2,1)S(1)} %copy-done, bf16[4,1040,128]{2,1,0:T(8,128)(2,1)S(1)} %collective-permute-done.2.refs_0_, bf16[4,1040,128]{2,1,0:T(8,128)(2,1)S(1)} %collective-permute-done.3.refs_1_, ...), custom_call_target="tpu_custom_call" | custom-call | flops 268435456 | bytes 10000000 | tf_op jit(solution)/shard_map/pallas_call | solution.py:289
  69.0 3.3 %collective-permute-done.refs_0_ = bf16[4,1040,128]{2,1,0:T(8,128)(2,1)S(1)} collective-permute-done((bf16[4,1040,128]{2,1,0:T(8,128)(2,1)S(1)}, bf16[4,1040,128]{2,1,0:T(8,128)(2,1)S(1)}, u32[]{:S(2)}, u32[]{:S(2)}) %collective-permute-start) | collective-permute-done | bytes 1064992 | tf_op jit(solution)/shard_map/ppermute | solution.py:379
  72.4 0.1 collective-permute-done.1.refs_1_
  72.4 4.2 %collective-permute-start.4 = (bf16[4,1040,128]{2,1,0:T(8,128)(2,1)S(1)}, bf16[4,1040,128]{2,1,0:T(8,128)(2,1)S(1)}, u32[]{:S(2)}, u32[]{:S(2)}) collective-permute-start(bf16[4,1040,128]{2,1,0:T(8,128)(2,1)S(1)} %collective-permute-done.refs_0_), channel_id=1, source_target_pairs={{0,1},{1,0},{2,3},{3,2},{4,5},{5,4},{6,7},{7,6},{8,9},{9,8},{10,11... | collective-permute-start | bytes 3194888 | tf_op jit(solution)/shard_map/ppermute | solution.py:376
  76.7 1.9 %collective-permute-start.5 = (bf16[4,1040,128]{2,1,0:T(8,128)(2,1)S(1)}, bf16[4,1040,128]{2,1,0:T(8,128)(2,1)S(1)}, u32[]{:S(2)}, u32[]{:S(2)}) collective-permute-start(bf16[4,1040,128]{2,1,0:T(8,128)(2,1)S(1)} %collective-permute-done.1.refs_1_), channel_id=1, source_target_pairs={{0,1},{1,0},{2,3},{3,2},{4,5},{5,4},{6,7},{7,6},{8,9},{9,8},{10,11... | collective-permute-start | bytes 3194888 | tf_op jit(solution)/shard_map/ppermute | solution.py:376
  79.2 0.0 copy-start.1
  79.3 4.4 %shard_map.89.before = f32[65,128,128]{2,1,0:T(8,128)S(1)} custom-call(s32[2,64]{1,0:T(2,128)S(1)} %bitcast.10, bf16[128,3584]{1,0:T(8,128)(2,1)S(1)} %copy-done, bf16[4,1040,128]{2,1,0:T(8,128)(2,1)S(1)} %collective-permute-done.refs_0_, bf16[4,1040,128]{2,1,0:T(8,128)(2,1)S(1)} %collective-permute-done.1.refs_1_, ...), custom_call_target="tpu_custom_call" | custom-call | flops 402653184 | bytes 10000000 | tf_op jit(solution)/shard_map/pallas_call | solution.py:289
  83.7 5.4 %shard_map.90 = (f32[65,128,128]{2,1,0:T(8,128)S(1)}, bf16[4,4,8,32,128]{4,3,2,1,0:T(8,128)(2,1)S(1)}) custom-call(s32[2,64]{1,0:T(2,128)S(1)} %bitcast.11, s32[1]{0:T(128)S(6)} %copy.10.counts, bf16[128,3584]{1,0:T(8,128)(2,1)S(1)} %copy-done, bf16[28,128,128]{2,1,0:T(8,128)(2,1)S(1)} %get-tuple-element.11.turned, ...), custom_call_target="tpu_custom_call" | custom-call | flops 402653184 | bytes 15000000 | tf_op jit(solution)/shard_map/pallas_call | solution.py:319
  89.1 2.2 %collective-permute-start.7 = (bf16[4,4,8,32,128]{4,3,2,1,0:T(8,128)(2,1)S(1)}, bf16[4,4,8,32,128]{4,3,2,1,0:T(8,128)(2,1)S(1)}, u32[]{:S(2)}, u32[]{:S(2)}) collective-permute-start(bf16[4,4,8,32,128]{4,3,2,1,0:T(8,128)(2,1)S(1)} %get-tuple-element.19), channel_id=1, source_target_pairs={{0,1},{1,0},{2,3},{3,2},{4,5},{5,4},{6,7},{7,6},{8,9},{9,8},{10,11... | collective-permute-start | bytes 3145736 | tf_op jit(solution)/shard_map/ppermute | solution.py:391
  91.3 2.9 %shard_map.91 = bf16[4,4,8,32,128]{4,3,2,1,0:T(8,128)(2,1)S(1)} custom-call(s32[2,64]{1,0:T(2,128)S(1)} %bitcast.12, s32[1]{0:T(128)S(6)} %copy.10.counts, bf16[28,128,128]{2,1,0:T(8,128)(2,1)S(1)} %get-tuple-element.11.turned, f32[65,128,128]{2,1,0:T(8,128)S(1)} %get-tuple-element.18.acc, bf16[128,14336]{1,0:T(8,128)(2,1)S(1)} %copy-done.1), custom_call_target="tpu_custom_call" | custom-call | flops 134217728 | bytes 8000000 | tf_op jit(solution)/shard_map/pallas_call | solution.py:343
  94.2 0.3 add_convert_fusion
  94.5 20.1 %all_to_all.27 = bf16[16,256,128]{2,1,0:T(8,128)(2,1)S(1)} all-to-all(bf16[16,256,128]{2,1,0:T(8,128)(2,1)S(1)} %bitcast.14), channel_id=1, replica_groups=mesh['x'=4,'zh'=2,'y'=4,'zl'=8,'c'=2] {'x','y'}, dimensions={0} | all-to-all | bytes 2097152 | tf_op jit(solution)/shard_map/all_to_all | solution.py:395
  114.5 0.1 reduce_sum.43
  114.7 23.7 %all_to_all.28 = bf16[16,32,128]{2,1,0:T(8,128)(2,1)S(1)} all-to-all(bf16[16,32,128]{2,1,0:T(8,128)(2,1)S(1)} %bitcast.16), channel_id=1, replica_groups=mesh['x'=4,'zh'=2,'y'=4,'zl'=8,'c'=2] {'zh','zl'}, dimensions={0} | all-to-all | bytes 262144 | tf_op jit(solution)/shard_map/all_to_all | solution.py:399
  138.5 8.1 %all_to_all.29 = f32[4,32,128]{2,1,0:T(8,128)S(1)} all-to-all(f32[4,32,128]{2,1,0:T(8,128)S(1)} %broadcast_in_dim.11), channel_id=1, replica_groups=mesh['x'=4,'zh'=2,'y'=4,'zl'=8,'c'=2] {'x'}, dimensions={0} | all-to-all | bytes 131072 | tf_op jit(solution)/shard_map/all_to_all | solution.py:54
  146.6 1.2 multiply_reduce_fusion
  (15 shorter events, 0.1 us)
Async XLA Ops:
  1.3 0.9 copy-start.2
  2.2 0.7 copy-start.4
  29.0 28.9 %copy-start = (bf16[128,3584]{1,0:T(8,128)(2,1)S(1)}, bf16[128,3584]{1,0:T(8,128)(2,1)}, u32[]{:S(2)}) copy-start(bf16[128,3584]{1,0:T(8,128)(2,1)} %tok_ref.7) | copy-start | bytes 2752516
  29.0 28.9 %copy-start.3 = (s32[64,2]{0,1:T(2,128)S(1)}, s32[64,2]{0,1:T(2,128)}, u32[]{:S(2)}) copy-start(s32[64,2]{0,1:T(2,128)} %param.12) | copy-start | bytes 1540
  42.6 18.6 %collective-permute-start.2 = (bf16[4,1040,128]{2,1,0:T(8,128)(2,1)S(1)}, bf16[4,1040,128]{2,1,0:T(8,128)(2,1)S(1)}, u32[]{:S(2)}, u32[]{:S(2)}) collective-permute-start(bf16[4,1040,128]{2,1,0:T(8,128)(2,1)S(1)} %all_to_all.26.refs_0_), channel_id=1, source_target_pairs={{0,256},{128,384},{256,0},{384,128},{16,272},{144,400},{272,16},{4... | collective-permute-start | bytes 3194888 | tf_op jit(solution)/shard_map/ppermute | solution.py:379
  47.5 17.8 %collective-permute-start.3 = (bf16[4,1040,128]{2,1,0:T(8,128)(2,1)S(1)}, bf16[4,1040,128]{2,1,0:T(8,128)(2,1)S(1)}, u32[]{:S(2)}, u32[]{:S(2)}) collective-permute-start(bf16[4,1040,128]{2,1,0:T(8,128)(2,1)S(1)} %all_to_all.26.refs_0_), channel_id=1, source_target_pairs={{0,1},{1,0},{2,3},{3,2},{4,5},{5,4},{6,7},{7,6},{8,9},{9,8},{10,11... | collective-permute-start | bytes 3194888 | tf_op jit(solution)/shard_map/ppermute | solution.py:376
  50.9 21.5 %collective-permute-start = (bf16[4,1040,128]{2,1,0:T(8,128)(2,1)S(1)}, bf16[4,1040,128]{2,1,0:T(8,128)(2,1)S(1)}, u32[]{:S(2)}, u32[]{:S(2)}) collective-permute-start(bf16[4,1040,128]{2,1,0:T(8,128)(2,1)S(1)} %all_to_all.26.refs_0_), channel_id=1, source_target_pairs={{0,128},{128,256},{256,384},{384,0},{16,144},{144,272},{272,400},{... | collective-permute-start | bytes 3194888 | tf_op jit(solution)/shard_map/ppermute | solution.py:379
  53.4 19.1 %collective-permute-start.1 = (bf16[4,1040,128]{2,1,0:T(8,128)(2,1)S(1)}, bf16[4,1040,128]{2,1,0:T(8,128)(2,1)S(1)}, u32[]{:S(2)}, u32[]{:S(2)}) collective-permute-start(bf16[4,1040,128]{2,1,0:T(8,128)(2,1)S(1)} %all_to_all.26.refs_0_), channel_id=1, source_target_pairs={{0,384},{128,0},{256,128},{384,256},{16,400},{144,16},{272,144},{4... | collective-permute-start | bytes 3194888 | tf_op jit(solution)/shard_map/ppermute | solution.py:379
  61.2 18.1 %collective-permute-start.6 = (bf16[4,1040,128]{2,1,0:T(8,128)(2,1)S(1)}, bf16[4,1040,128]{2,1,0:T(8,128)(2,1)S(1)}, u32[]{:S(2)}, u32[]{:S(2)}) collective-permute-start(bf16[4,1040,128]{2,1,0:T(8,128)(2,1)S(1)} %collective-permute-done.2.refs_0_), channel_id=1, source_target_pairs={{0,1},{1,0},{2,3},{3,2},{4,5},{5,4},{6,7},{7,6},{8,9},{9,8},{10,11... | collective-permute-start | bytes 3194888 | tf_op jit(solution)/shard_map/ppermute | solution.py:376
  72.4 11.2 %collective-permute-start.4 = (bf16[4,1040,128]{2,1,0:T(8,128)(2,1)S(1)}, bf16[4,1040,128]{2,1,0:T(8,128)(2,1)S(1)}, u32[]{:S(2)}, u32[]{:S(2)}) collective-permute-start(bf16[4,1040,128]{2,1,0:T(8,128)(2,1)S(1)} %collective-permute-done.refs_0_), channel_id=1, source_target_pairs={{0,1},{1,0},{2,3},{3,2},{4,5},{5,4},{6,7},{7,6},{8,9},{9,8},{10,11... | collective-permute-start | bytes 3194888 | tf_op jit(solution)/shard_map/ppermute | solution.py:376
  76.7 7.0 %collective-permute-start.5 = (bf16[4,1040,128]{2,1,0:T(8,128)(2,1)S(1)}, bf16[4,1040,128]{2,1,0:T(8,128)(2,1)S(1)}, u32[]{:S(2)}, u32[]{:S(2)}) collective-permute-start(bf16[4,1040,128]{2,1,0:T(8,128)(2,1)S(1)} %collective-permute-done.1.refs_1_), channel_id=1, source_target_pairs={{0,1},{1,0},{2,3},{3,2},{4,5},{5,4},{6,7},{7,6},{8,9},{9,8},{10,11... | collective-permute-start | bytes 3194888 | tf_op jit(solution)/shard_map/ppermute | solution.py:376
  79.2 4.4 %copy-start.1 = (bf16[128,14336]{1,0:T(8,128)(2,1)S(1)}, bf16[128,14336]{1,0:T(8,128)(2,1)}, u32[]{:S(2)}) copy-start(bf16[128,14336]{1,0:T(8,128)(2,1)} %grad_ref.3) | copy-start | bytes 11010052
  89.1 5.1 %collective-permute-start.7 = (bf16[4,4,8,32,128]{4,3,2,1,0:T(8,128)(2,1)S(1)}, bf16[4,4,8,32,128]{4,3,2,1,0:T(8,128)(2,1)S(1)}, u32[]{:S(2)}, u32[]{:S(2)}) collective-permute-start(bf16[4,4,8,32,128]{4,3,2,1,0:T(8,128)(2,1)S(1)} %get-tuple-element.19), channel_id=1, source_target_pairs={{0,1},{1,0},{2,3},{3,2},{4,5},{5,4},{6,7},{7,6},{8,9},{9,8},{10,11... | collective-permute-start | bytes 3145736 | tf_op jit(solution)/shard_map/ppermute | solution.py:391

commit v6 on v5

--- a/solution.py
+++ b/solution.py
@@ -13,7 +13,7 @@
 BLK = 128
 TAIL = 16
 PIECE = NZL * BLK + TAIL
-MUL = 8
+MUL = 16
 LIMIT1 = 20
 LIMIT2 = 24
 
@@ -62,10 +62,11 @@
 
 def read_places(tails, numbers, places, sem):
     row = lax.broadcasted_iota(jnp.int32, (TAIL, BLK), 0)
-    table = jnp.zeros((TAIL, BLK), jnp.float32)
-    for p in range(tails.shape[0]):
-        table = jnp.where(row == p, tails[p].astype(jnp.float32), table)
-    numbers[...] = table.astype(jnp.int32)
+    for start in range(0, tails.shape[0], TAIL):
+        table = jnp.zeros((TAIL, BLK), jnp.float32)
+        for p in range(start, min(start + TAIL, tails.shape[0])):
+            table = jnp.where(row == p - start, tails[p].astype(jnp.float32), table)
+        numbers[pl.ds(start, TAIL), :] = table.astype(jnp.int32)
     move = pltpu.make_async_copy(numbers, places, sem)
     move.start()
     move.wait()
@@ -232,14 +233,14 @@
             out_ref[x, y, z] = part[x * 32 : (x + 1) * 32]
         return carry
 
-    lax.fori_loop(0, cand.shape[1] // NC, gradient, 0, unroll=8)
+    lax.fori_loop(0, cand.shape[1] // NC, gradient, 0, unroll=16)
 
 
 def second_kernel(
-    cand, counts, tok_ref, turned, one, two, before, grad_ref, acc, send_ref,
+    cand, counts, tok_ref, turned, one, two, three, four, before, grad_ref, acc, send_ref,
     weights, tails, numbers, places, slot_of, rows, slots, offs, sem, tail_sem, move_sem,
 ):
-    wait_tails, wait_blocks = fetch_pieces([one, two], weights, tails, sem, tail_sem)
+    wait_tails, wait_blocks = fetch_pieces([one, two, three, four], weights, tails, sem, tail_sem)
     spare = acc.shape[0] - 1
     give_slots(cand, slot_of, spare)
 
@@ -266,8 +267,8 @@
 def place_scratch(packs):
     return [
         pltpu.VMEM((packs, TAIL, BLK), jnp.bfloat16),
-        pltpu.VMEM((TAIL, BLK), jnp.int32),
-        pltpu.SMEM((TAIL, BLK), jnp.int32),
+        pltpu.VMEM((pl.cdiv(packs, TAIL) * TAIL, BLK), jnp.int32),
+        pltpu.SMEM((pl.cdiv(packs, TAIL) * TAIL, BLK), jnp.int32),
     ]
 
 
@@ -322,12 +323,12 @@
         grid_spec=pltpu.PrefetchScalarGridSpec(
             num_scalar_prefetch=2,
             grid=(),
-            in_specs=[VMEM, VMEM, ANY, ANY, VMEM, VMEM],
+            in_specs=[VMEM, VMEM] + [ANY] * len(pieces) + [VMEM, VMEM],
             out_specs=(VMEM, VMEM),
             scratch_shapes=[pltpu.VMEM((packs, PIECE, BLK), jnp.bfloat16)]
             + place_scratch(packs)
             + lists(col_blocks, packs * NZL)
-            + [pltpu.SemaphoreType.DMA((2,))] * 2
+            + [pltpu.SemaphoreType.DMA((len(pieces),))] * 2
             + [pltpu.SemaphoreType.DMA],
         ),
         compiler_params=pltpu.CompilerParams(vmem_limit_bytes=LIMIT2 * 1024 * 1024),
@@ -382,11 +383,16 @@
     one, acc = lax.optimization_barrier((one, acc))
     one_other = swapped(one)
     acc = add_pieces(tokens, [one, line_other], cand, cols, acc)
-    two, three, acc = lax.optimization_barrier((two, three, acc))
-    two_other, three_other = swapped(two), swapped(three)
-    acc = add_pieces(tokens, [two, three, one_other], cand, cols, acc)
+    two, three, one_other, acc = lax.optimization_barrier((two, three, one_other, acc))
+    both_other = swapped(jnp.concatenate([two, three], axis=0))
     acc, send = second_half(
-        tokens, turned, [two_other, three_other], acc, out_grad, cand, group_counts
+        tokens,
+        turned,
+        [two, three, one_other, both_other],
+        acc,
+        out_grad,
+        cand,
+        group_counts,
     )
     given = lax.ppermute(send, "c", [(0, 1), (1, 0)])
     keep = third_part(turned, acc, out_grad, cand, group_counts)

time: 151 us -> 149 us (0.987)
  waiting for transfers between devices: 3.44 us -> 7.72 us
  Pallas kernels: 20.2 us -> 16.9 us
  starting transfers between devices: 27.8 us -> 24.6 us
    pallas_call x3 -> x2, Pallas kernels: 11.2 us -> 6.75 us  [add_pieces(): pl.pallas_call(functools.partial(add_kernel, count, later), out_shape=sum...]
    ppermute x4 -> x3, waiting for transfers between devices: 0.01 us -> 3.17 us  [swapped(): return lax.ppermute(value, AXES, swap)]
    ppermute x4 -> x3, starting transfers between devices: 13.7 us -> 11.9 us  [swapped(): return lax.ppermute(value, AXES, swap)]
  transfers between devices with their start and end apart: 8 -> 7, of which waited for: 2 -> 3; matrix products, arithmetic and copies ran while one was open for 0% -> 0% of each run, Pallas kernels for 9% -> 6%
where the time goes in v6:
time: 149 us; the launch traced here: 148 us
  blocking collectives  90.7 us (61%)
  starting transfers between devices  24.6 us (17%)
  Pallas kernels  16.9 us (11%)
  waiting for transfers between devices  7.72 us (5%)
  between operations  3.97 us (3%)
  other arithmetic  1.92 us (1%)
  local copies, waits for them, and re-layouts  1.79 us (1%)
    all_to_all x1, blocking collectives, per_device(): lax.all_to_all(pieces, AXES, 0, 0, axis_index_groups=runs_along_z(), tile...  25.3 us
    all_to_all x1, blocking collectives, per_device(): strips = lax.all_to_all(strips, ('zh', 'zl'), 0, 0, tiled=True)  23.6 us
    all_to_all x2, blocking collectives, to_all(): lax.all_to_all(copies, axis, 0, 0, axis_index_groups=groups, tiled=True)  21.5 us
    all_to_all x1, blocking collectives, per_device(): planes = lax.all_to_all(mine, ('x', 'y'), 0, 0, tiled=True)  20.3 us
    ppermute x3, starting transfers between devices, swapped(): return lax.ppermute(value, AXES, swap)  11.9 us
    ppermute x3, starting transfers between devices, per_device(): lax.ppermute(line, AXES, shift(rings, by))  10.8 us
    pallas_call x1, Pallas kernels, second_half(): pl.pallas_call(second_kernel, out_shape=(jax.ShapeDtypeStruct(before.shap...  6.84 us
    pallas_call x2, Pallas kernels, add_pieces(): pl.pallas_call(functools.partial(add_kernel, count, later), out_shape=sum...  6.75 us
  transfers between devices with their start and end apart: 7, of which 3 were waited for; matrix products, arithmetic and copies ran while one was open for 0% of the time, Pallas kernels for 6%

profile of v6, /device:TPU:24, one launch (start us, length us, event | category | flops | bytes accessed | tf_op | source)
XLA Modules:
  0.0 147.6 jit_solution(5144784993307389064)
XLA Ops:
  1.3 0.9 copy-done.2
  2.2 0.7 copy-done.4
  2.9 0.7 shard_map.86
  3.5 25.3 %all_to_all.25 = bf16[8,144,128]{2,1,0:T(8,128)(2,1)S(1)} all-to-all(bf16[8,144,128]{2,1,0:T(8,128)(2,1)S(1)} %shard_map.86), channel_id=1, replica_groups={{8,10,12,14,64,66,68,70},{72,74,76,78,0,2,4,6},{24,26,28,30,80,82,84,86..., dimensions={0} | all-to-all | bytes 589824 | tf_op jit(solution)/shard_map/all_to_all | solution.py:366
  28.9 0.0 copy-start.1
  28.9 0.0 copy-start.3
  28.9 0.1 broadcast_in_dim.8
  29.1 13.5 %all_to_all.26.refs_0_ = bf16[4,1040,128]{2,1,0:T(8,128)(2,1)S(1)} all-to-all(bf16[4,1040,128]{2,1,0:T(8,128)(2,1)S(1)} %broadcast_in_dim.8), channel_id=1, replica_groups={{0,16,32,48},{128,144,160,176},{256,272,288,304},{384,400,416,432},{2,1..., dimensions={0} | all-to-all | bytes 2129920 | tf_op jit(solution)/shard_map/all_to_all | solution.py:54
  42.6 4.9 %collective-permute-start.2 = (bf16[4,1040,128]{2,1,0:T(8,128)(2,1)S(1)}, bf16[4,1040,128]{2,1,0:T(8,128)(2,1)S(1)}, u32[]{:S(2)}, u32[]{:S(2)}) collective-permute-start(bf16[4,1040,128]{2,1,0:T(8,128)(2,1)S(1)} %all_to_all.26.refs_0_), channel_id=1, source_target_pairs={{0,256},{128,384},{256,0},{384,128},{16,272},{144,400},{272,16},{4... | collective-permute-start | bytes 3194888 | tf_op jit(solution)/shard_map/ppermute | solution.py:380
  47.5 3.4 %collective-permute-start.4 = (bf16[4,1040,128]{2,1,0:T(8,128)(2,1)S(1)}, bf16[4,1040,128]{2,1,0:T(8,128)(2,1)S(1)}, u32[]{:S(2)}, u32[]{:S(2)}) collective-permute-start(bf16[4,1040,128]{2,1,0:T(8,128)(2,1)S(1)} %all_to_all.26.refs_0_), channel_id=1, source_target_pairs={{0,1},{1,0},{2,3},{3,2},{4,5},{5,4},{6,7},{7,6},{8,9},{9,8},{10,11... | collective-permute-start | bytes 3194888 | tf_op jit(solution)/shard_map/ppermute | solution.py:377
  50.9 3.1 %collective-permute-start.1 = (bf16[4,1040,128]{2,1,0:T(8,128)(2,1)S(1)}, bf16[4,1040,128]{2,1,0:T(8,128)(2,1)S(1)}, u32[]{:S(2)}, u32[]{:S(2)}) collective-permute-start(bf16[4,1040,128]{2,1,0:T(8,128)(2,1)S(1)} %all_to_all.26.refs_0_), channel_id=1, source_target_pairs={{0,384},{128,0},{256,128},{384,256},{16,400},{144,16},{272,144},{4... | collective-permute-start | bytes 3194888 | tf_op jit(solution)/shard_map/ppermute | solution.py:380
  54.0 2.8 %collective-permute-start = (bf16[4,1040,128]{2,1,0:T(8,128)(2,1)S(1)}, bf16[4,1040,128]{2,1,0:T(8,128)(2,1)S(1)}, u32[]{:S(2)}, u32[]{:S(2)}) collective-permute-start(bf16[4,1040,128]{2,1,0:T(8,128)(2,1)S(1)} %all_to_all.26.refs_0_), channel_id=1, source_target_pairs={{0,128},{128,256},{256,384},{384,0},{16,144},{144,272},{272,400},{... | collective-permute-start | bytes 3194888 | tf_op jit(solution)/shard_map/ppermute | solution.py:380
  56.8 3.4 %shard_map.87 = (f32[65,128,128]{2,1,0:T(8,128)S(1)}, bf16[28,128,128]{2,1,0:T(8,128)(2,1)S(1)}) custom-call(s32[2,64]{1,0:T(2,128)S(1)} %bitcast.8, bf16[128,3584]{1,0:T(8,128)(2,1)S(1)} %copy-done.1, bf16[4,1040,128]{2,1,0:T(8,128)(2,1)S(1)} %all_to_all.26.refs_0_), custom_call_target="tpu_custom_call" | custom-call | flops 134217728 | bytes 10000000 | tf_op jit(solution)/shard_map/pallas_call | solution.py:290
  60.2 0.8 collective-permute-done.2.refs_0_
  61.0 4.4 %collective-permute-start.3 = (bf16[4,1040,128]{2,1,0:T(8,128)(2,1)S(1)}, bf16[4,1040,128]{2,1,0:T(8,128)(2,1)S(1)}, u32[]{:S(2)}, u32[]{:S(2)}) collective-permute-start(bf16[4,1040,128]{2,1,0:T(8,128)(2,1)S(1)} %collective-permute-done.2.refs_0_), channel_id=1, source_target_pairs={{0,1},{1,0},{2,3},{3,2},{4,5},{5,4},{6,7},{7,6},{8,9},{9,8},{10,11... | collective-permute-start | bytes 3194888 | tf_op jit(solution)/shard_map/ppermute | solution.py:377
  65.3 0.0 collective-permute-done.4.refs_1_
  65.4 3.4 %shard_map.88.before = f32[65,128,128]{2,1,0:T(8,128)S(1)} custom-call(s32[2,64]{1,0:T(2,128)S(1)} %bitcast.9, bf16[128,3584]{1,0:T(8,128)(2,1)S(1)} %copy-done.1, bf16[4,1040,128]{2,1,0:T(8,128)(2,1)S(1)} %collective-permute-done.2.refs_0_, bf16[4,1040,128]{2,1,0:T(8,128)(2,1)S(1)} %collective-permute-done.4.refs_1_, ...), custom_call_target="tpu_custom_call" | custom-call | flops 268435456 | bytes 10000000 | tf_op jit(solution)/shard_map/pallas_call | solution.py:290
  68.8 0.0 copy-start
  68.8 3.7 %collective-permute-done.1.two = bf16[4,1040,128]{2,1,0:T(8,128)(2,1)S(1)} collective-permute-done((bf16[4,1040,128]{2,1,0:T(8,128)(2,1)S(1)}, bf16[4,1040,128]{2,1,0:T(8,128)(2,1)S(1)}, u32[]{:S(2)}, u32[]{:S(2)}) %collective-permute-start.1) | collective-permute-done | bytes 1064992 | tf_op jit(solution)/shard_map/ppermute | solution.py:380
  72.5 0.0 collective-permute-done.3.three
  72.5 0.2 pad_maximum_fusion
  72.7 4.2 %collective-permute-start.5 = (bf16[8,1040,128]{2,1,0:T(8,128)(2,1)S(1)}, bf16[8,1040,128]{2,1,0:T(8,128)(2,1)S(1)}, u32[]{:S(2)}, u32[]{:S(2)}) collective-permute-start(bf16[8,1040,128]{2,1,0:T(8,128)(2,1)S(1)} %pad_maximum_fusion), channel_id=1, source_target_pairs={{0,1},{1,0},{2,3},{3,2},{4,5},{5,4},{6,7},{7,6},{8,9},{9,8},{10,11... | collective-permute-start | bytes 6389768 | tf_op jit(solution)/shard_map/ppermute | solution.py:377
  77.5 3.2 %collective-permute-done.5.four = bf16[8,1040,128]{2,1,0:T(8,128)(2,1)S(1)} collective-permute-done((bf16[8,1040,128]{2,1,0:T(8,128)(2,1)S(1)}, bf16[8,1040,128]{2,1,0:T(8,128)(2,1)S(1)}, u32[]{:S(2)}, u32[]{:S(2)}) %collective-permute-start.5) | collective-permute-done | bytes 2129952 | tf_op jit(solution)/shard_map/ppermute | solution.py:377
  80.7 6.8 %shard_map.89 = (f32[65,128,128]{2,1,0:T(8,128)S(1)}, bf16[4,4,8,32,128]{4,3,2,1,0:T(8,128)(2,1)S(1)}) custom-call(s32[2,64]{1,0:T(2,128)S(1)} %bitcast.10, s32[1]{0:T(128)S(6)} %copy.10.counts, bf16[128,3584]{1,0:T(8,128)(2,1)S(1)} %copy-done.1, bf16[28,128,128]{2,1,0:T(8,128)(2,1)S(1)} %get-tuple-element.12.turned, ...), custom_call_target="tpu_custom_call" | custom-call | flops 805306368 | bytes 15000000 | tf_op jit(solution)/shard_map/pallas_call | solution.py:320
  87.5 1.9 %collective-permute-start.6 = (bf16[4,4,8,32,128]{4,3,2,1,0:T(8,128)(2,1)S(1)}, bf16[4,4,8,32,128]{4,3,2,1,0:T(8,128)(2,1)S(1)}, u32[]{:S(2)}, u32[]{:S(2)}) collective-permute-start(bf16[4,4,8,32,128]{4,3,2,1,0:T(8,128)(2,1)S(1)} %get-tuple-element.21), channel_id=1, source_target_pairs={{0,1},{1,0},{2,3},{3,2},{4,5},{5,4},{6,7},{7,6},{8,9},{9,8},{10,11... | collective-permute-start | bytes 3145736 | tf_op jit(solution)/shard_map/ppermute | solution.py:397
  89.5 2.7 %shard_map.90 = bf16[4,4,8,32,128]{4,3,2,1,0:T(8,128)(2,1)S(1)} custom-call(s32[2,64]{1,0:T(2,128)S(1)} %bitcast.11, s32[1]{0:T(128)S(6)} %copy.10.counts, bf16[28,128,128]{2,1,0:T(8,128)(2,1)S(1)} %get-tuple-element.12.turned, f32[65,128,128]{2,1,0:T(8,128)S(1)} %get-tuple-element.20.acc, bf16[128,14336]{1,0:T(8,128)(2,1)S(1)} %copy-done), custom_call_target="tpu_custom_call" | custom-call | flops 134217728 | bytes 8000000 | tf_op jit(solution)/shard_map/pallas_call | solution.py:344
  92.2 0.3 add_convert_fusion
  92.5 20.3 %all_to_all.27 = bf16[16,256,128]{2,1,0:T(8,128)(2,1)S(1)} all-to-all(bf16[16,256,128]{2,1,0:T(8,128)(2,1)S(1)} %bitcast.13), channel_id=1, replica_groups=mesh['x'=4,'zh'=2,'y'=4,'zl'=8,'c'=2] {'x','y'}, dimensions={0} | all-to-all | bytes 2097152 | tf_op jit(solution)/shard_map/all_to_all | solution.py:401
  112.7 0.1 reduce_sum.43
  112.9 23.6 %all_to_all.28 = bf16[16,32,128]{2,1,0:T(8,128)(2,1)S(1)} all-to-all(bf16[16,32,128]{2,1,0:T(8,128)(2,1)S(1)} %bitcast.15), channel_id=1, replica_groups=mesh['x'=4,'zh'=2,'y'=4,'zl'=8,'c'=2] {'zh','zl'}, dimensions={0} | all-to-all | bytes 262144 | tf_op jit(solution)/shard_map/all_to_all | solution.py:405
  136.6 8.0 %all_to_all.29 = f32[4,32,128]{2,1,0:T(8,128)S(1)} all-to-all(f32[4,32,128]{2,1,0:T(8,128)S(1)} %broadcast_in_dim.11), channel_id=1, replica_groups=mesh['x'=4,'zh'=2,'y'=4,'zl'=8,'c'=2] {'x'}, dimensions={0} | all-to-all | bytes 131072 | tf_op jit(solution)/shard_map/all_to_all | solution.py:54
  144.6 1.2 multiply_reduce_fusion
  (13 shorter events, 0.1 us)
Async XLA Ops:
  1.3 0.9 copy-start.2
  2.2 0.7 copy-start.4
  28.9 27.9 %copy-start.1 = (bf16[128,3584]{1,0:T(8,128)(2,1)S(1)}, bf16[128,3584]{1,0:T(8,128)(2,1)}, u32[]{:S(2)}) copy-start(bf16[128,3584]{1,0:T(8,128)(2,1)} %tok_ref.5) | copy-start | bytes 2752516
  28.9 27.9 %copy-start.3 = (s32[64,2]{0,1:T(2,128)S(1)}, s32[64,2]{0,1:T(2,128)}, u32[]{:S(2)}) copy-start(s32[64,2]{0,1:T(2,128)} %param.12) | copy-start | bytes 1540
  42.6 18.4 %collective-permute-start.2 = (bf16[4,1040,128]{2,1,0:T(8,128)(2,1)S(1)}, bf16[4,1040,128]{2,1,0:T(8,128)(2,1)S(1)}, u32[]{:S(2)}, u32[]{:S(2)}) collective-permute-start(bf16[4,1040,128]{2,1,0:T(8,128)(2,1)S(1)} %all_to_all.26.refs_0_), channel_id=1, source_target_pairs={{0,256},{128,384},{256,0},{384,128},{16,272},{144,400},{272,16},{4... | collective-permute-start | bytes 3194888 | tf_op jit(solution)/shard_map/ppermute | solution.py:380
  47.5 17.8 %collective-permute-start.4 = (bf16[4,1040,128]{2,1,0:T(8,128)(2,1)S(1)}, bf16[4,1040,128]{2,1,0:T(8,128)(2,1)S(1)}, u32[]{:S(2)}, u32[]{:S(2)}) collective-permute-start(bf16[4,1040,128]{2,1,0:T(8,128)(2,1)S(1)} %all_to_all.26.refs_0_), channel_id=1, source_target_pairs={{0,1},{1,0},{2,3},{3,2},{4,5},{5,4},{6,7},{7,6},{8,9},{9,8},{10,11... | collective-permute-start | bytes 3194888 | tf_op jit(solution)/shard_map/ppermute | solution.py:377
  50.9 21.6 %collective-permute-start.1 = (bf16[4,1040,128]{2,1,0:T(8,128)(2,1)S(1)}, bf16[4,1040,128]{2,1,0:T(8,128)(2,1)S(1)}, u32[]{:S(2)}, u32[]{:S(2)}) collective-permute-start(bf16[4,1040,128]{2,1,0:T(8,128)(2,1)S(1)} %all_to_all.26.refs_0_), channel_id=1, source_target_pairs={{0,384},{128,0},{256,128},{384,256},{16,400},{144,16},{272,144},{4... | collective-permute-start | bytes 3194888 | tf_op jit(solution)/shard_map/ppermute | solution.py:380
  54.0 18.5 %collective-permute-start = (bf16[4,1040,128]{2,1,0:T(8,128)(2,1)S(1)}, bf16[4,1040,128]{2,1,0:T(8,128)(2,1)S(1)}, u32[]{:S(2)}, u32[]{:S(2)}) collective-permute-start(bf16[4,1040,128]{2,1,0:T(8,128)(2,1)S(1)} %all_to_all.26.refs_0_), channel_id=1, source_target_pairs={{0,128},{128,256},{256,384},{384,0},{16,144},{144,272},{272,400},{... | collective-permute-start | bytes 3194888 | tf_op jit(solution)/shard_map/ppermute | solution.py:380
  61.0 11.5 %collective-permute-start.3 = (bf16[4,1040,128]{2,1,0:T(8,128)(2,1)S(1)}, bf16[4,1040,128]{2,1,0:T(8,128)(2,1)S(1)}, u32[]{:S(2)}, u32[]{:S(2)}) collective-permute-start(bf16[4,1040,128]{2,1,0:T(8,128)(2,1)S(1)} %collective-permute-done.2.refs_0_), channel_id=1, source_target_pairs={{0,1},{1,0},{2,3},{3,2},{4,5},{5,4},{6,7},{7,6},{8,9},{9,8},{10,11... | collective-permute-start | bytes 3194888 | tf_op jit(solution)/shard_map/ppermute | solution.py:377
  68.8 11.9 %copy-start = (bf16[128,14336]{1,0:T(8,128)(2,1)S(1)}, bf16[128,14336]{1,0:T(8,128)(2,1)}, u32[]{:S(2)}) copy-start(bf16[128,14336]{1,0:T(8,128)(2,1)} %grad_ref.3) | copy-start | bytes 11010052
  72.7 8.0 %collective-permute-start.5 = (bf16[8,1040,128]{2,1,0:T(8,128)(2,1)S(1)}, bf16[8,1040,128]{2,1,0:T(8,128)(2,1)S(1)}, u32[]{:S(2)}, u32[]{:S(2)}) collective-permute-start(bf16[8,1040,128]{2,1,0:T(8,128)(2,1)S(1)} %pad_maximum_fusion), channel_id=1, source_target_pairs={{0,1},{1,0},{2,3},{3,2},{4,5},{5,4},{6,7},{7,6},{8,9},{9,8},{10,11... | collective-permute-start | bytes 6389768 | tf_op jit(solution)/shard_map/ppermute | solution.py:377
  87.5 4.6 %collective-permute-start.6 = (bf16[4,4,8,32,128]{4,3,2,1,0:T(8,128)(2,1)S(1)}, bf16[4,4,8,32,128]{4,3,2,1,0:T(8,128)(2,1)S(1)}, u32[]{:S(2)}, u32[]{:S(2)}) collective-permute-start(bf16[4,4,8,32,128]{4,3,2,1,0:T(8,128)(2,1)S(1)} %get-tuple-element.21), channel_id=1, source_target_pairs={{0,1},{1,0},{2,3},{3,2},{4,5},{5,4},{6,7},{7,6},{8,9},{9,8},{10,11... | collective-permute-start | bytes 3145736 | tf_op jit(solution)/shard_map/ppermute | solution.py:397

commit v7 on v6

--- a/solution.py
+++ b/solution.py
@@ -233,14 +233,14 @@
             out_ref[x, y, z] = part[x * 32 : (x + 1) * 32]
         return carry
 
-    lax.fori_loop(0, cand.shape[1] // NC, gradient, 0, unroll=16)
+    lax.fori_loop(0, cand.shape[1] // NC, gradient, 0, unroll=32)
 
 
 def second_kernel(
-    cand, counts, tok_ref, turned, one, two, three, four, before, grad_ref, acc, send_ref,
+    cand, counts, tok_ref, turned, one, two, before, grad_ref, acc, send_ref,
     weights, tails, numbers, places, slot_of, rows, slots, offs, sem, tail_sem, move_sem,
 ):
-    wait_tails, wait_blocks = fetch_pieces([one, two, three, four], weights, tails, sem, tail_sem)
+    wait_tails, wait_blocks = fetch_pieces([one, two], weights, tails, sem, tail_sem)
     spare = acc.shape[0] - 1
     give_slots(cand, slot_of, spare)
 
@@ -385,14 +385,9 @@
     acc = add_pieces(tokens, [one, line_other], cand, cols, acc)
     two, three, one_other, acc = lax.optimization_barrier((two, three, one_other, acc))
     both_other = swapped(jnp.concatenate([two, three], axis=0))
+    acc = add_pieces(tokens, [two, three], cand, cols, acc)
     acc, send = second_half(
-        tokens,
-        turned,
-        [two, three, one_other, both_other],
-        acc,
-        out_grad,
-        cand,
-        group_counts,
+        tokens, turned, [one_other, both_other], acc, out_grad, cand, group_counts
     )
     given = lax.ppermute(send, "c", [(0, 1), (1, 0)])
     keep = third_part(turned, acc, out_grad, cand, group_counts)

time: 149 us -> 148 us (level)
  waiting for transfers between devices: 7.72 us -> 3.73 us
    ppermute x3, waiting for transfers between devices: 3.17 us -> 0.01 us  [swapped(): return lax.ppermute(value, AXES, swap)]
    pallas_call x2 -> x3, Pallas kernels: 6.75 us -> 9.8 us  [add_pieces(): pl.pallas_call(functools.partial(add_kernel, count, later), out_shape=sum...]
  transfers between devices with their start and end apart: 7 -> 7, of which waited for: 3 -> 2; matrix products, arithmetic and copies ran while one was open for 0% -> 0% of each run, Pallas kernels for 6% -> 8%
where the time goes in v7:
time: 148 us; the launch traced here: 146 us
  blocking collectives  90.4 us (61%)
  starting transfers between devices  25.9 us (18%)
  Pallas kernels  18.3 us (12%)
  between operations  3.99 us (3%)
  waiting for transfers between devices  3.73 us (3%)
  other arithmetic  1.92 us (1%)
  local copies, waits for them, and re-layouts  1.79 us (1%)
    all_to_all x1, blocking collectives, per_device(): lax.all_to_all(pieces, AXES, 0, 0, axis_index_groups=runs_along_z(), tile...  25.3 us
    all_to_all x1, blocking collectives, per_device(): strips = lax.all_to_all(strips, ('zh', 'zl'), 0, 0, tiled=True)  23.1 us
    all_to_all x2, blocking collectives, to_all(): lax.all_to_all(copies, axis, 0, 0, axis_index_groups=groups, tiled=True)  21.8 us
    all_to_all x1, blocking collectives, per_device(): planes = lax.all_to_all(mine, ('x', 'y'), 0, 0, tiled=True)  20.2 us
    ppermute x3, starting transfers between devices, per_device(): lax.ppermute(line, AXES, shift(rings, by))  12 us
    ppermute x3, starting transfers between devices, swapped(): return lax.ppermute(value, AXES, swap)  11.9 us
    pallas_call x3, Pallas kernels, add_pieces(): pl.pallas_call(functools.partial(add_kernel, count, later), out_shape=sum...  9.8 us
    pallas_call x1, Pallas kernels, second_half(): pl.pallas_call(second_kernel, out_shape=(jax.ShapeDtypeStruct(before.shap...  5.36 us
  transfers between devices with their start and end apart: 7, of which 2 were waited for; matrix products, arithmetic and copies ran while one was open for 0% of the time, Pallas kernels for 8%

profile of v7, /device:TPU:24, one launch (start us, length us, event | category | flops | bytes accessed | tf_op | source)
XLA Modules:
  0.0 146.0 jit_solution(8928651777446015695)
XLA Ops:
  1.3 0.9 copy-done.2
  2.2 0.7 copy-done.4
  2.9 0.7 shard_map.86
  3.5 25.3 %all_to_all.25 = bf16[8,144,128]{2,1,0:T(8,128)(2,1)S(1)} all-to-all(bf16[8,144,128]{2,1,0:T(8,128)(2,1)S(1)} %shard_map.86), channel_id=1, replica_groups={{8,10,12,14,64,66,68,70},{72,74,76,78,0,2,4,6},{24,26,28,30,80,82,84,86..., dimensions={0} | all-to-all | bytes 589824 | tf_op jit(solution)/shard_map/all_to_all | solution.py:366
  28.8 0.0 copy-start
  28.8 0.0 copy-start.3
  28.9 0.1 broadcast_in_dim.8
  29.1 13.5 %all_to_all.26.refs_0_ = bf16[4,1040,128]{2,1,0:T(8,128)(2,1)S(1)} all-to-all(bf16[4,1040,128]{2,1,0:T(8,128)(2,1)S(1)} %broadcast_in_dim.8), channel_id=1, replica_groups={{0,16,32,48},{128,144,160,176},{256,272,288,304},{384,400,416,432},{2,1..., dimensions={0} | all-to-all | bytes 2129920 | tf_op jit(solution)/shard_map/all_to_all | solution.py:54
  42.6 4.9 %collective-permute-start.2 = (bf16[4,1040,128]{2,1,0:T(8,128)(2,1)S(1)}, bf16[4,1040,128]{2,1,0:T(8,128)(2,1)S(1)}, u32[]{:S(2)}, u32[]{:S(2)}) collective-permute-start(bf16[4,1040,128]{2,1,0:T(8,128)(2,1)S(1)} %all_to_all.26.refs_0_), channel_id=1, source_target_pairs={{0,256},{128,384},{256,0},{384,128},{16,272},{144,400},{272,16},{4... | collective-permute-start | bytes 3194888 | tf_op jit(solution)/shard_map/ppermute | solution.py:380
  47.5 3.4 %collective-permute-start.4 = (bf16[4,1040,128]{2,1,0:T(8,128)(2,1)S(1)}, bf16[4,1040,128]{2,1,0:T(8,128)(2,1)S(1)}, u32[]{:S(2)}, u32[]{:S(2)}) collective-permute-start(bf16[4,1040,128]{2,1,0:T(8,128)(2,1)S(1)} %all_to_all.26.refs_0_), channel_id=1, source_target_pairs={{0,1},{1,0},{2,3},{3,2},{4,5},{5,4},{6,7},{7,6},{8,9},{9,8},{10,11... | collective-permute-start | bytes 3194888 | tf_op jit(solution)/shard_map/ppermute | solution.py:377
  50.9 2.5 %collective-permute-start = (bf16[4,1040,128]{2,1,0:T(8,128)(2,1)S(1)}, bf16[4,1040,128]{2,1,0:T(8,128)(2,1)S(1)}, u32[]{:S(2)}, u32[]{:S(2)}) collective-permute-start(bf16[4,1040,128]{2,1,0:T(8,128)(2,1)S(1)} %all_to_all.26.refs_0_), channel_id=1, source_target_pairs={{0,128},{128,256},{256,384},{384,0},{16,144},{144,272},{272,400},{... | collective-permute-start | bytes 3194888 | tf_op jit(solution)/shard_map/ppermute | solution.py:380
  53.4 4.6 %collective-permute-start.1 = (bf16[4,1040,128]{2,1,0:T(8,128)(2,1)S(1)}, bf16[4,1040,128]{2,1,0:T(8,128)(2,1)S(1)}, u32[]{:S(2)}, u32[]{:S(2)}) collective-permute-start(bf16[4,1040,128]{2,1,0:T(8,128)(2,1)S(1)} %all_to_all.26.refs_0_), channel_id=1, source_target_pairs={{0,384},{128,0},{256,128},{384,256},{16,400},{144,16},{272,144},{4... | collective-permute-start | bytes 3194888 | tf_op jit(solution)/shard_map/ppermute | solution.py:380
  58.0 3.0 %shard_map.87 = (f32[65,128,128]{2,1,0:T(8,128)S(1)}, bf16[28,128,128]{2,1,0:T(8,128)(2,1)S(1)}) custom-call(s32[2,64]{1,0:T(2,128)S(1)} %bitcast.8, bf16[128,3584]{1,0:T(8,128)(2,1)S(1)} %copy-done, bf16[4,1040,128]{2,1,0:T(8,128)(2,1)S(1)} %all_to_all.26.refs_0_), custom_call_target="tpu_custom_call" | custom-call | flops 134217728 | bytes 10000000 | tf_op jit(solution)/shard_map/pallas_call | solution.py:290
  61.0 0.0 collective-permute-done.2.refs_0_
  61.1 4.3 %collective-permute-start.3 = (bf16[4,1040,128]{2,1,0:T(8,128)(2,1)S(1)}, bf16[4,1040,128]{2,1,0:T(8,128)(2,1)S(1)}, u32[]{:S(2)}, u32[]{:S(2)}) collective-permute-start(bf16[4,1040,128]{2,1,0:T(8,128)(2,1)S(1)} %collective-permute-done.2.refs_0_), channel_id=1, source_target_pairs={{0,1},{1,0},{2,3},{3,2},{4,5},{5,4},{6,7},{7,6},{8,9},{9,8},{10,11... | collective-permute-start | bytes 3194888 | tf_op jit(solution)/shard_map/ppermute | solution.py:377
  65.4 3.4 %shard_map.88.refs_2_ = f32[65,128,128]{2,1,0:T(8,128)S(1)} custom-call(s32[2,64]{1,0:T(2,128)S(1)} %bitcast.9, bf16[128,3584]{1,0:T(8,128)(2,1)S(1)} %copy-done, bf16[4,1040,128]{2,1,0:T(8,128)(2,1)S(1)} %collective-permute-done.2.refs_0_, bf16[4,1040,128]{2,1,0:T(8,128)(2,1)S(1)} %collective-permute-done.4.refs_1_, ...), custom_call_target="tpu_custom_call" | custom-call | flops 268435456 | bytes 10000000 | tf_op jit(solution)/shard_map/pallas_call | solution.py:290
  68.7 3.6 %collective-permute-done.refs_0_ = bf16[4,1040,128]{2,1,0:T(8,128)(2,1)S(1)} collective-permute-done((bf16[4,1040,128]{2,1,0:T(8,128)(2,1)S(1)}, bf16[4,1040,128]{2,1,0:T(8,128)(2,1)S(1)}, u32[]{:S(2)}, u32[]{:S(2)}) %collective-permute-start) | collective-permute-done | bytes 1064992 | tf_op jit(solution)/shard_map/ppermute | solution.py:380
  72.4 0.1 collective-permute-done.1.refs_1_
  72.4 0.0 collective-permute-done.3.one
  72.4 0.2 pad_maximum_fusion
  72.6 4.2 %collective-permute-start.5 = (bf16[8,1040,128]{2,1,0:T(8,128)(2,1)S(1)}, bf16[8,1040,128]{2,1,0:T(8,128)(2,1)S(1)}, u32[]{:S(2)}, u32[]{:S(2)}) collective-permute-start(bf16[8,1040,128]{2,1,0:T(8,128)(2,1)S(1)} %pad_maximum_fusion), channel_id=1, source_target_pairs={{0,1},{1,0},{2,3},{3,2},{4,5},{5,4},{6,7},{7,6},{8,9},{9,8},{10,11... | collective-permute-start | bytes 6389768 | tf_op jit(solution)/shard_map/ppermute | solution.py:377
  77.5 0.0 copy-start.1
  77.5 3.4 %shard_map.89.before = f32[65,128,128]{2,1,0:T(8,128)S(1)} custom-call(s32[2,64]{1,0:T(2,128)S(1)} %bitcast.10, bf16[128,3584]{1,0:T(8,128)(2,1)S(1)} %copy-done, bf16[4,1040,128]{2,1,0:T(8,128)(2,1)S(1)} %collective-permute-done.refs_0_, bf16[4,1040,128]{2,1,0:T(8,128)(2,1)S(1)} %collective-permute-done.1.refs_1_, f32[65,128,128]{2,1,0:T(8,128)S(1)} %shard_map.88.refs_2_), custom_call_target="tpu_custom_call" | custom-call | flops 268435456 | bytes 10000000 | tf_op jit(solution)/shard_map/pallas_call | solution.py:290
  80.9 5.4 %shard_map.90 = (f32[65,128,128]{2,1,0:T(8,128)S(1)}, bf16[4,4,8,32,128]{4,3,2,1,0:T(8,128)(2,1)S(1)}) custom-call(s32[2,64]{1,0:T(2,128)S(1)} %bitcast.11, s32[1]{0:T(128)S(6)} %copy.10.counts, bf16[128,3584]{1,0:T(8,128)(2,1)S(1)} %copy-done, bf16[28,128,128]{2,1,0:T(8,128)(2,1)S(1)} %get-tuple-element.12.turned, ...), custom_call_target="tpu_custom_call" | custom-call | flops 536870912 | bytes 15000000 | tf_op jit(solution)/shard_map/pallas_call | solution.py:320
  86.3 2.0 %collective-permute-start.6 = (bf16[4,4,8,32,128]{4,3,2,1,0:T(8,128)(2,1)S(1)}, bf16[4,4,8,32,128]{4,3,2,1,0:T(8,128)(2,1)S(1)}, u32[]{:S(2)}, u32[]{:S(2)}) collective-permute-start(bf16[4,4,8,32,128]{4,3,2,1,0:T(8,128)(2,1)S(1)} %get-tuple-element.21), channel_id=1, source_target_pairs={{0,1},{1,0},{2,3},{3,2},{4,5},{5,4},{6,7},{7,6},{8,9},{9,8},{10,11... | collective-permute-start | bytes 3145736 | tf_op jit(solution)/shard_map/ppermute | solution.py:392
  88.3 2.5 %shard_map.91 = bf16[4,4,8,32,128]{4,3,2,1,0:T(8,128)(2,1)S(1)} custom-call(s32[2,64]{1,0:T(2,128)S(1)} %bitcast.12, s32[1]{0:T(128)S(6)} %copy.10.counts, bf16[28,128,128]{2,1,0:T(8,128)(2,1)S(1)} %get-tuple-element.12.turned, f32[65,128,128]{2,1,0:T(8,128)S(1)} %get-tuple-element.20.acc, bf16[128,14336]{1,0:T(8,128)(2,1)S(1)} %copy-done.1), custom_call_target="tpu_custom_call" | custom-call | flops 134217728 | bytes 8000000 | tf_op jit(solution)/shard_map/pallas_call | solution.py:344
  90.9 0.3 add_convert_fusion
  91.2 20.2 %all_to_all.27 = bf16[16,256,128]{2,1,0:T(8,128)(2,1)S(1)} all-to-all(bf16[16,256,128]{2,1,0:T(8,128)(2,1)S(1)} %bitcast.14), channel_id=1, replica_groups=mesh['x'=4,'zh'=2,'y'=4,'zl'=8,'c'=2] {'x','y'}, dimensions={0} | all-to-all | bytes 2097152 | tf_op jit(solution)/shard_map/all_to_all | solution.py:396
  111.4 0.1 reduce_sum.43
  111.6 23.1 %all_to_all.28 = bf16[16,32,128]{2,1,0:T(8,128)(2,1)S(1)} all-to-all(bf16[16,32,128]{2,1,0:T(8,128)(2,1)S(1)} %bitcast.16), channel_id=1, replica_groups=mesh['x'=4,'zh'=2,'y'=4,'zl'=8,'c'=2] {'zh','zl'}, dimensions={0} | all-to-all | bytes 262144 | tf_op jit(solution)/shard_map/all_to_all | solution.py:400
  134.7 8.3 %all_to_all.29 = f32[4,32,128]{2,1,0:T(8,128)S(1)} all-to-all(f32[4,32,128]{2,1,0:T(8,128)S(1)} %broadcast_in_dim.11), channel_id=1, replica_groups=mesh['x'=4,'zh'=2,'y'=4,'zl'=8,'c'=2] {'x'}, dimensions={0} | all-to-all | bytes 131072 | tf_op jit(solution)/shard_map/all_to_all | solution.py:54
  143.0 1.2 multiply_reduce_fusion
  (14 shorter events, 0.1 us)
Async XLA Ops:
  1.3 0.9 copy-start.2
  2.2 0.7 copy-start.4
  28.8 29.1 %copy-start = (bf16[128,3584]{1,0:T(8,128)(2,1)S(1)}, bf16[128,3584]{1,0:T(8,128)(2,1)}, u32[]{:S(2)}) copy-start(bf16[128,3584]{1,0:T(8,128)(2,1)} %tok_ref.7) | copy-start | bytes 2752516
  28.8 29.1 %copy-start.3 = (s32[64,2]{0,1:T(2,128)S(1)}, s32[64,2]{0,1:T(2,128)}, u32[]{:S(2)}) copy-start(s32[64,2]{0,1:T(2,128)} %param.12) | copy-start | bytes 1540
  42.6 18.5 %collective-permute-start.2 = (bf16[4,1040,128]{2,1,0:T(8,128)(2,1)S(1)}, bf16[4,1040,128]{2,1,0:T(8,128)(2,1)S(1)}, u32[]{:S(2)}, u32[]{:S(2)}) collective-permute-start(bf16[4,1040,128]{2,1,0:T(8,128)(2,1)S(1)} %all_to_all.26.refs_0_), channel_id=1, source_target_pairs={{0,256},{128,384},{256,0},{384,128},{16,272},{144,400},{272,16},{4... | collective-permute-start | bytes 3194888 | tf_op jit(solution)/shard_map/ppermute | solution.py:380
  47.5 17.8 %collective-permute-start.4 = (bf16[4,1040,128]{2,1,0:T(8,128)(2,1)S(1)}, bf16[4,1040,128]{2,1,0:T(8,128)(2,1)S(1)}, u32[]{:S(2)}, u32[]{:S(2)}) collective-permute-start(bf16[4,1040,128]{2,1,0:T(8,128)(2,1)S(1)} %all_to_all.26.refs_0_), channel_id=1, source_target_pairs={{0,1},{1,0},{2,3},{3,2},{4,5},{5,4},{6,7},{7,6},{8,9},{9,8},{10,11... | collective-permute-start | bytes 3194888 | tf_op jit(solution)/shard_map/ppermute | solution.py:377
  50.9 21.5 %collective-permute-start = (bf16[4,1040,128]{2,1,0:T(8,128)(2,1)S(1)}, bf16[4,1040,128]{2,1,0:T(8,128)(2,1)S(1)}, u32[]{:S(2)}, u32[]{:S(2)}) collective-permute-start(bf16[4,1040,128]{2,1,0:T(8,128)(2,1)S(1)} %all_to_all.26.refs_0_), channel_id=1, source_target_pairs={{0,128},{128,256},{256,384},{384,0},{16,144},{144,272},{272,400},{... | collective-permute-start | bytes 3194888 | tf_op jit(solution)/shard_map/ppermute | solution.py:380
  53.4 19.1 %collective-permute-start.1 = (bf16[4,1040,128]{2,1,0:T(8,128)(2,1)S(1)}, bf16[4,1040,128]{2,1,0:T(8,128)(2,1)S(1)}, u32[]{:S(2)}, u32[]{:S(2)}) collective-permute-start(bf16[4,1040,128]{2,1,0:T(8,128)(2,1)S(1)} %all_to_all.26.refs_0_), channel_id=1, source_target_pairs={{0,384},{128,0},{256,128},{384,256},{16,400},{144,16},{272,144},{4... | collective-permute-start | bytes 3194888 | tf_op jit(solution)/shard_map/ppermute | solution.py:380
  61.1 11.4 %collective-permute-start.3 = (bf16[4,1040,128]{2,1,0:T(8,128)(2,1)S(1)}, bf16[4,1040,128]{2,1,0:T(8,128)(2,1)S(1)}, u32[]{:S(2)}, u32[]{:S(2)}) collective-permute-start(bf16[4,1040,128]{2,1,0:T(8,128)(2,1)S(1)} %collective-permute-done.2.refs_0_), channel_id=1, source_target_pairs={{0,1},{1,0},{2,3},{3,2},{4,5},{5,4},{6,7},{7,6},{8,9},{9,8},{10,11... | collective-permute-start | bytes 3194888 | tf_op jit(solution)/shard_map/ppermute | solution.py:377
  72.6 8.3 %collective-permute-start.5 = (bf16[8,1040,128]{2,1,0:T(8,128)(2,1)S(1)}, bf16[8,1040,128]{2,1,0:T(8,128)(2,1)S(1)}, u32[]{:S(2)}, u32[]{:S(2)}) collective-permute-start(bf16[8,1040,128]{2,1,0:T(8,128)(2,1)S(1)} %pad_maximum_fusion), channel_id=1, source_target_pairs={{0,1},{1,0},{2,3},{3,2},{4,5},{5,4},{6,7},{7,6},{8,9},{9,8},{10,11... | collective-permute-start | bytes 6389768 | tf_op jit(solution)/shard_map/ppermute | solution.py:377
  77.5 3.4 %copy-start.1 = (bf16[128,14336]{1,0:T(8,128)(2,1)S(1)}, bf16[128,14336]{1,0:T(8,128)(2,1)}, u32[]{:S(2)}) copy-start(bf16[128,14336]{1,0:T(8,128)(2,1)} %grad_ref.3) | copy-start | bytes 11010052
  86.3 4.6 %collective-permute-start.6 = (bf16[4,4,8,32,128]{4,3,2,1,0:T(8,128)(2,1)S(1)}, bf16[4,4,8,32,128]{4,3,2,1,0:T(8,128)(2,1)S(1)}, u32[]{:S(2)}, u32[]{:S(2)}) collective-permute-start(bf16[4,4,8,32,128]{4,3,2,1,0:T(8,128)(2,1)S(1)} %get-tuple-element.21), channel_id=1, source_target_pairs={{0,1},{1,0},{2,3},{3,2},{4,5},{5,4},{6,7},{7,6},{8,9},{9,8},{10,11... | collective-permute-start | bytes 3145736 | tf_op jit(solution)/shard_map/ppermute | solution.py:392
